TPU v7x, 32 devices: a whole 2x2x4 slice. The times are simulated.
32 devices in a mesh: row: 8 (over y, x, core), col: 4 (over z).
Axes of the slice: x: 2, y: 2, z: 4, core: 2. Of those that a mesh axis runs over, the one named last changes fastest.
Arguments:
- phi: bfloat16 [80, 80, 80, 256], P('col', 'row'), may hold values from -1 to 1
- psi: bfloat16 [80, 80, 80, 256], P('col', 'row'), may hold values from -1 to 1
- points: int32 [16384], P(('row', 'col')), may hold values from 0 to 511999, as said below
Outputs:
- schur: float32 [16384, 16384], P('row', 'col')
- panel: float32 [16384, 256], P('row')
- potential: float32 [80, 80, 80, 256], P('col', 'row')
Inputs may be any that keep to these rules, and one draw needn't show every extreme that they name: `points`: block k of 512 consecutive entries holds distinct indices (x 80 + y) * 80 + z of cells with x // 20 = k mod (4) and y // 10 = k div (4).
All inputs are finite; a program needn't handle non-finite values.
Results may differ from a plain program's by a relative error of at most 0.0003.
Values may be sent and summed in bfloat16 or wider, within the bound.
No kernel may reach another device: no remote copies, remote signals or barrier semaphores. Data moves between devices by JAX's collectives and lax.ppermute only.
A program may use at most 256 MiB of HBM per device.

v0:
```python
import math

import jax
import jax.numpy as jnp
from jax import lax
from jax.sharding import PartitionSpec as P

NMU = 16384
PB = 256
GX = 80
GY = 80
GZ = 80


shift_value = 4.0
box_length = 2.0
highest = lax.Precision.HIGHEST


def signed_of(index, length):
    return jnp.where(2 * index < length, index, index - length).astype(jnp.float32)


def signed_frequency(count, length):
    index = jnp.arange(count, dtype=jnp.int32)
    return signed_of(index, length)


def coulomb_table(x_freq, y_freq, z_freq):
    squared = x_freq[:, None, None] ** 2 + y_freq[None, :, None] ** 2 + z_freq[None, None, :] ** 2
    safe = jnp.maximum(squared, 1.0)
    return jnp.where(squared > 0.5, box_length * box_length / math.pi / safe, 0.0)


def twiddles(length):
    rows_iota = lax.broadcasted_iota(jnp.int32, (length, length), 0)
    cols_iota = lax.broadcasted_iota(jnp.int32, (length, length), 1)
    angle = (rows_iota * cols_iota % length).astype(jnp.float32) * (2.0 * math.pi / length)
    return (jnp.cos(angle), jnp.sin(angle))


def transform(stacked, form, length, inverse):
    cosine, sine = twiddles(length)
    real_part = stacked[0]
    imag_part = stacked[1]
    cos_real = jnp.einsum(form, cosine, real_part, precision=highest)
    cos_imag = jnp.einsum(form, cosine, imag_part, precision=highest)
    sin_real = jnp.einsum(form, sine, real_part, precision=highest)
    sin_imag = jnp.einsum(form, sine, imag_part, precision=highest)
    if inverse:
        factor = 1.0 / length
        return jnp.stack([(cos_real - sin_imag) * factor, (cos_imag + sin_real) * factor])
    return jnp.stack([cos_real + sin_imag, cos_imag - sin_real])


def hadamard_gram(left, right, left_index, right_index):
    first = jnp.dot(left[0], right[0].T, preferred_element_type=jnp.float32)
    second = jnp.dot(left[1], right[1].T, preferred_element_type=jnp.float32)
    return first * second + shift_value * (left_index[:, None] == right_index[None, :]).astype(
        jnp.float32
    )


def on_device(phi, psi, points):
    col_count = lax.axis_size("col")
    row_count = lax.axis_size("row")
    col_index = lax.axis_index("col")
    row_index = lax.axis_index("row")
    plane_count, line_count, depth_count, orbital_count = phi.shape
    cells = plane_count * line_count * depth_count
    flat_phi = phi.reshape(cells, orbital_count)
    flat_psi = psi.reshape(cells, orbital_count)
    global_x = points // (GY * GZ)
    global_y = points // GZ % GY
    global_z = points % GZ
    local_cell = (
        (global_x - col_index * plane_count) * line_count + global_y - row_index * line_count
    ) * GZ + global_z
    own_samples = jnp.stack(
        [jnp.take(flat_phi, local_cell, axis=0), jnp.take(flat_psi, local_cell, axis=0)]
    )
    row_block = NMU // row_count
    col_block = NMU // col_count
    every_sample = lax.all_gather(own_samples, ("row", "col"), axis=1, tiled=True)
    row_samples = lax.dynamic_slice_in_dim(every_sample, row_index * row_block, row_block, 1)
    col_samples = lax.dynamic_slice_in_dim(every_sample, col_index * col_block, col_block, 1)
    pivot = every_sample[:, :PB]
    row_global = row_index * row_block + jnp.arange(row_block, dtype=jnp.int32)
    col_global = col_index * col_block + jnp.arange(col_block, dtype=jnp.int32)
    pivots = jnp.arange(PB, dtype=jnp.int32)
    corner = hadamard_gram(pivot, pivot, pivots, pivots)
    lower_factor = jnp.linalg.cholesky(corner)
    inverse = lax.linalg.triangular_solve(
        lower_factor, jnp.eye(PB, dtype=jnp.float32), left_side=True, lower=True
    )
    pair_rows = jnp.dot(flat_phi, pivot[0].T, preferred_element_type=jnp.float32) * jnp.dot(
        flat_psi, pivot[1].T, preferred_element_type=jnp.float32
    )
    fitting = jnp.dot(pair_rows, inverse.T, precision=highest).reshape(
        plane_count, line_count, depth_count, PB
    )
    half_count = PB // 2
    packed = jnp.stack([fitting[..., :half_count], fitting[..., half_count:]])
    spectra = transform(packed, "kj,abjh->abkh", depth_count, False)
    device_count = row_count * col_count
    per_device = depth_count * half_count // device_count
    grouped = spectra.reshape(2, plane_count * line_count, device_count, per_device)
    piece = lax.all_to_all(grouped, ("row", "col"), split_axis=2, concat_axis=1, tiled=True)
    item_count = piece.shape[3]
    whole_grid = piece.reshape(2, row_count, col_count, plane_count, line_count, item_count)
    whole_grid = whole_grid.transpose(0, 2, 3, 1, 4, 5).reshape(2, GX, GY, item_count)
    whole_grid = transform(whole_grid, "kj,jbh->kbh", GX, False)
    planes = transform(whole_grid, "kj,ajh->akh", GY, False)
    depth_index = (row_index * col_count + col_index) * per_device + jnp.arange(
        per_device, dtype=jnp.int32
    )
    depth_freq = signed_of(depth_index // half_count, GZ)
    kernel = coulomb_table(signed_frequency(GX, GX), signed_frequency(GY, GY), depth_freq)
    planes = planes * kernel[None]
    planes = transform(planes, "kj,jbh->kbh", GX, True)
    planes = transform(planes, "kj,ajh->akh", GY, True)
    blocked = planes.reshape(2, col_count, plane_count, row_count, line_count, per_device)
    blocked = blocked.transpose(0, 3, 1, 2, 4, 5).reshape(
        2, device_count, plane_count * line_count, per_device
    )
    piece = lax.all_to_all(blocked, ("row", "col"), split_axis=1, concat_axis=3, tiled=True)
    cells_here = piece.shape[2]
    columns = piece.reshape(2, cells_here, depth_count, half_count)
    returned = transform(columns, "kj,ajh->akh", GZ, True)
    returned = returned.reshape(2, plane_count, line_count, depth_count, half_count)
    potential = jnp.concatenate([returned[0], returned[1]], axis=3)
    panel_rows = jnp.dot(
        hadamard_gram(row_samples, pivot, row_global, pivots), inverse.T, precision=highest
    )
    panel_cols = jnp.dot(
        hadamard_gram(col_samples, pivot, col_global, pivots), inverse.T, precision=highest
    )
    schur = hadamard_gram(row_samples, col_samples, row_global, col_global) - jnp.dot(
        panel_rows, panel_cols.T, precision=highest
    )
    return (schur, panel_rows, potential)


def solution(mesh):
    in_specs = (P("col", "row", None, None), P("col", "row", None, None), P(("row", "col")))
    out_specs = (P("row", "col"), P("row", None), P("col", "row", None, None))
    return jax.shard_map(
        on_device, mesh=mesh, in_specs=in_specs, out_specs=out_specs, check_vma=False
    )
```

profile of v0, /device:TPU:1, one launch (start us, length us, event | category | flops | bytes accessed | tf_op | source)
XLA Modules:
  0.0 1772.5 jit_solution(4389014118311483180)
XLA Ops:
  21.1 117.4 %all-gather.2.cloned.1.call-done = bf16[2,16384,256]{2,1,0:T(8,128)(2,1)} async-done(((bf16[2,512,256]{2,1,0:T(8,128)(2,1)}), bf16[2,16384,256]{2,1,0:T(8,128)(2,1)}) %all-gather.2.cloned.1.call-update) | async-done | bytes 16777232 | tf_op jit(solution)/shard_map/all_gather | solution.py:84
  181.0 19.9 %custom-call.15 = f32[2,128,128]{1,2,0:T(8,128)S(1)} custom-call(f32[2,128,128]{2,1,0:T(8,128)S(1)} %get-tuple-element.11), custom_call_target="InvertDiagBlocksLowerTriangular" | custom-call | tf_op jit(solution)/shard_map/triangular_solve | solution.py:93
  213.6 16.4 convolution_multiply_fusion
  230.0 33.2 %fusion.55 = f32[16000,256]{1,0:T(8,128)} fusion(f32[256,16000]{1,0:T(8,128)} %convolution_multiply_fusion, f32[128,256]{1,0:T(8,128)S(1)} %fusion.63, f32[128,256]{1,0:T(8,128)S(1)} %fusion.58), kind=kOutput, calls=%fused_computation.85 | convolution fusion | flops 12582977536 | bytes 33030144 | tf_op jit(solution)/shard_map/dot_general | solution.py:99
  353.8 22.2 %pad_maximum_fusion = f32[2,200,32,320]{3,0,1,2:T(2,128)} fusion(f32[1,200,32,320]{3,0,1,2:T(1,128)} %copy.40, f32[1,200,32,320]{3,0,1,2:T(1,128)S(1)} %copy.39), kind=kLoop, calls=%fused_computation.7 | loop fusion | flops 4096000 | bytes 32768000 | tf_op jit(solution)/shard_map/stack | solution.py:53
  385.3 412.5 %all-to-all-done = f32[2,200,32,320]{3,0,1,2:T(2,128)} async-done(((f32[2,200,32,320]{3,0,1,2:T(2,128)}), f32[2,200,32,320]{3,0,1,2:T(2,128)}, u32[]{:S(2)}, u32[]{:S(2)}) %all-to-all-start) | async-done | bytes 16384032 | tf_op jit(solution)/shard_map/all_to_all | solution.py:108
  797.9 20.0 %fusion.294 = (f32[1,4,20,8,10,320]{5,0,4,2,1,3:T(1,128)}, f32[1,4,20,8,10,320]{5,0,4,2,1,3:T(1,128)S(1)}) fusion(f32[2,4,20,8,10,320]{5,0,4,2,1,3:T(2,128)} %bitcast.28), kind=kLoop, calls=%fused_computation.316 | loop fusion | bytes 32768000 | tf_op jit(solution)/shard_map/slice | solution.py:44
  898.5 16.6 fusion.18
  942.6 15.2 subtract_bitcast_fusion
  957.8 15.5 add_bitcast_fusion
  973.3 17.6 maximum_multiply_fusion
  1025.6 15.4 add_multiply_fusion
  1056.2 15.2 fusion.4
  1071.4 15.8 subtract_multiply_fusion
  1091.0 16.7 multiply_bitcast_fusion
  1125.6 17.2 multiply_bitcast_fusion.1
  1160.8 17.3 maximum_bitcast_fusion
  1178.1 33.4 %copy.57 = f32[2,8,4,20,10,320]{5,0,4,3,2,1:T(2,128)} copy(f32[2,8,4,20,10,320]{5,3,2,4,1,0:T(8,128)} %maximum_bitcast_fusion) | data formatting | bytes 32768000 | tf_op jit(solution)/shard_map/transpose | solution.py:123
  1211.5 22.9 %all-to-all-start.1 = ((f32[2,32,200,320]{3,0,2,1:T(2,128)}), f32[2,32,200,320]{3,0,2,1:T(2,128)}, u32[]{:S(2)}, u32[]{:S(2)}) async-start(f32[2,32,200,320]{3,0,2,1:T(2,128)} %bitcast.195), calls=%async_computation.1 | async-start | bytes 39321600 | tf_op jit(solution)/shard_map/all_to_all | solution.py:126
  1249.9 17.6 fusion.53
  1267.5 31.1 %fusion.295 = f32[2048,4096]{1,0:T(8,128)} fusion(f32[2048,256]{1,0:T(8,128)S(1)} %fusion.57, f32[4096,256]{1,0:T(8,128)S(1)} %fusion.56), kind=kOutput, calls=%fused_computation.317 | convolution fusion | flops 25769803776 | bytes 39845888 | tf_op jit(solution)/shard_map/dot_general | solution.py:138
  1298.6 35.5 %add_subtract_fusion = f32[2048,4096]{1,0:T(8,128)} fusion(f32[2048,4096]{1,0:T(8,128)} %fusion.295, f32[2048,4096]{1,0:T(8,128)} %fusion.53, s32[4096]{0:T(1024)S(1)} %iota_add_fusion, s32[2048]{0:T(1024)S(1)} %iota_add_fusion.1, bf16[2,16384,256]{2,1,0:T(8,128)(2,1)} %all-gather.2.cloned.1.call-done, s32[]{:T(128)S(6)} %add.287, s32[]{:T(128)S(6)} %select_n.139, ...), kind=kOutput, calls=%fused_computation.4 | convolution fusion | flops 4336910336 | bytes 103835648 | tf_op jit(solution)/shard_map/dot_general | solution.py:58
  1334.1 317.5 %all-to-all-done.1 = f32[2,32,200,320]{3,0,2,1:T(2,128)} async-done(((f32[2,32,200,320]{3,0,2,1:T(2,128)}), f32[2,32,200,320]{3,0,2,1:T(2,128)}, u32[]{:S(2)}, u32[]{:S(2)}) %all-to-all-start.1) | async-done | bytes 16384032 | tf_op jit(solution)/shard_map/all_to_all | solution.py:126
  1651.7 20.0 %fusion.293 = (f32[1,1,200,32,320]{4,0,2,3,1:T(1,128)}, f32[1,1,200,32,320]{4,0,2,3,1:T(1,128)S(1)}) fusion(f32[2,1,200,32,320]{4,0,2,3,1:T(2,128)} %bitcast.44), kind=kLoop, calls=%fused_computation.315 | loop fusion | bytes 32768000 | tf_op jit(solution)/shard_map/slice | solution.py:44
  (121 shorter events, 478.2 us)
Async XLA Ops:
  7.2 131.3 %all-gather.2.cloned.1.call-start = ((), (), s32[]{:S(2)}) async-start(), calls=%async_computation.2 | async-start | bytes 17301504 | tf_op jit(solution)/shard_map/all_gather | solution.py:84
  201.1 28.8 %copy-start.8 = (f32[128,256]{1,0:T(8,128)}, f32[128,256]{1,0:T(8,128)S(1)}, u32[]{:S(2)}) copy-start(f32[128,256]{1,0:T(8,128)S(1)} %fusion.58) | copy-start | bytes 393220
  201.7 28.2 %copy-start.10 = (f32[128,256]{1,0:T(8,128)}, f32[128,256]{1,0:T(8,128)S(1)}, u32[]{:S(2)}) copy-start(f32[128,256]{1,0:T(8,128)S(1)} %fusion.63) | copy-start | bytes 393220
  263.2 10.3 copy-start
  376.0 421.9 %all-to-all-start = ((f32[2,200,32,320]{3,0,1,2:T(2,128)}), f32[2,200,32,320]{3,0,1,2:T(2,128)}, u32[]{:S(2)}, u32[]{:S(2)}) async-start(f32[2,200,32,320]{3,0,1,2:T(2,128)} %pad_maximum_fusion), calls=%async_computation | async-start | bytes 39321600 | tf_op jit(solution)/shard_map/all_to_all | solution.py:108
  870.3 15.1 copy-start.2
  898.5 16.6 copy-start.3
  898.5 31.6 %slice-start = ((s8[9830400]{0:T(1024)(128)(4,1)}), s8[4194304]{0:T(1024)(128)(4,1)S(1)}, s32[]{:S(2)}) async-start(s8[9830400]{0:T(1024)(128)(4,1)} %bitcast.193), calls=%async_computation.3 | async-start | bytes 8388608
  898.5 31.6 %slice-start.1 = ((s8[9830400]{0:T(1024)(128)(4,1)}), s8[4194304]{0:T(1024)(128)(4,1)S(1)}, s32[]{:S(2)}) async-start(s8[9830400]{0:T(1024)(128)(4,1)} %bitcast.193), calls=%async_computation.4 | async-start | bytes 8388608
  915.0 15.1 slice-start.2
  942.6 15.3 copy-start.5
  1087.2 3.7 copy-start.1
  1211.5 26.5 %copy-start.9 = (f32[128,256]{1,0:T(8,128)S(1)}, f32[128,256]{1,0:T(8,128)}, u32[]{:S(2)}) copy-start(f32[128,256]{1,0:T(8,128)} %copy-done.8) | copy-start | bytes 393220
  1211.5 26.5 %copy-start.11 = (f32[128,256]{1,0:T(8,128)S(1)}, f32[128,256]{1,0:T(8,128)}, u32[]{:S(2)}) copy-start(f32[128,256]{1,0:T(8,128)} %copy-done.10) | copy-start | bytes 393220
  1211.5 440.1 %all-to-all-start.1 = ((f32[2,32,200,320]{3,0,2,1:T(2,128)}), f32[2,32,200,320]{3,0,2,1:T(2,128)}, u32[]{:S(2)}, u32[]{:S(2)}) async-start(f32[2,32,200,320]{3,0,2,1:T(2,128)} %bitcast.195), calls=%async_computation.1 | async-start | bytes 39321600 | tf_op jit(solution)/shard_map/all_to_all | solution.py:126
  1239.9 27.6 %copy-start.7 = (f32[2048,256]{1,0:T(8,128)}, f32[2048,256]{1,0:T(8,128)S(1)}, u32[]{:S(2)}) copy-start(f32[2048,256]{1,0:T(8,128)S(1)} %fusion.57) | copy-start | bytes 6291460
  1721.8 11.1 copy-start.4
  1721.8 23.3 %slice-start.3 = ((s8[8192000]{0:T(1024)(128)(4,1)}), s8[4194304]{0:T(1024)(128)(4,1)S(1)}, s32[]{:S(2)}) async-start(s8[8192000]{0:T(1024)(128)(4,1)} %bitcast.196), calls=%async_computation.6 | async-start | bytes 8388608
  1732.9 12.2 slice-start.4
  1745.1 10.6 copy-start.6
Sparse Core Ops, SparseCore 0:
  21.1 117.2 all-gather.1
where the time goes:
time: 1800 us; the launch traced here: 1770 us
  waiting for transfers between devices  847 us (47%)
  matrix products  493 us (27%)
  local copies, waits for them, and re-layouts  261 us (14%)
  other arithmetic  127 us (7%)
  starting transfers between devices  27.3 us (2%)
    all_to_all x1, waiting for transfers between devices, on_device(): lax.all_to_all(grouped, ('row', 'col'), split_axis=2, concat_axis=1, tile...  413 us
    all_to_all x1, waiting for transfers between devices, on_device(): lax.all_to_all(blocked, ('row', 'col'), split_axis=1, concat_axis=3, tile...  318 us
    all_gather x1, waiting for transfers between devices, on_device(): lax.all_gather(own_samples, ('row', 'col'), axis=1, tiled=True)  117 us
    dot_general x6, matrix products, transform(): cos_real = jnp.einsum(form, cosine, real_part, precision=highest)  87.9 us
    dot_general x6, matrix products, transform(): sin_real = jnp.einsum(form, sine, real_part, precision=highest)  82.6 us
    dot_general x6, matrix products, transform(): cos_imag = jnp.einsum(form, cosine, imag_part, precision=highest)  81.6 us
    dot_general x6, matrix products, transform(): sin_imag = jnp.einsum(form, sine, imag_part, precision=highest)  76.7 us
    slice x4, local copies, waits for them, and re-layouts, transform(): real_part = stacked[0]  59.4 us
  transfers between devices with their start and end apart: 3, of which 3 were waited for; matrix products, arithmetic and copies ran while one was open for 6% of the time, Pallas kernels for 0%

commit v1 on v0

v1 whole, which is shorter than its diff:
```python
import math

import jax
import jax.numpy as jnp
import ml_dtypes
import numpy as np
from jax import lax
from jax.experimental import pallas as pl
from jax.experimental.pallas import tpu as pltpu
from jax.sharding import PartitionSpec as P


PB = 256
LANES = 128
SHIFT = 4.0
BOX = 2.0
LEVELS = 32767.0
STEPS_PER_OCTAVE = 256.0
MIB = 1 << 20
NT = (((1,), (1,)), ((), ()))
highest = lax.Precision.HIGHEST


def cas_table(length):
    index = np.arange(length)
    angle = (index[:, None] * index[None, :] % length) * (2.0 * math.pi / length)
    table = ((np.cos(angle) + np.sin(angle)) / math.sqrt(length)).astype(np.float32)
    high = table.astype(ml_dtypes.bfloat16)
    low = (table - high.astype(np.float32)).astype(ml_dtypes.bfloat16)
    return np.concatenate([high, high, low], axis=1)


def split(value):
    high = value.astype(jnp.bfloat16)
    return high, (value - high.astype(jnp.float32)).astype(jnp.bfloat16)


def stacked(value):
    high, low = split(value)
    return jnp.concatenate([high, low, high], axis=0)


def transform(table, columns):
    data = jnp.concatenate([stacked(c) for c in columns], axis=1)
    out = jnp.dot(table, data, preferred_element_type=jnp.float32)
    return [out[:, i * LANES : (i + 1) * LANES] for i in range(len(columns))]


def encode(rows, padded):
    count = rows.shape[0]
    peak = jnp.maximum(jnp.max(jnp.abs(rows), axis=0, keepdims=True), 1e-30)
    octave = jnp.ceil(jnp.log2(peak) * STEPS_PER_OCTAVE)
    scale = jnp.exp2(octave * (-1.0 / STEPS_PER_OCTAVE)) * LEVELS
    code = jnp.clip(jnp.round(rows * scale), -LEVELS, LEVELS)
    tail = jnp.broadcast_to(octave, (padded - count, LANES))
    return jnp.concatenate([code, tail], axis=0).astype(jnp.int32).astype(jnp.int16)


def decode(block, count):
    value = block.astype(jnp.int32).astype(jnp.float32)
    scale = jnp.exp2(value[count : count + 1] * (1.0 / STEPS_PER_OCTAVE)) * (1.0 / LEVELS)
    return value[:count] * scale


def source_kernel(group, cells, depth, padded, pieces, *refs):
    phi, psi, pivot_a, pivot_b, inverse, table = refs[:6]
    outs, grid_rows = refs[6:-1], refs[-1]
    step = pl.program_id(0)
    first = lax.dot_general(phi[...], pivot_a[...], NT, preferred_element_type=jnp.float32)
    second = lax.dot_general(psi[...], pivot_b[...], NT, preferred_element_type=jnp.float32)
    pair_high, pair_low = split(first * second)
    inv_high, inv_low = split(inverse[...])
    fitting = (
        lax.dot_general(pair_high, inv_high, NT, preferred_element_type=jnp.float32)
        + lax.dot_general(pair_low, inv_high, NT, preferred_element_type=jnp.float32)
        + lax.dot_general(pair_high, inv_low, NT, preferred_element_type=jnp.float32)
    )
    columns = [fitting[g * depth : (g + 1) * depth] for g in range(group)]
    for g, out in enumerate(transform(table[...], columns)):
        grid_rows[pl.ds(step * group + g, depth, stride=cells), :] = out

    @pl.when(step == pl.num_programs(0) - 1)
    def _():
        base = 0
        for out_ref, count in zip(outs, pieces):

            def one(i, carry, base=base, out_ref=out_ref):
                start = pl.multiple_of((base + i) * cells, math.gcd(cells, 8))
                out_ref[i] = encode(grid_rows[pl.ds(start, cells), :], padded)
                return carry

            lax.fori_loop(0, count, one, 0)
            base += count


def source(phi, psi, pivot_a, pivot_b, inverse, table, cells, depth, padded, pieces):
    group = max(g for g in range(1, 11) if cells % g == 0)
    orbitals = phi.shape[1]
    pivots = pivot_a.shape[0]
    whole = lambda shape: pl.BlockSpec(shape, lambda i: (0,) * len(shape))
    return pl.pallas_call(
        lambda *refs: source_kernel(group, cells, depth, padded, pieces, *refs),
        grid=(cells // group,),
        in_specs=[
            pl.BlockSpec((group * depth, orbitals), lambda i: (i, 0)),
            pl.BlockSpec((group * depth, orbitals), lambda i: (i, 0)),
            whole(pivot_a.shape),
            whole(pivot_b.shape),
            whole(inverse.shape),
            whole(table.shape),
        ],
        out_specs=[whole((n, padded, LANES)) for n in pieces],
        out_shape=[jax.ShapeDtypeStruct((n, padded, LANES), jnp.int16) for n in pieces],
        scratch_shapes=[pltpu.VMEM((depth * cells, LANES), jnp.float32)],
        compiler_params=pltpu.CompilerParams(vmem_limit_bytes=50 * MIB),
        cost_estimate=pl.CostEstimate(
            flops=4 * cells * depth * orbitals * pivots + 10 * cells * depth * pivots * LANES,
            bytes_accessed=4 * cells * depth * orbitals + 2 * depth * padded * LANES,
            transcendentals=0,
        ),
        name="source",
    )(phi, psi, pivot_a, pivot_b, inverse, table)


def middle_kernel(sizes, padded, z_freq, piece, x_table, y_table, out_ref, arrived, spectrum):
    grid_x, grid_y, lines, blocks = sizes
    cells = grid_x * grid_y // blocks
    batch = 4

    def load(i, carry):
        start = pl.multiple_of(i * cells, math.gcd(cells, 8))
        arrived[pl.ds(start, cells), :] = decode(piece[i], cells)
        return carry

    lax.fori_loop(0, blocks, load, 0)

    def line_start(y):
        return y // lines * (grid_x * lines) + y % lines

    def x_forward(i, carry):
        ys = [i * batch + b for b in range(batch)]
        columns = [arrived[pl.ds(line_start(y), grid_x, stride=lines), :] for y in ys]
        for y, out in zip(ys, transform(x_table[...], columns)):
            spectrum[pl.ds(y, grid_x, stride=grid_y), :] = out
        return carry

    lax.fori_loop(0, grid_y // batch, x_forward, 0)

    y_index = lax.broadcasted_iota(jnp.int32, (grid_y, LANES), 0)
    y_freq = jnp.minimum(y_index, grid_y - y_index).astype(jnp.float32)
    z_squared = (z_freq[0] * z_freq[0]).astype(jnp.float32)
    yz_squared = y_freq * y_freq + z_squared

    def y_both(i, carry):
        xs = [i * batch + b for b in range(batch)]
        columns = [spectrum[pl.ds(pl.multiple_of(x * grid_y, 8), grid_y), :] for x in xs]
        scaled = []
        for x, out in zip(xs, transform(y_table[...], columns)):
            x_freq = jnp.minimum(x, grid_x - x)
            squared = yz_squared + (x_freq * x_freq).astype(jnp.float32)
            kernel = BOX * BOX / math.pi / jnp.maximum(squared, 1.0)
            scaled.append(jnp.where(squared > 0.5, kernel, 0.0) * out)
        for x, out in zip(xs, transform(y_table[...], scaled)):
            spectrum[pl.ds(pl.multiple_of(x * grid_y, 8), grid_y), :] = out
        return carry

    lax.fori_loop(0, grid_x // batch, y_both, 0)

    def x_back(i, carry):
        ys = [i * batch + b for b in range(batch)]
        columns = [spectrum[pl.ds(y, grid_x, stride=grid_y), :] for y in ys]
        for y, out in zip(ys, transform(x_table[...], columns)):
            arrived[pl.ds(line_start(y), grid_x, stride=lines), :] = out
        return carry

    lax.fori_loop(0, grid_y // batch, x_back, 0)

    def store(i, carry):
        start = pl.multiple_of(i * cells, math.gcd(cells, 8))
        out_ref[i] = encode(arrived[pl.ds(start, cells), :], padded)
        return carry

    lax.fori_loop(0, blocks, store, 0)


def middle(z_freq, piece, x_table, y_table, grid_x, grid_y, lines):
    blocks, padded, _ = piece.shape
    sizes = (grid_x, grid_y, lines, blocks)
    vmem = pl.BlockSpec(memory_space=pltpu.VMEM)
    points = grid_x * grid_y
    return pl.pallas_call(
        lambda *refs: middle_kernel(sizes, padded, *refs),
        in_specs=[pl.BlockSpec(memory_space=pltpu.SMEM), vmem, vmem, vmem],
        out_specs=vmem,
        out_shape=jax.ShapeDtypeStruct(piece.shape, jnp.int16),
        scratch_shapes=[
            pltpu.VMEM((points, LANES), jnp.float32),
            pltpu.VMEM((points, LANES), jnp.float32),
        ],
        compiler_params=pltpu.CompilerParams(vmem_limit_bytes=32 * MIB),
        cost_estimate=pl.CostEstimate(
            flops=12 * points * LANES * (grid_x + grid_y),
            bytes_accessed=4 * blocks * padded * LANES,
            transcendentals=0,
        ),
        name="middle",
    )(z_freq, piece, x_table, y_table)


def target_kernel(group, cells, depth, spans, aliased, *refs):
    count = len(spans)
    arrived, table = refs[:count], refs[count]
    out_ref, grid_rows = refs[-2:]
    step = pl.program_id(0)

    @pl.when(step == 0)
    def _():
        base = 0
        for piece, (start, number) in zip(arrived, spans):

            def one(i, carry, base=base, start=start, piece=piece):
                row = pl.multiple_of((base + i) * cells, math.gcd(cells, 8))
                grid_rows[pl.ds(row, cells), :] = decode(piece[start + i], cells)
                return carry

            lax.fori_loop(0, number, one, 0)
            base += number

    columns = [
        grid_rows[pl.ds(step * group + g, depth, stride=cells), :] for g in range(group)
    ]
    for g, out in enumerate(transform(table[...], columns)):
        out_ref[pl.ds(g * depth, depth), :] = out


def target(pieces, spans, table, before, half, cells, depth, functions):
    group = max(g for g in range(1, 11) if cells % g == 0)
    whole = lambda shape: pl.BlockSpec(shape, lambda i: (0,) * len(shape))
    in_specs = [whole(p.shape) for p in pieces] + [whole(table.shape)]
    operands = [*pieces, table]
    aliases = {}
    if before is not None:
        in_specs.append(pl.BlockSpec(memory_space=pl.ANY))
        aliases = {len(operands): 0}
        operands.append(before)
    return pl.pallas_call(
        lambda *refs: target_kernel(group, cells, depth, spans, before is not None, *refs),
        grid=(cells // group,),
        in_specs=in_specs,
        out_specs=pl.BlockSpec((group * depth, LANES), lambda i: (i, half)),
        out_shape=jax.ShapeDtypeStruct((cells * depth, functions), jnp.float32),
        scratch_shapes=[pltpu.VMEM((depth * cells, LANES), jnp.float32)],
        input_output_aliases=aliases,
        compiler_params=pltpu.CompilerParams(vmem_limit_bytes=50 * MIB),
        cost_estimate=pl.CostEstimate(
            flops=6 * cells * depth * LANES * depth,
            bytes_accessed=6 * cells * depth * LANES,
            transcendentals=0,
        ),
        name="target",
    )(*operands)


def panel_kernel(first_row, left_a, left_b, pivot_a, pivot_b, inverse, panel, high_ref, low_ref):
    step = pl.program_id(0)
    rows, pivots = panel.shape
    gram = lax.dot_general(left_a[...], pivot_a[...], NT, preferred_element_type=jnp.float32)
    gram *= lax.dot_general(left_b[...], pivot_b[...], NT, preferred_element_type=jnp.float32)
    row = lax.broadcasted_iota(jnp.int32, (rows, pivots), 0) + first_row[0] + step * rows
    gram += jnp.where(row == lax.broadcasted_iota(jnp.int32, (rows, pivots), 1), SHIFT, 0.0)
    value = lax.dot_general(
        gram, inverse[...], NT, precision=highest, preferred_element_type=jnp.float32
    )
    panel[...] = value
    high_ref[...], low_ref[...] = split(value)


def panel_rows(first_row, left, pivot, inverse):
    _, rows, orbitals = left.shape
    pivots = pivot.shape[1]
    tile = math.gcd(rows, 512)
    whole = lambda shape: pl.BlockSpec(shape, lambda i: (0,) * len(shape))
    block = lambda width: pl.BlockSpec((tile, width), lambda i: (i, 0))
    shape = lambda dtype: jax.ShapeDtypeStruct((rows, pivots), dtype)
    return pl.pallas_call(
        panel_kernel,
        grid=(rows // tile,),
        in_specs=[
            pl.BlockSpec(memory_space=pltpu.SMEM),
            block(orbitals),
            block(orbitals),
            whole((pivots, orbitals)),
            whole((pivots, orbitals)),
            whole((pivots, pivots)),
        ],
        out_specs=[block(pivots)] * 3,
        out_shape=[shape(jnp.float32), shape(jnp.bfloat16), shape(jnp.bfloat16)],
        compiler_params=pltpu.CompilerParams(vmem_limit_bytes=32 * MIB),
        cost_estimate=pl.CostEstimate(
            flops=16 * rows * pivots * orbitals,
            bytes_accessed=4 * rows * orbitals + 8 * rows * pivots,
            transcendentals=0,
        ),
        name="panel",
    )(first_row, left[0], left[1], pivot[0], pivot[1], inverse)


def schur_kernel(
    offsets, row_a, row_b, row_high, row_low, col_a, col_b, col_high, col_low, out_ref
):
    rows, cols = out_ref.shape
    product = lambda left, right: lax.dot_general(
        left[...], right[...], NT, preferred_element_type=jnp.float32
    )
    gram = product(row_a, col_a) * product(row_b, col_b)
    update = product(row_high, col_high) + (
        product(row_high, col_low) + product(row_low, col_high)
    )
    row_start = offsets[0] + pl.program_id(0) * rows
    col_start = offsets[1] + pl.program_id(1) * cols
    out_ref[...] = gram - update
    overlap = jnp.logical_and(row_start < col_start + cols, col_start < row_start + rows)

    @pl.when(overlap)
    def _():
        row = lax.broadcasted_iota(jnp.int32, (rows, cols), 0) + row_start
        col = lax.broadcasted_iota(jnp.int32, (rows, cols), 1) + col_start
        out_ref[...] += jnp.where(row == col, SHIFT, 0.0)


def schur_block(offsets, row_side, col_side):
    rows, orbitals = row_side[0].shape
    cols = col_side[0].shape[0]
    row_tile, col_tile = math.gcd(rows, 512), math.gcd(cols, 1024)
    row_block = lambda a: pl.BlockSpec((row_tile, a.shape[1]), lambda i, j: (i, 0))
    col_block = lambda a: pl.BlockSpec((col_tile, a.shape[1]), lambda i, j: (j, 0))
    return pl.pallas_call(
        schur_kernel,
        grid=(rows // row_tile, cols // col_tile),
        in_specs=[
            pl.BlockSpec(memory_space=pltpu.SMEM),
            *[row_block(a) for a in row_side],
            *[col_block(a) for a in col_side],
        ],
        out_specs=pl.BlockSpec((row_tile, col_tile), lambda i, j: (i, j)),
        out_shape=jax.ShapeDtypeStruct((rows, cols), jnp.float32),
        compiler_params=pltpu.CompilerParams(vmem_limit_bytes=50 * MIB),
        cost_estimate=pl.CostEstimate(
            flops=10 * rows * cols * orbitals,
            bytes_accessed=4 * rows * cols + 8 * (rows + cols) * orbitals,
            transcendentals=0,
        ),
        name="schur",
    )(offsets, *row_side, *col_side)


def lower_inverse(corner):
    factor = lax.linalg.cholesky(corner, symmetrize_input=False)
    return factor, lax.linalg.triangular_solve(
        factor, jnp.eye(corner.shape[0], dtype=jnp.float32), left_side=True, lower=True
    )


def on_device(phi, psi, points):
    col_count = lax.axis_size("col")
    row_count = lax.axis_size("row")
    col_index = lax.axis_index("col")
    row_index = lax.axis_index("row")
    axes = ("row", "col")
    devices = row_count * col_count
    me = row_index * col_count + col_index
    plane_count, line_count, depth, orbitals = phi.shape
    grid_x, grid_y = plane_count * col_count, line_count * row_count
    cells = plane_count * line_count
    flat_phi = phi.reshape(cells * depth, orbitals)
    flat_psi = psi.reshape(cells * depth, orbitals)
    owned = points.shape[0]
    half = PB // 2

    global_x = points // (grid_y * depth)
    global_y = points // depth % grid_y
    local_cell = (
        (global_x - col_index * plane_count) * line_count + global_y - row_index * line_count
    ) * depth + points % depth

    slot = jnp.arange(PB, dtype=jnp.int32) - me * owned
    is_owned = jnp.logical_and(slot >= 0, slot < owned)
    pivot_cell = jnp.take(local_cell, jnp.clip(slot, 0, owned - 1), axis=0, mode="clip")
    pivot = jnp.stack(
        [
            jnp.take(flat_phi, pivot_cell, axis=0, mode="clip"),
            jnp.take(flat_psi, pivot_cell, axis=0, mode="clip"),
        ]
    )
    pivot = jnp.where(is_owned[None, :, None], pivot, jnp.zeros_like(pivot))
    pivot = lax.psum(pivot, axes)

    own = jnp.stack(
        [
            jnp.take(flat_phi, local_cell, axis=0, mode="clip"),
            jnp.take(flat_psi, local_cell, axis=0, mode="clip"),
        ]
    )
    swap = [
        (c * row_count + r, r * col_count + c)
        for r in range(row_count)
        for c in range(col_count)
    ]
    crossed = lax.ppermute(own, axes, swap)
    row_samples = lax.all_gather(own, "col", axis=1, tiled=True)
    col_samples = lax.all_gather(crossed, "row", axis=1, tiled=True)

    gram = lambda left, right: lax.dot_general(
        pivot[0, left], pivot[0, right], NT, preferred_element_type=jnp.float32
    ) * lax.dot_general(pivot[1, left], pivot[1, right], NT, preferred_element_type=jnp.float32)
    shift = SHIFT * jnp.eye(half, dtype=jnp.float32)
    lead, rest = slice(0, half), slice(half, PB)
    _, lead_inverse = lower_inverse(gram(lead, lead) + shift)
    matmul = lambda a, b: jnp.dot(a, b, precision=highest)
    coupling = matmul(gram(rest, lead), lead_inverse.T)
    _, rest_inverse = lower_inverse(gram(rest, rest) + shift - matmul(coupling, coupling.T))
    lower_left = -matmul(rest_inverse, matmul(coupling, lead_inverse))
    rest_rows = jnp.concatenate([lower_left, rest_inverse], axis=1)
    lead_rows = jnp.concatenate([lead_inverse, jnp.zeros_like(lead_inverse)], axis=1)
    inverse = jnp.concatenate([lead_rows, rest_rows], axis=0)

    x_table, y_table, z_table = (jnp.asarray(cas_table(n)) for n in (grid_x, grid_y, depth))
    padded = (cells // 16 + 1) * 16
    halves = PB // LANES
    rounds = -(-depth * halves // devices)
    parts = []
    for h in range(halves):
        edges = [h * depth, (h + 1) * depth]
        cuts = [k * devices for k in range(rounds) if edges[0] < k * devices < edges[1]]
        marks = [edges[0], *cuts, edges[1]]
        parts.append([(a // devices, a % devices, b - a) for a, b in zip(marks, marks[1:])])

    outgoing = [[] for _ in range(rounds)]
    for h, rows in enumerate((lead_inverse, rest_rows)):
        used = rows.shape[1]
        made = source(
            flat_phi,
            flat_psi,
            pivot[0, :used],
            pivot[1, :used],
            rows,
            z_table,
            cells,
            depth,
            padded,
            [n for _, _, n in parts[h]],
        )
        for (k, _, _), piece in zip(parts[h], made):
            outgoing[k].append(piece)
    spare = rounds * devices - depth * halves
    if spare:
        outgoing[-1].append(jnp.zeros((spare, padded, LANES), jnp.int16))

    exchange = lambda a: lax.all_to_all(a, axes, split_axis=0, concat_axis=0, tiled=True)
    returned = []
    for k, pieces in enumerate(outgoing):
        sent = pieces[0] if len(pieces) == 1 else jnp.concatenate(pieces, axis=0)
        unit = k * devices + me
        z_index = unit % depth
        z_freq = jnp.minimum(z_index, depth - z_index).astype(jnp.int32).reshape(1)
        back = middle(z_freq, exchange(sent), x_table, y_table, grid_x, grid_y, line_count)
        returned.append(exchange(back))

    potential = None
    for h in range(halves):
        potential = target(
            [returned[k] for k, _, _ in parts[h]],
            [(a, n) for _, a, n in parts[h]],
            z_table,
            potential,
            h,
            cells,
            depth,
            PB,
        )
    potential = potential.reshape(plane_count, line_count, depth, PB)

    row_start = row_index * row_samples.shape[1]
    col_start = col_index * col_samples.shape[1]
    scalar = lambda *v: jnp.stack([jnp.asarray(a, jnp.int32) for a in v])
    panel, row_high, row_low = panel_rows(scalar(row_start), row_samples, pivot, inverse)
    _, col_high, col_low = panel_rows(scalar(col_start), col_samples, pivot, inverse)
    schur = schur_block(
        scalar(row_start, col_start),
        (row_samples[0], row_samples[1], row_high, row_low),
        (col_samples[0], col_samples[1], col_high, col_low),
    )
    return (schur, panel, potential)


def solution(mesh):
    in_specs = (P("col", "row", None, None), P("col", "row", None, None), P(("row", "col")))
    out_specs = (P("row", "col"), P("row", None), P("col", "row", None, None))
    return jax.shard_map(
        on_device, mesh=mesh, in_specs=in_specs, out_specs=out_specs, check_vma=False
    )
```

time: 1800 us -> 826 us (0.46); the launches traced: 1770 us -> 823 us
  waiting for transfers between devices: 847 us -> 332 us
  matrix products: 493 us -> 11.4 us
  Pallas kernels: 0 us -> 228 us
  local copies, waits for them, and re-layouts: 261 us -> 55.8 us
  blocking collectives: 0 us -> 90.1 us
  other arithmetic: 127 us -> 56.7 us
    all_to_all x2 -> x8, waiting for transfers between devices: 730 us -> 143 us  [on_device(): lax.all_to_all(a, axes, split_axis=0, concat_axis=0, tiled=True)]
    dot_general x38 -> x10, matrix products: 492 us -> 9.37 us  [the longest x4 4.19 us: on_device(): matmul = lambda a, b: jnp.dot(a, b, precision=highest)]
    pallas_call x0 -> x12, Pallas kernels: none -> 228 us  [the longest x5 90.5 us: middle(): pl.pallas_call(lambda *refs: middle_kernel(sizes, padded, *refs), in_spec...]
    psum x0 -> x1, waiting for transfers between devices: none -> 126 us  [on_device(): pivot = lax.psum(pivot, axes)]
    all_gather x1 -> x2, waiting for transfers between devices: 117 us -> 0.05 us  [the longest x1 0.03 us: on_device(): row_samples = lax.all_gather(own, 'col', axis=1, tiled=True)]
    all_to_all x0 -> x2, blocking collectives: none -> 90.1 us  [on_device(): lax.all_to_all(a, axes, split_axis=0, concat_axis=0, tiled=True)]
    another operation x15 -> x1, local copies, waits for them, and re-layouts: 73.5 us -> 1.55 us  [lower_inverse(): lax.linalg.triangular_solve(factor, jnp.eye(corner.shape[0], dtype=jnp.fl...]
    slice x6 -> x0, local copies, waits for them, and re-layouts: 71.2 us -> none  [the longest x4 59.4 us: transform(): real_part = stacked[0]]
  transfers between devices with their start and end apart: 3 -> 12, of which waited for: 3 -> 8; matrix products, arithmetic and copies ran while one was open for 6% -> 7% of each run, Pallas kernels for 0% -> 19%
where the time goes in v1:
time: 826 us; the launch traced here: 823 us
  waiting for transfers between devices  332 us (40%)
  Pallas kernels  228 us (28%)
  blocking collectives  90.1 us (11%)
  other arithmetic  56.7 us (7%)
  local copies, waits for them, and re-layouts  55.8 us (7%)
  starting transfers between devices  33.3 us (4%)
  between operations  16.2 us (2%)
  matrix products  11.4 us (1%)
    all_to_all x8, waiting for transfers between devices, on_device(): lax.all_to_all(a, axes, split_axis=0, concat_axis=0, tiled=True)  143 us
    psum x1, waiting for transfers between devices, on_device(): pivot = lax.psum(pivot, axes)  126 us
    pallas_call x5, Pallas kernels, middle(): pl.pallas_call(lambda *refs: middle_kernel(sizes, padded, *refs), in_spec...  90.5 us
    all_to_all x2, blocking collectives, on_device(): lax.all_to_all(a, axes, split_axis=0, concat_axis=0, tiled=True)  90.1 us
    ppermute x1, waiting for transfers between devices, on_device(): crossed = lax.ppermute(own, axes, swap)  62.7 us
    pallas_call x2, Pallas kernels, source(): pl.pallas_call(lambda *refs: source_kernel(group, cells, depth, padded, p...  61.4 us
    pallas_call x1, Pallas kernels, schur_block(): pl.pallas_call(schur_kernel, grid=(rows // row_tile, cols // col_tile), i...  34.5 us
    all_to_all x8, starting transfers between devices, on_device(): lax.all_to_all(a, axes, split_axis=0, concat_axis=0, tiled=True)  29.4 us
  transfers between devices with their start and end apart: 12, of which 8 were waited for; matrix products, arithmetic and copies ran while one was open for 7% of the time, Pallas kernels for 19%

profile of v1, /device:TPU:1, one launch (start us, length us, event | category | flops | bytes accessed | tf_op | source)
XLA Modules:
  0.0 823.0 jit_solution(4449926086844550427)
XLA Ops:
  22.3 126.4 %all-reduce.3.cloned.1.call-done = bf16[2,256,256]{2,1,0:T(8,128)(2,1)} async-done(((bf16[2,256,256]{2,1,0:T(8,128)(2,1)}), bf16[2,256,256]{2,1,0:T(8,128)(2,1)}) %all-reduce.3.cloned.1.call-update) | async-done | bytes 262160 | tf_op jit(solution)/shard_map/psum | solution.py:396
  150.9 11.7 %custom-call.8 = f32[128,128]{1,0:T(8,128)S(1)} custom-call(f32[128,128]{1,0:T(8,128)S(1)} %fusion.1), custom_call_target="Cholesky" | custom-call | tf_op jit(solution)/shard_map/cholesky/custom-call.1 | solution.py:358
  163.9 9.8 %custom-call.9 = f32[1,128,128]{1,2,0:T(8,128)S(1)} custom-call(f32[1,128,128]{2,1,0:T(8,128)S(1)} %fusion.6), custom_call_target="InvertDiagBlocksLowerTriangular" | custom-call | tf_op jit(solution)/shard_map/triangular_solve/custom-call.0 | solution.py:359
  174.9 28.2 %source.2 = (s16[32,208,128]{2,1,0:T(8,128)(2,1)}, s16[32,208,128]{2,1,0:T(8,128)(2,1)}, s16[16,208,128]{2,1,0:T(8,128)(2,1)S(1)}) custom-call(bf16[16000,256]{1,0:T(8,128)(2,1)} %bitcast.67, bf16[16000,256]{1,0:T(8,128)(2,1)} %bitcast.63, bf16[128,256]{1,0:T(8,128)(2,1)S(1)} %get-tuple-element.32.refs_2_, bf16[128,256]{1,0:T(8,128)(2,1)S(1)} %get-tuple-element.31.refs_3_, ...), custom_call_target="tpu_custom_call" | custom-call | flops 4718592000 | bytes 20643840 | tf_op jit(solution)/shard_map/source/pallas_call | solution.py:101
  209.9 39.1 %all-to-all-done.6.refs_1_ = s16[32,208,128]{2,1,0:T(8,128)(2,1)S(1)} async-done(((s16[32,208,128]{2,1,0:T(8,128)(2,1)}), s16[32,208,128]{2,1,0:T(8,128)(2,1)S(1)}, u32[]{:S(2)}, u32[]{:S(2)}) %all-to-all-start.6) | async-done | bytes 1703968 | tf_op jit(solution)/shard_map/all_to_all | solution.py:459
  256.3 13.2 %custom-call.10 = f32[128,128]{1,0:T(8,128)} custom-call(f32[128,128]{1,0:T(8,128)} %convolution_subtract_fusion), custom_call_target="Cholesky" | custom-call | tf_op jit(solution)/shard_map/cholesky/custom-call.1 | solution.py:358
  273.2 11.3 %custom-call.11 = f32[1,128,128]{1,2,0:T(8,128)} custom-call(f32[1,128,128]{2,1,0:T(8,128)} %fusion.7), custom_call_target="InvertDiagBlocksLowerTriangular" | custom-call | tf_op jit(solution)/shard_map/triangular_solve/custom-call.0 | solution.py:359
  291.9 33.1 %source.3 = (s16[16,208,128]{2,1,0:T(8,128)(2,1)S(1)}, s16[32,208,128]{2,1,0:T(8,128)(2,1)S(1)}, s16[32,208,128]{2,1,0:T(8,128)(2,1)}) custom-call(bf16[16000,256]{1,0:T(8,128)(2,1)} %bitcast.68, bf16[16000,256]{1,0:T(8,128)(2,1)} %bitcast.64, bf16[256,256]{1,0:T(8,128)(2,1)S(1)} %get-tuple-element.34.pivot_a.refs_2_, ...), custom_call_target="tpu_custom_call" | custom-call | flops 9437184000 | bytes 20643840 | tf_op jit(solution)/shard_map/source/pallas_call | solution.py:101
  327.6 46.5 %all_to_all.50.refs_1_ = s16[32,208,128]{2,1,0:T(8,128)(2,1)} all-to-all(s16[32,208,128]{2,1,0:T(8,128)(2,1)} %pad_add_fusion), channel_id=1, replica_groups=mesh['row'=8,'col'=4] {'row','col'}, dimensions={0} | all-to-all | bytes 3407872 | tf_op jit(solution)/shard_map/all_to_all | solution.py:459
  374.1 43.6 %all_to_all.51.refs_1_ = s16[32,208,128]{2,1,0:T(8,128)(2,1)} all-to-all(s16[32,208,128]{2,1,0:T(8,128)(2,1)S(1)} %copy-done.17), channel_id=1, replica_groups=mesh['row'=8,'col'=4] {'row','col'}, dimensions={0} | all-to-all | bytes 3407872 | tf_op jit(solution)/shard_map/all_to_all | solution.py:459
  420.8 17.9 %middle.8 = s16[32,208,128]{2,1,0:T(8,128)(2,1)S(1)} custom-call(s32[1]{0:T(128)} %bitcast.26.refs_0_, s16[32,208,128]{2,1,0:T(8,128)(2,1)S(1)} %all-to-all-done.6.refs_1_, bf16[80,240]{1,0:T(8,128)(2,1)S(1)} %copy-done.26, bf16[80,240]{1,0:T(8,128)(2,1)S(1)} %copy-done.26), custom_call_target="tpu_custom_call" | custom-call | flops 1572864000 | bytes 3407872 | tf_op jit(solution)/shard_map/middle/pallas_call | solution.py:191
  439.9 21.0 %all-to-all-done.4.refs_1_ = s16[32,208,128]{2,1,0:T(8,128)(2,1)S(1)} async-done(((s16[32,208,128]{2,1,0:T(8,128)(2,1)}), s16[32,208,128]{2,1,0:T(8,128)(2,1)S(1)}, u32[]{:S(2)}, u32[]{:S(2)}) %all-to-all-start.4) | async-done | bytes 1703968 | tf_op jit(solution)/shard_map/all_to_all | solution.py:459
  466.7 17.9 %middle.9 = s16[32,208,128]{2,1,0:T(8,128)(2,1)S(1)} custom-call(s32[1]{0:T(128)} %bitcast.27.refs_0_, s16[32,208,128]{2,1,0:T(8,128)(2,1)S(1)} %copy-done.10, bf16[80,240]{1,0:T(8,128)(2,1)S(1)} %copy-done.26, bf16[80,240]{1,0:T(8,128)(2,1)S(1)} %copy-done.26), custom_call_target="tpu_custom_call" | custom-call | flops 1572864000 | bytes 3407872 | tf_op jit(solution)/shard_map/middle/pallas_call | solution.py:191
  485.8 19.5 %all-to-all-done.7.refs_0_ = s16[32,208,128]{2,1,0:T(8,128)(2,1)S(1)} async-done(((s16[32,208,128]{2,1,0:T(8,128)(2,1)}), s16[32,208,128]{2,1,0:T(8,128)(2,1)S(1)}, u32[]{:S(2)}, u32[]{:S(2)}) %all-to-all-start.7) | async-done | bytes 1703968 | tf_op jit(solution)/shard_map/all_to_all | solution.py:459
  525.3 17.9 %middle.5 = s16[32,208,128]{2,1,0:T(8,128)(2,1)S(1)} custom-call(s32[1]{0:T(128)} %bitcast.23.refs_0_, s16[32,208,128]{2,1,0:T(8,128)(2,1)S(1)} %copy-done.11, bf16[80,240]{1,0:T(8,128)(2,1)S(1)} %copy-done.26, bf16[80,240]{1,0:T(8,128)(2,1)S(1)} %copy-done.26), custom_call_target="tpu_custom_call" | custom-call | flops 1572864000 | bytes 3407872 | tf_op jit(solution)/shard_map/middle/pallas_call | solution.py:191
  544.3 26.8 %all-to-all-done.9.refs_1_ = s16[32,208,128]{2,1,0:T(8,128)(2,1)S(1)} async-done(((s16[32,208,128]{2,1,0:T(8,128)(2,1)}), s16[32,208,128]{2,1,0:T(8,128)(2,1)S(1)}, u32[]{:S(2)}, u32[]{:S(2)}) %all-to-all-start.9) | async-done | bytes 1703968 | tf_op jit(solution)/shard_map/all_to_all | solution.py:459
  580.8 62.7 %collective-permute-done = bf16[2,512,256]{2,1,0:T(8,128)(2,1)} collective-permute-done((bf16[2,512,256]{2,1,0:T(8,128)(2,1)}, bf16[2,512,256]{2,1,0:T(8,128)(2,1)}, u32[]{:S(2)}, u32[]{:S(2)}) %collective-permute-start) | collective-permute-done | bytes 524320 | tf_op jit(solution)/shard_map/ppermute | solution.py:409
  645.0 17.9 %middle.6 = s16[32,208,128]{2,1,0:T(8,128)(2,1)S(1)} custom-call(s32[1]{0:T(128)} %bitcast.24.refs_0_, s16[32,208,128]{2,1,0:T(8,128)(2,1)S(1)} %copy-done.8, bf16[80,240]{1,0:T(8,128)(2,1)S(1)} %copy-done.26, bf16[80,240]{1,0:T(8,128)(2,1)S(1)} %copy-done.26), custom_call_target="tpu_custom_call" | custom-call | flops 1572864000 | bytes 3407872 | tf_op jit(solution)/shard_map/middle/pallas_call | solution.py:191
  670.7 19.0 %middle.7 = s16[32,208,128]{2,1,0:T(8,128)(2,1)} custom-call(s32[1]{0:T(128)} %bitcast.25.refs_0_, s16[32,208,128]{2,1,0:T(8,128)(2,1)S(1)} %copy-done.7, bf16[80,240]{1,0:T(8,128)(2,1)S(1)} %copy-done.26, bf16[80,240]{1,0:T(8,128)(2,1)S(1)} %copy-done.26), custom_call_target="tpu_custom_call" | custom-call | flops 1572864000 | bytes 3407872 | tf_op jit(solution)/shard_map/middle/pallas_call | solution.py:191
  689.8 19.6 %all-to-all-done.3.refs_1_ = s16[32,208,128]{2,1,0:T(8,128)(2,1)} async-done(((s16[32,208,128]{2,1,0:T(8,128)(2,1)}), s16[32,208,128]{2,1,0:T(8,128)(2,1)}, u32[]{:S(2)}, u32[]{:S(2)}) %all-to-all-start.3) | async-done | bytes 1703968 | tf_op jit(solution)/shard_map/all_to_all | solution.py:459
  722.6 13.4 %target.2.refs_4_ = f32[16000,256]{1,0:T(8,128)} custom-call(s16[32,208,128]{2,1,0:T(8,128)(2,1)S(1)} %all-to-all-done.7.refs_0_, s16[32,208,128]{2,1,0:T(8,128)(2,1)S(1)} %copy-done.3, s16[32,208,128]{2,1,0:T(8,128)(2,1)} %copy-done, bf16[80,240]{1,0:T(8,128)(2,1)S(1)} %copy-done.26), custom_call_target="tpu_custom_call" | custom-call | flops 983040000 | bytes 12288000 | tf_op jit(solution)/shard_map/target/pallas_call | solution.py:246
  736.1 16.6 %all-to-all-done.5.refs_2_ = s16[32,208,128]{2,1,0:T(8,128)(2,1)} async-done(((s16[32,208,128]{2,1,0:T(8,128)(2,1)}), s16[32,208,128]{2,1,0:T(8,128)(2,1)}, u32[]{:S(2)}, u32[]{:S(2)}) %all-to-all-start.5) | async-done | bytes 1703968 | tf_op jit(solution)/shard_map/all_to_all | solution.py:459
  752.7 13.8 %target.3 = f32[16000,256]{1,0:T(8,128)} custom-call(s16[32,208,128]{2,1,0:T(8,128)(2,1)S(1)} %copy-done.1, s16[32,208,128]{2,1,0:T(8,128)(2,1)} %all-to-all-done.3.refs_1_, s16[32,208,128]{2,1,0:T(8,128)(2,1)} %all-to-all-done.5.refs_2_, bf16[80,240]{1,0:T(8,128)(2,1)S(1)} %copy-done.26, f32[16000,256]{1,0:T(8,128)} %target.2.refs_4_), custom_call_target="tpu_custom_call", output_to_operand_aliasing={{}: (4, {})} | custom-call | flops 983040000 | bytes 12288000 | tf_op jit(solution)/shard_map/target/pallas_call | solution.py:246
  781.0 34.5 %schur.1 = f32[2048,4096]{1,0:T(8,128)} custom-call(s32[2]{0:T(128)S(1)} %pad_add_fusion.1.offsets, bf16[2048,256]{1,0:T(8,128)(2,1)S(1)} %copy-done.21, bf16[2048,256]{1,0:T(8,128)(2,1)S(1)} %copy-done.19, bf16[2048,256]{1,0:T(8,128)(2,1)S(1)} %copy-done.34, bf16[2048,256]{1,0:T(8,128)(2,1)} %copy-done.35, bf16[4096,256]{1,0:T(8,128)(2,1)} %copy-done.5, ...), custom_call_target="tpu_custom_call" | custom-call | flops 21474836480 | bytes 46137344 | tf_op jit(solution)/shard_map/schur/pallas_call | solution.py:337
  (147 shorter events, 125.4 us)
Async XLA Ops:
  8.0 140.7 %all-reduce.3.cloned.1.call-start = ((), (), s32[]{:S(2)}) async-start(), calls=%async_computation.11 | async-start | bytes 524288 | tf_op jit(solution)/shard_map/psum | solution.py:396
  16.1 158.8 %copy-start.26 = (bf16[80,240]{1,0:T(8,128)(2,1)S(1)}, bf16[80,240]{1,0:T(8,128)(2,1)}, u32[]{:S(2)}) copy-start(bf16[80,240]{1,0:T(8,128)(2,1)} %constant.102.clone.refs_5_.refs_2_.refs_3_) | copy-start | bytes 115204
  204.1 44.9 %all-to-all-start.6 = ((s16[32,208,128]{2,1,0:T(8,128)(2,1)}), s16[32,208,128]{2,1,0:T(8,128)(2,1)S(1)}, u32[]{:S(2)}, u32[]{:S(2)}) async-start(s16[32,208,128]{2,1,0:T(8,128)(2,1)} %get-tuple-element.25), calls=%async_computation.6 | async-start | bytes 3407872 | tf_op jit(solution)/shard_map/all_to_all | solution.py:459
  249.0 78.6 %all-to-all-start.8 = ((s16[32,208,128]{2,1,0:T(8,128)(2,1)}), s16[32,208,128]{2,1,0:T(8,128)(2,1)S(1)}, u32[]{:S(2)}, u32[]{:S(2)}) async-start(s16[32,208,128]{2,1,0:T(8,128)(2,1)} %get-tuple-element.26), calls=%async_computation.8 | async-start | bytes 3407872 | tf_op jit(solution)/shard_map/all_to_all | solution.py:459
  291.8 33.2 %copy-start.27 = (bf16[256,256]{1,0:T(8,128)(2,1)}, bf16[256,256]{1,0:T(8,128)(2,1)S(1)}, u32[]{:S(2)}) copy-start(bf16[256,256]{1,0:T(8,128)(2,1)S(1)} %get-tuple-element.33.pivot_b.refs_3_) | copy-start | bytes 393220
  291.9 33.2 %copy-start.30 = (bf16[256,256]{1,0:T(8,128)(2,1)}, bf16[256,256]{1,0:T(8,128)(2,1)S(1)}, u32[]{:S(2)}) copy-start(bf16[256,256]{1,0:T(8,128)(2,1)S(1)} %get-tuple-element.34.pivot_a.refs_2_) | copy-start | bytes 393220
  291.9 34.4 %copy-start.23 = (s16[16,208,128]{2,1,0:T(8,128)(2,1)S(1)}, s16[16,208,128]{2,1,0:T(8,128)(2,1)}, u32[]{:S(2)}) copy-start(s16[16,208,128]{2,1,0:T(8,128)(2,1)} %copy-done.22) | copy-start | bytes 2555908
  327.6 46.5 %copy-start.9 = (s16[32,208,128]{2,1,0:T(8,128)(2,1)}, s16[32,208,128]{2,1,0:T(8,128)(2,1)S(1)}, u32[]{:S(2)}) copy-start(s16[32,208,128]{2,1,0:T(8,128)(2,1)S(1)} %all-to-all-done.8.refs_1_) | copy-start | bytes 5111812
  327.6 46.5 %copy-start.17 = (s16[32,208,128]{2,1,0:T(8,128)(2,1)S(1)}, s16[32,208,128]{2,1,0:T(8,128)(2,1)}, u32[]{:S(2)}) copy-start(s16[32,208,128]{2,1,0:T(8,128)(2,1)} %copy-done.16) | copy-start | bytes 5111812
  417.6 43.2 %all-to-all-start.4 = ((s16[32,208,128]{2,1,0:T(8,128)(2,1)}), s16[32,208,128]{2,1,0:T(8,128)(2,1)S(1)}, u32[]{:S(2)}, u32[]{:S(2)}) async-start(s16[32,208,128]{2,1,0:T(8,128)(2,1)} %get-tuple-element.24), calls=%async_computation.4 | async-start | bytes 3407872 | tf_op jit(solution)/shard_map/all_to_all | solution.py:459
  462.1 43.2 %all-to-all-start.7 = ((s16[32,208,128]{2,1,0:T(8,128)(2,1)}), s16[32,208,128]{2,1,0:T(8,128)(2,1)S(1)}, u32[]{:S(2)}, u32[]{:S(2)}) async-start(s16[32,208,128]{2,1,0:T(8,128)(2,1)} %copy-done.15), calls=%async_computation.7 | async-start | bytes 3407872 | tf_op jit(solution)/shard_map/all_to_all | solution.py:459
  505.3 65.8 %all-to-all-start.9 = ((s16[32,208,128]{2,1,0:T(8,128)(2,1)}), s16[32,208,128]{2,1,0:T(8,128)(2,1)S(1)}, u32[]{:S(2)}, u32[]{:S(2)}) async-start(s16[32,208,128]{2,1,0:T(8,128)(2,1)} %copy-done.12), calls=%async_computation.9 | async-start | bytes 3407872 | tf_op jit(solution)/shard_map/all_to_all | solution.py:459
  508.5 204.2 %all-gather.3.cloned.1.call-start = ((), (), s32[]{:S(2)}) async-start(), calls=%async_computation.10 | async-start | bytes 2621440 | tf_op jit(solution)/shard_map/all_gather | solution.py:410
  572.3 91.8 %all-to-all-start.1 = ((s16[32,208,128]{2,1,0:T(8,128)(2,1)}), s16[32,208,128]{2,1,0:T(8,128)(2,1)S(1)}, u32[]{:S(2)}, u32[]{:S(2)}) async-start(s16[32,208,128]{2,1,0:T(8,128)(2,1)} %copy-done.13), calls=%async_computation.1 | async-start | bytes 3407872 | tf_op jit(solution)/shard_map/all_to_all | solution.py:459
  577.2 189.3 %all-gather.5.cloned.1.call-start = ((), (), s32[]{:S(2)}) async-start(), calls=%async_computation.12 | async-start | bytes 4718592 | tf_op jit(solution)/shard_map/all_gather | solution.py:411
  577.3 66.2 %collective-permute-start = (bf16[2,512,256]{2,1,0:T(8,128)(2,1)}, bf16[2,512,256]{2,1,0:T(8,128)(2,1)}, u32[]{:S(2)}, u32[]{:S(2)}) collective-permute-start(bf16[2,512,256]{2,1,0:T(8,128)(2,1)} %pad_maximum_fusion), channel_id=1, source_target_pairs={{0,0},{8,1},{16,2},{24,3},{1,4},{9,5},{17,6},{25,7},{2,8},{10,9},{... | collective-permute-start | bytes 1572872 | tf_op jit(solution)/shard_map/ppermute | solution.py:409
  665.3 44.1 %all-to-all-start.3 = ((s16[32,208,128]{2,1,0:T(8,128)(2,1)}), s16[32,208,128]{2,1,0:T(8,128)(2,1)}, u32[]{:S(2)}, u32[]{:S(2)}) async-start(s16[32,208,128]{2,1,0:T(8,128)(2,1)} %copy-done.14), calls=%async_computation.3 | async-start | bytes 3407872 | tf_op jit(solution)/shard_map/all_to_all | solution.py:459
  689.8 22.8 %copy-start.41 = (f32[128,128]{1,0:T(8,128)S(1)}, f32[128,128]{1,0:T(8,128)}, u32[]{:S(2)}) copy-start(f32[128,128]{1,0:T(8,128)} %copy-done.40) | copy-start | bytes 196612
  689.8 22.9 %copy-start.42 = (f32[128,128]{1,0:T(8,128)S(1)}, f32[128,128]{1,0:T(8,128)}, u32[]{:S(2)}) copy-start(f32[128,128]{1,0:T(8,128)} %copy.13) | copy-start | bytes 196612
  709.3 43.3 %all-to-all-start.5 = ((s16[32,208,128]{2,1,0:T(8,128)(2,1)}), s16[32,208,128]{2,1,0:T(8,128)(2,1)}, u32[]{:S(2)}, u32[]{:S(2)}) async-start(s16[32,208,128]{2,1,0:T(8,128)(2,1)} %middle.7), calls=%async_computation.5 | async-start | bytes 3407872 | tf_op jit(solution)/shard_map/all_to_all | solution.py:459
  722.6 30.1 %copy-start.1 = (s16[32,208,128]{2,1,0:T(8,128)(2,1)S(1)}, s16[32,208,128]{2,1,0:T(8,128)(2,1)}, u32[]{:S(2)}) copy-start(s16[32,208,128]{2,1,0:T(8,128)(2,1)} %copy-done) | copy-start | bytes 5111812
  769.1 11.9 %copy-start.19 = (bf16[2048,256]{1,0:T(8,128)(2,1)S(1)}, bf16[2048,256]{1,0:T(8,128)(2,1)}, u32[]{:S(2)}) copy-start(bf16[2048,256]{1,0:T(8,128)(2,1)} %copy-done.18) | copy-start | bytes 3145732
  769.1 11.9 %copy-start.21 = (bf16[2048,256]{1,0:T(8,128)(2,1)S(1)}, bf16[2048,256]{1,0:T(8,128)(2,1)}, u32[]{:S(2)}) copy-start(bf16[2048,256]{1,0:T(8,128)(2,1)} %copy-done.20) | copy-start | bytes 3145732
  769.1 11.9 %copy-start.34 = (bf16[2048,256]{1,0:T(8,128)(2,1)S(1)}, bf16[2048,256]{1,0:T(8,128)(2,1)}, u32[]{:S(2)}) copy-start(bf16[2048,256]{1,0:T(8,128)(2,1)} %copy-done.33) | copy-start | bytes 3145732
  (31 other events, 74.9 us)
Sparse Core Ops, SparseCore 0:
  22.4 126.2 all-reduce.2
Sparse Core Ops, SparseCore 1:
  523.9 62.3 all-gather.2
  643.6 49.5 all-gather.4

commit v2 on v1

--- a/solution.py
+++ b/solution.py
@@ -21,6 +21,12 @@
 highest = lax.Precision.HIGHEST
 
 
+def cost(micros, moved):
+    return pl.CostEstimate(
+        flops=int(micros * 1.15e9), bytes_accessed=int(moved), transcendentals=0
+    )
+
+
 def cas_table(length):
     index = np.arange(length)
     angle = (index[:, None] * index[None, :] % length) * (2.0 * math.pi / length)
@@ -70,10 +76,9 @@
     second = lax.dot_general(psi[...], pivot_b[...], NT, preferred_element_type=jnp.float32)
     pair_high, pair_low = split(first * second)
     inv_high, inv_low = split(inverse[...])
-    fitting = (
-        lax.dot_general(pair_high, inv_high, NT, preferred_element_type=jnp.float32)
-        + lax.dot_general(pair_low, inv_high, NT, preferred_element_type=jnp.float32)
-        + lax.dot_general(pair_high, inv_low, NT, preferred_element_type=jnp.float32)
+    fitting = product_nt(
+        jnp.concatenate([pair_high, pair_low, pair_high], axis=1),
+        jnp.concatenate([inv_high, inv_high, inv_low], axis=1),
     )
     columns = [fitting[g * depth : (g + 1) * depth] for g in range(group)]
     for g, out in enumerate(transform(table[...], columns)):
@@ -93,7 +98,7 @@
             base += count
 
 
-def source(phi, psi, pivot_a, pivot_b, inverse, table, cells, depth, padded, pieces):
+def source(phi, psi, pivot_a, pivot_b, inverse, half, table, cells, depth, padded, pieces):
     group = max(g for g in range(1, 11) if cells % g == 0)
     orbitals = phi.shape[1]
     pivots = pivot_a.shape[0]
@@ -106,17 +111,15 @@
             pl.BlockSpec((group * depth, orbitals), lambda i: (i, 0)),
             whole(pivot_a.shape),
             whole(pivot_b.shape),
-            whole(inverse.shape),
+            pl.BlockSpec((LANES, pivots), lambda i: (half, 0)),
             whole(table.shape),
         ],
         out_specs=[whole((n, padded, LANES)) for n in pieces],
         out_shape=[jax.ShapeDtypeStruct((n, padded, LANES), jnp.int16) for n in pieces],
         scratch_shapes=[pltpu.VMEM((depth * cells, LANES), jnp.float32)],
         compiler_params=pltpu.CompilerParams(vmem_limit_bytes=50 * MIB),
-        cost_estimate=pl.CostEstimate(
-            flops=4 * cells * depth * orbitals * pivots + 10 * cells * depth * pivots * LANES,
-            bytes_accessed=4 * cells * depth * orbitals + 2 * depth * padded * LANES,
-            transcendentals=0,
+        cost_estimate=cost(
+            cells * depth / 600, 4 * cells * depth * orbitals
         ),
         name="source",
     )(phi, psi, pivot_a, pivot_b, inverse, table)
@@ -183,14 +186,20 @@
     lax.fori_loop(0, blocks, store, 0)
 
 
-def middle(z_freq, piece, x_table, y_table, grid_x, grid_y, lines):
+def middle(z_freq, piece, x_table, y_table, grid_x, grid_y, lines, after):
     blocks, padded, _ = piece.shape
     sizes = (grid_x, grid_y, lines, blocks)
     vmem = pl.BlockSpec(memory_space=pltpu.VMEM)
     points = grid_x * grid_y
     return pl.pallas_call(
-        lambda *refs: middle_kernel(sizes, padded, *refs),
-        in_specs=[pl.BlockSpec(memory_space=pltpu.SMEM), vmem, vmem, vmem],
+        lambda *refs: middle_kernel(sizes, padded, *refs[:4], *refs[4 + len(after) :]),
+        in_specs=[
+            pl.BlockSpec(memory_space=pltpu.SMEM),
+            vmem,
+            vmem,
+            vmem,
+            *[pl.BlockSpec(memory_space=pl.ANY) for _ in after],
+        ],
         out_specs=vmem,
         out_shape=jax.ShapeDtypeStruct(piece.shape, jnp.int16),
         scratch_shapes=[
@@ -198,16 +207,12 @@
             pltpu.VMEM((points, LANES), jnp.float32),
         ],
         compiler_params=pltpu.CompilerParams(vmem_limit_bytes=32 * MIB),
-        cost_estimate=pl.CostEstimate(
-            flops=12 * points * LANES * (grid_x + grid_y),
-            bytes_accessed=4 * blocks * padded * LANES,
-            transcendentals=0,
-        ),
+        cost_estimate=cost(points / 400, 4 * blocks * padded * LANES),
         name="middle",
-    )(z_freq, piece, x_table, y_table)
-
-
-def target_kernel(group, cells, depth, spans, aliased, *refs):
+    )(z_freq, piece, x_table, y_table, *after)
+
+
+def target_kernel(group, cells, depth, spans, *refs):
     count = len(spans)
     arrived, table = refs[:count], refs[count]
     out_ref, grid_rows = refs[-2:]
@@ -244,7 +249,7 @@
         aliases = {len(operands): 0}
         operands.append(before)
     return pl.pallas_call(
-        lambda *refs: target_kernel(group, cells, depth, spans, before is not None, *refs),
+        lambda *refs: target_kernel(group, cells, depth, spans, *refs),
         grid=(cells // group,),
         in_specs=in_specs,
         out_specs=pl.BlockSpec((group * depth, LANES), lambda i: (i, half)),
@@ -252,11 +257,7 @@
         scratch_shapes=[pltpu.VMEM((depth * cells, LANES), jnp.float32)],
         input_output_aliases=aliases,
         compiler_params=pltpu.CompilerParams(vmem_limit_bytes=50 * MIB),
-        cost_estimate=pl.CostEstimate(
-            flops=6 * cells * depth * LANES * depth,
-            bytes_accessed=6 * cells * depth * LANES,
-            transcendentals=0,
-        ),
+        cost_estimate=cost(cells * depth / 1200, 6 * cells * depth * LANES),
         name="target",
     )(*operands)
 
@@ -296,11 +297,7 @@
         out_specs=[block(pivots)] * 3,
         out_shape=[shape(jnp.float32), shape(jnp.bfloat16), shape(jnp.bfloat16)],
         compiler_params=pltpu.CompilerParams(vmem_limit_bytes=32 * MIB),
-        cost_estimate=pl.CostEstimate(
-            flops=16 * rows * pivots * orbitals,
-            bytes_accessed=4 * rows * orbitals + 8 * rows * pivots,
-            transcendentals=0,
-        ),
+        cost_estimate=cost(rows / 400, 4 * rows * orbitals + 8 * rows * pivots),
         name="panel",
     )(first_row, left[0], left[1], pivot[0], pivot[1], inverse)
 
@@ -345,20 +342,92 @@
         out_specs=pl.BlockSpec((row_tile, col_tile), lambda i, j: (i, j)),
         out_shape=jax.ShapeDtypeStruct((rows, cols), jnp.float32),
         compiler_params=pltpu.CompilerParams(vmem_limit_bytes=50 * MIB),
-        cost_estimate=pl.CostEstimate(
-            flops=10 * rows * cols * orbitals,
-            bytes_accessed=4 * rows * cols + 8 * (rows + cols) * orbitals,
-            transcendentals=0,
-        ),
+        cost_estimate=cost(rows * cols / 240000, 4 * rows * cols),
         name="schur",
     )(offsets, *row_side, *col_side)
 
 
-def lower_inverse(corner):
-    factor = lax.linalg.cholesky(corner, symmetrize_input=False)
-    return factor, lax.linalg.triangular_solve(
-        factor, jnp.eye(corner.shape[0], dtype=jnp.float32), left_side=True, lower=True
-    )
+def factor_inverse(matrix):
+    size = matrix.shape[0]
+    strip_rows = 16
+    row = lax.broadcasted_iota(jnp.int32, (size, size), 0)
+    col = lax.broadcasted_iota(jnp.int32, (size, size), 1)
+    work = jnp.concatenate([matrix, jnp.where(row == col, 1.0, 0.0)], axis=1)
+    strip_row = lax.broadcasted_iota(jnp.int32, (strip_rows, size), 0)
+    inverse = []
+    for start in range(0, size, strip_rows):
+        strip = work[start : start + strip_rows]
+        cols = [
+            jnp.broadcast_to(strip[:, start + t : start + t + 1], (strip_rows, size))
+            for t in range(strip_rows)
+        ]
+        diagonal = jnp.ones((strip_rows, size), jnp.float32)
+        for t in range(strip_rows):
+            factor = jnp.where(strip_row > t, cols[t] * (1.0 / cols[t][t : t + 1]), 0.0)
+            diagonal = jnp.where(strip_row == t, cols[t], diagonal)
+            for u in range(t + 1, strip_rows):
+                cols[u] = cols[u] - factor * cols[u][t : t + 1]
+            strip = strip - jnp.concatenate([factor, factor], axis=1) * strip[t : t + 1]
+        root = lax.rsqrt(diagonal)
+        root = root * (1.5 - 0.5 * diagonal * root * root)
+        strip = strip * jnp.concatenate([root, root], axis=1)
+        inverse.append(strip[:, size:])
+        if start + strip_rows < size:
+            work = work - lax.dot_general(
+                strip[:, :size],
+                strip,
+                (((0,), (0,)), ((), ())),
+                precision=highest,
+                preferred_element_type=jnp.float32,
+            )
+    return jnp.concatenate(inverse, axis=0)
+
+
+def product_nt(left, right):
+    return lax.dot_general(left, right, NT, preferred_element_type=jnp.float32)
+
+
+def exact(left, right, dims=(((1,), (0,)), ((), ()))):
+    return lax.dot_general(
+        left, right, dims, precision=highest, preferred_element_type=jnp.float32
+    )
+
+
+def shifted(gram):
+    row = lax.broadcasted_iota(jnp.int32, gram.shape, 0)
+    col = lax.broadcasted_iota(jnp.int32, gram.shape, 1)
+    return gram + jnp.where(row == col, SHIFT, 0.0)
+
+
+def lead_kernel(pivot_a, pivot_b, inverse):
+    a, b = pivot_a[...], pivot_b[...]
+    inverse[...] = factor_inverse(shifted(product_nt(a, a) * product_nt(b, b)))
+
+
+def rest_kernel(pivot_a, pivot_b, lead_inverse, inverse):
+    half = lead_inverse.shape[0]
+    lead = lead_inverse[...]
+    gram = product_nt(pivot_a[pl.ds(half, half), :], pivot_a[...]) * product_nt(
+        pivot_b[pl.ds(half, half), :], pivot_b[...]
+    )
+    coupling = exact(gram[:, :half], lead, NT)
+    rest = factor_inverse(shifted(gram[:, half:]) - exact(coupling, coupling, NT))
+    inverse[pl.ds(0, half), :] = jnp.concatenate([lead, jnp.zeros_like(lead)], axis=1)
+    lower_left = -exact(rest, exact(coupling, lead))
+    inverse[pl.ds(half, half), :] = jnp.concatenate([lower_left, rest], axis=1)
+
+
+def factor_call(kernel, name, size, micros, *operands):
+    vmem = pl.BlockSpec(memory_space=pltpu.VMEM)
+    return pl.pallas_call(
+        kernel,
+        in_specs=[vmem] * len(operands),
+        out_specs=vmem,
+        out_shape=jax.ShapeDtypeStruct((size, size), jnp.float32),
+        compiler_params=pltpu.CompilerParams(vmem_limit_bytes=32 * MIB),
+        cost_estimate=cost(micros, 8 * size * size),
+        name=name,
+    )(*operands)
 
 
 def on_device(phi, psi, points):
@@ -383,24 +452,23 @@
         (global_x - col_index * plane_count) * line_count + global_y - row_index * line_count
     ) * depth + points % depth
 
-    slot = jnp.arange(PB, dtype=jnp.int32) - me * owned
-    is_owned = jnp.logical_and(slot >= 0, slot < owned)
-    pivot_cell = jnp.take(local_cell, jnp.clip(slot, 0, owned - 1), axis=0, mode="clip")
-    pivot = jnp.stack(
-        [
-            jnp.take(flat_phi, pivot_cell, axis=0, mode="clip"),
-            jnp.take(flat_psi, pivot_cell, axis=0, mode="clip"),
-        ]
-    )
-    pivot = jnp.where(is_owned[None, :, None], pivot, jnp.zeros_like(pivot))
-    pivot = lax.psum(pivot, axes)
-
     own = jnp.stack(
         [
             jnp.take(flat_phi, local_cell, axis=0, mode="clip"),
             jnp.take(flat_psi, local_cell, axis=0, mode="clip"),
         ]
     )
+    exchange = lambda a: lax.all_to_all(a, axes, split_axis=0, concat_axis=0, tiled=True)
+
+    held = min(owned, PB)
+    piece_rows = 2 * PB // devices
+    offered = jnp.concatenate([own[:, :held]] * (PB // held), axis=1)
+    offered = exchange(offered.reshape(devices, piece_rows, orbitals))
+    owner = me * piece_rows % PB // owned
+    piece = lax.dynamic_index_in_dim(offered, owner, axis=0, keepdims=True)
+    pivot = exchange(jnp.broadcast_to(piece, offered.shape)).reshape(2, PB, orbitals)
+
+    own, pivot = lax.optimization_barrier((own, pivot))
     swap = [
         (c * row_count + r, r * col_count + c)
         for r in range(row_count)
@@ -410,19 +478,8 @@
     row_samples = lax.all_gather(own, "col", axis=1, tiled=True)
     col_samples = lax.all_gather(crossed, "row", axis=1, tiled=True)
 
-    gram = lambda left, right: lax.dot_general(
-        pivot[0, left], pivot[0, right], NT, preferred_element_type=jnp.float32
-    ) * lax.dot_general(pivot[1, left], pivot[1, right], NT, preferred_element_type=jnp.float32)
-    shift = SHIFT * jnp.eye(half, dtype=jnp.float32)
-    lead, rest = slice(0, half), slice(half, PB)
-    _, lead_inverse = lower_inverse(gram(lead, lead) + shift)
-    matmul = lambda a, b: jnp.dot(a, b, precision=highest)
-    coupling = matmul(gram(rest, lead), lead_inverse.T)
-    _, rest_inverse = lower_inverse(gram(rest, rest) + shift - matmul(coupling, coupling.T))
-    lower_left = -matmul(rest_inverse, matmul(coupling, lead_inverse))
-    rest_rows = jnp.concatenate([lower_left, rest_inverse], axis=1)
-    lead_rows = jnp.concatenate([lead_inverse, jnp.zeros_like(lead_inverse)], axis=1)
-    inverse = jnp.concatenate([lead_rows, rest_rows], axis=0)
+    lead_inverse = factor_call(lead_kernel, "lead", half, 10, pivot[0, :half], pivot[1, :half])
+    inverse = factor_call(rest_kernel, "rest", PB, 14, pivot[0], pivot[1], lead_inverse)
 
     x_table, y_table, z_table = (jnp.asarray(cas_table(n)) for n in (grid_x, grid_y, depth))
     padded = (cells // 16 + 1) * 16
@@ -436,7 +493,7 @@
         parts.append([(a // devices, a % devices, b - a) for a, b in zip(marks, marks[1:])])
 
     outgoing = [[] for _ in range(rounds)]
-    for h, rows in enumerate((lead_inverse, rest_rows)):
+    for h, rows in enumerate((lead_inverse, inverse)):
         used = rows.shape[1]
         made = source(
             flat_phi,
@@ -444,6 +501,7 @@
             pivot[0, :used],
             pivot[1, :used],
             rows,
+            h,
             z_table,
             cells,
             depth,
@@ -456,15 +514,50 @@
     if spare:
         outgoing[-1].append(jnp.zeros((spare, padded, LANES), jnp.int16))
 
-    exchange = lambda a: lax.all_to_all(a, axes, split_axis=0, concat_axis=0, tiled=True)
-    returned = []
-    for k, pieces in enumerate(outgoing):
-        sent = pieces[0] if len(pieces) == 1 else jnp.concatenate(pieces, axis=0)
-        unit = k * devices + me
-        z_index = unit % depth
-        z_freq = jnp.minimum(z_index, depth - z_index).astype(jnp.int32).reshape(1)
-        back = middle(z_freq, exchange(sent), x_table, y_table, grid_x, grid_y, line_count)
-        returned.append(exchange(back))
+    row_start = row_index * row_samples.shape[1]
+    col_start = col_index * col_samples.shape[1]
+    scalar = lambda *v: jnp.stack([jnp.asarray(a, jnp.int32) for a in v])
+    panel, row_high, row_low = panel_rows(scalar(row_start), row_samples, pivot, inverse)
+    _, col_high, col_low = panel_rows(scalar(col_start), col_samples, pivot, inverse)
+    schur = schur_block(
+        scalar(row_start, col_start),
+        (row_samples[0], row_samples[1], row_high, row_low),
+        (col_samples[0], col_samples[1], col_high, col_low),
+    )
+
+    waits = [[] for _ in range(rounds)]
+    waits[0] += [made[-1], row_samples, col_samples]
+    waits[min(2, rounds - 1)] += [row_high, col_high]
+    waits[min(3, rounds - 1)] += [schur]
+    latest = None
+
+    def in_turn(block):
+        nonlocal latest
+        if latest is not None:
+            block, latest = lax.optimization_barrier((block, latest))
+        latest = exchange(block)
+        return latest
+
+    arrived, returned = [], []
+    for k in range(rounds + 1):
+        if k < rounds:
+            pieces = outgoing[k]
+            sent = pieces[0] if len(pieces) == 1 else jnp.concatenate(pieces, axis=0)
+            arrived.append(in_turn(sent))
+        if k > 0:
+            z_index = ((k - 1) * devices + me) % depth
+            z_freq = jnp.minimum(z_index, depth - z_index).astype(jnp.int32).reshape(1)
+            back = middle(
+                z_freq,
+                arrived[k - 1],
+                x_table,
+                y_table,
+                grid_x,
+                grid_y,
+                line_count,
+                waits[k - 1],
+            )
+            returned.append(in_turn(back))
 
     potential = None
     for h in range(halves):
@@ -479,17 +572,6 @@
             PB,
         )
     potential = potential.reshape(plane_count, line_count, depth, PB)
-
-    row_start = row_index * row_samples.shape[1]
-    col_start = col_index * col_samples.shape[1]
-    scalar = lambda *v: jnp.stack([jnp.asarray(a, jnp.int32) for a in v])
-    panel, row_high, row_low = panel_rows(scalar(row_start), row_samples, pivot, inverse)
-    _, col_high, col_low = panel_rows(scalar(col_start), col_samples, pivot, inverse)
-    schur = schur_block(
-        scalar(row_start, col_start),
-        (row_samples[0], row_samples[1], row_high, row_low),
-        (col_samples[0], col_samples[1], col_high, col_low),
-    )
     return (schur, panel, potential)
 
 

time: 826 us -> 649 us (0.79)
  blocking collectives: 90.1 us -> 0 us
  other arithmetic: 56.7 us -> 5.08 us
  waiting for transfers between devices: 332 us -> 292 us
  starting transfers between devices: 33.3 us -> 49.9 us
  Pallas kernels: 228 us -> 240 us
  matrix products: 11.4 us -> 0 us
  local copies, waits for them, and re-layouts: 55.8 us -> 44.9 us
    psum x1 -> x0, waiting for transfers between devices: 126 us -> none  [on_device(): pivot = lax.psum(pivot, axes)]
    all_to_all x8 -> x12, waiting for transfers between devices: 143 us -> 234 us  [on_device(): lax.all_to_all(a, axes, split_axis=0, concat_axis=0, tiled=True)]
    all_to_all x2 -> x0, blocking collectives: 90.1 us -> none  [on_device(): lax.all_to_all(a, axes, split_axis=0, concat_axis=0, tiled=True)]
    another operation x10 -> x0, other arithmetic: 51 us -> none  [the longest x6 27.1 us: lower_inverse(): factor = lax.linalg.cholesky(corner, symmetrize_input=False)]
    all_to_all x8 -> x12, starting transfers between devices: 29.4 us -> 47.1 us  [on_device(): lax.all_to_all(a, axes, split_axis=0, concat_axis=0, tiled=True)]
    pallas_call x7 -> x9, Pallas kernels: 118 us -> 132 us  [the longest x5 93.5 us: middle(): pl.pallas_call(lambda *refs: middle_kernel(sizes, padded, *refs[:4], *ref...]
    gather x3 -> x0, local copies, waits for them, and re-layouts: 12.6 us -> none  [the longest x1 5.35 us: on_device(): jnp.take(flat_phi, pivot_cell, axis=0, mode='clip')]
    dot_general x10 -> x0, matrix products: 9.37 us -> none  [the longest x4 4.19 us: on_device(): matmul = lambda a, b: jnp.dot(a, b, precision=highest)]
  transfers between devices with their start and end apart: 12 -> 15, of which waited for: 8 -> 11; matrix products, arithmetic and copies ran while one was open for 7% -> 1% of each run, Pallas kernels for 19% -> 35%
where the time goes in v2:
time: 649 us; the launch traced here: 646 us
  waiting for transfers between devices  292 us (45%)
  Pallas kernels  240 us (37%)
  starting transfers between devices  49.9 us (8%)
  local copies, waits for them, and re-layouts  44.9 us (7%)
  between operations  14.6 us (2%)
    all_to_all x12, waiting for transfers between devices, on_device(): lax.all_to_all(a, axes, split_axis=0, concat_axis=0, tiled=True)  234 us
    pallas_call x5, Pallas kernels, middle(): pl.pallas_call(lambda *refs: middle_kernel(sizes, padded, *refs[:4], *ref...  93.5 us
    pallas_call x2, Pallas kernels, source(): pl.pallas_call(lambda *refs: source_kernel(group, cells, depth, padded, p...  59.7 us
    ppermute x1, waiting for transfers between devices, on_device(): crossed = lax.ppermute(own, axes, swap)  58.3 us
    all_to_all x12, starting transfers between devices, on_device(): lax.all_to_all(a, axes, split_axis=0, concat_axis=0, tiled=True)  47.1 us
    pallas_call x1, Pallas kernels, schur_block(): pl.pallas_call(schur_kernel, grid=(rows // row_tile, cols // col_tile), i...  34.5 us
    unnamed x80, local copies, waits for them, and re-layouts  29.6 us
    pallas_call x2, Pallas kernels, target(): pl.pallas_call(lambda *refs: target_kernel(group, cells, depth, spans, *r...  27.2 us
  transfers between devices with their start and end apart: 15, of which 11 were waited for; matrix products, arithmetic and copies ran while one was open for 1% of the time, Pallas kernels for 35%

profile of v2, /device:TPU:1, one launch (start us, length us, event | category | flops | bytes accessed | tf_op | source)
XLA Modules:
  0.0 646.3 jit_solution(2511112575928315860)
XLA Ops:
  7.9 5.9 gather_fusion.1
  13.8 5.9 gather_fusion
  20.5 7.1 %all-to-all-start = ((bf16[32,16,256]{2,1,0:T(8,128)(2,1)}), bf16[32,16,256]{2,1,0:T(8,128)(2,1)S(1)}, u32[]{:S(2)}, u32[]{:S(2)}) async-start(bf16[32,16,256]{2,1,0:T(8,128)(2,1)} %bitcast.6), calls=%async_computation | async-start | bytes 524288 | tf_op jit(solution)/shard_map/all_to_all | solution.py:461
  27.7 10.3 %all-to-all-done = bf16[32,16,256]{2,1,0:T(8,128)(2,1)S(1)} async-done(((bf16[32,16,256]{2,1,0:T(8,128)(2,1)}), bf16[32,16,256]{2,1,0:T(8,128)(2,1)S(1)}, u32[]{:S(2)}, u32[]{:S(2)}) %all-to-all-start) | async-done | bytes 262176 | tf_op jit(solution)/shard_map/all_to_all | solution.py:461
  42.2 9.4 %all-to-all-done.1 = bf16[32,16,256]{2,1,0:T(8,128)(2,1)S(1)} async-done(((bf16[32,16,256]{2,1,0:T(8,128)(2,1)}), bf16[32,16,256]{2,1,0:T(8,128)(2,1)S(1)}, u32[]{:S(2)}, u32[]{:S(2)}) %all-to-all-start.1) | async-done | bytes 262176 | tf_op jit(solution)/shard_map/all_to_all | solution.py:461
  59.5 58.3 %collective-permute-done = bf16[2,512,256]{2,1,0:T(8,128)(2,1)S(1)} collective-permute-done((bf16[2,512,256]{2,1,0:T(8,128)(2,1)}, bf16[2,512,256]{2,1,0:T(8,128)(2,1)S(1)}, u32[]{:S(2)}, u32[]{:S(2)}) %collective-permute-start) | collective-permute-done | bytes 524320 | tf_op jit(solution)/shard_map/ppermute | solution.py:477
  118.6 26.0 %source.2 = (s16[32,208,128]{2,1,0:T(8,128)(2,1)}, s16[32,208,128]{2,1,0:T(8,128)(2,1)}, s16[16,208,128]{2,1,0:T(8,128)(2,1)S(1)}) custom-call(bf16[16000,256]{1,0:T(8,128)(2,1)} %bitcast.42, bf16[16000,256]{1,0:T(8,128)(2,1)} %bitcast.39, bf16[128,256]{1,0:T(8,128)(2,1)S(1)} %get-tuple-element.52.pivot_a.refs_2_, ...), custom_call_target="tpu_custom_call" | custom-call | flops 30666665984 | bytes 16384000 | tf_op jit(solution)/shard_map/source/pallas_call | solution.py:106
  156.1 32.7 %all-to-all-done.2.refs_1_ = s16[32,208,128]{2,1,0:T(8,128)(2,1)S(1)} async-done(((s16[32,208,128]{2,1,0:T(8,128)(2,1)}), s16[32,208,128]{2,1,0:T(8,128)(2,1)S(1)}, u32[]{:S(2)}, u32[]{:S(2)}) %all-to-all-start.2) | async-done | bytes 1703968 | tf_op jit(solution)/shard_map/all_to_all | solution.py:461
  194.7 33.7 %source.3 = (s16[16,208,128]{2,1,0:T(8,128)(2,1)S(1)}, s16[32,208,128]{2,1,0:T(8,128)(2,1)}, s16[32,208,128]{2,1,0:T(8,128)(2,1)}) custom-call(bf16[16000,256]{1,0:T(8,128)(2,1)} %bitcast.43, bf16[16000,256]{1,0:T(8,128)(2,1)} %bitcast.40, bf16[256,256]{1,0:T(8,128)(2,1)S(1)} %copy-done.22, bf16[256,256]{1,0:T(8,128)(2,1)S(1)} %get-tuple-element.53.pivot_b.refs_3_, ...), custom_call_target="tpu_custom_call" | custom-call | flops 30666665984 | bytes 16384000 | tf_op jit(solution)/shard_map/source/pallas_call | solution.py:106
  233.9 17.9 %middle.5 = s16[32,208,128]{2,1,0:T(8,128)(2,1)S(1)} custom-call(s32[1]{0:T(128)} %bitcast.18.refs_0_, s16[32,208,128]{2,1,0:T(8,128)(2,1)S(1)} %all-to-all-done.2.refs_1_, bf16[80,240]{1,0:T(8,128)(2,1)S(1)} %copy-done.26, bf16[80,240]{1,0:T(8,128)(2,1)S(1)} %copy-done.26, s16[32,208,128]{2,1,0:T(8,128)(2,1)} %get-tuple-element.44.refs_4_, ...), custom_call_target="tpu_custom_call" | custom-call | flops 18400000000 | bytes 3407872 | tf_op jit(solution)/shard_map/middle/pallas_call | solution.py:194
  261.5 37.4 %all-to-all-done.4.refs_0_ = s16[32,208,128]{2,1,0:T(8,128)(2,1)S(1)} async-done(((s16[32,208,128]{2,1,0:T(8,128)(2,1)}), s16[32,208,128]{2,1,0:T(8,128)(2,1)S(1)}, u32[]{:S(2)}, u32[]{:S(2)}) %all-to-all-start.4) | async-done | bytes 1703968 | tf_op jit(solution)/shard_map/all_to_all | solution.py:461
  302.9 17.9 %middle.7 = s16[32,208,128]{2,1,0:T(8,128)(2,1)S(1)} custom-call(s32[1]{0:T(128)} %bitcast.19.refs_0_, s16[32,208,128]{2,1,0:T(8,128)(2,1)S(1)} %all-to-all-done.3.refs_1_, bf16[80,240]{1,0:T(8,128)(2,1)S(1)} %copy-done.27, bf16[80,240]{1,0:T(8,128)(2,1)S(1)} %copy-done.27), custom_call_target="tpu_custom_call" | custom-call | flops 18400000000 | bytes 3407872 | tf_op jit(solution)/shard_map/middle/pallas_call | solution.py:194
  322.0 20.3 %all-to-all-done.5.refs_1_ = s16[32,208,128]{2,1,0:T(8,128)(2,1)} async-done(((s16[32,208,128]{2,1,0:T(8,128)(2,1)}), s16[32,208,128]{2,1,0:T(8,128)(2,1)}, u32[]{:S(2)}, u32[]{:S(2)}) %all-to-all-start.5) | async-done | bytes 1703968 | tf_op jit(solution)/shard_map/all_to_all | solution.py:461
  354.5 31.2 %all-to-all-done.6.refs_1_ = s16[32,208,128]{2,1,0:T(8,128)(2,1)} async-done(((s16[32,208,128]{2,1,0:T(8,128)(2,1)}), s16[32,208,128]{2,1,0:T(8,128)(2,1)}, u32[]{:S(2)}, u32[]{:S(2)}) %all-to-all-start.6) | async-done | bytes 1703968 | tf_op jit(solution)/shard_map/all_to_all | solution.py:461
  391.5 9.1 %panel.3 = (f32[4096,256]{1,0:T(8,128)}, bf16[4096,256]{1,0:T(8,128)(2,1)S(1)}, bf16[4096,256]{1,0:T(8,128)(2,1)S(1)}) custom-call(s32[1]{0:T(128)} %bitcast.1.first_row, bf16[4096,256]{1,0:T(8,128)(2,1)S(1)} %get-tuple-element.48.left_a.col_a, bf16[4096,256]{1,0:T(8,128)(2,1)S(1)} %get-tuple-element.47.left_b.col_b, bf16[256,256]{1,0:T(8,128)(2,1)S(1)} %copy-done.23, ...), custom_call_target="tpu_custom_call" | custom-call | flops 11776000000 | bytes 12582912 | tf_op jit(solution)/shard_map/panel/pallas_call | solution.py:286
  402.0 20.5 %middle.6 = s16[32,208,128]{2,1,0:T(8,128)(2,1)} custom-call(s32[1]{0:T(128)} %bitcast.17.refs_0_, s16[32,208,128]{2,1,0:T(8,128)(2,1)} %all-to-all-done.5.refs_1_, bf16[80,240]{1,0:T(8,128)(2,1)S(1)} %copy-done.28, bf16[80,240]{1,0:T(8,128)(2,1)S(1)} %copy-done.28, bf16[2048,256]{1,0:T(8,128)(2,1)S(1)} %get-tuple-element.27.row_high.refs_4_, ...), custom_call_target="tpu_custom_call" | custom-call | flops 18400000000 | bytes 3407872 | tf_op jit(solution)/shard_map/middle/pallas_call | solution.py:194
  432.4 40.0 %all-to-all-done.8.refs_2_.refs_0_ = s16[32,208,128]{2,1,0:T(8,128)(2,1)S(1)} async-done(((s16[32,208,128]{2,1,0:T(8,128)(2,1)}), s16[32,208,128]{2,1,0:T(8,128)(2,1)S(1)}, u32[]{:S(2)}, u32[]{:S(2)}) %all-to-all-start.8) | async-done | bytes 1703968 | tf_op jit(solution)/shard_map/all_to_all | solution.py:461
  479.2 34.5 %schur.1.refs_4_ = f32[2048,4096]{1,0:T(8,128)} custom-call(s32[2]{0:T(128)S(1)} %pad_add_fusion.1.offsets, bf16[2048,256]{1,0:T(8,128)(2,1)S(1)} %copy-done.18, bf16[2048,256]{1,0:T(8,128)(2,1)S(1)} %copy-done.16, bf16[2048,256]{1,0:T(8,128)(2,1)S(1)} %copy-done.31, bf16[2048,256]{1,0:T(8,128)(2,1)} %copy-done.32, bf16[4096,256]{1,0:T(8,128)(2,1)} %copy-done.4, ...), custom_call_target="tpu_custom_call" | custom-call | flops 40195411968 | bytes 33554432 | tf_op jit(solution)/shard_map/schur/pallas_call | solution.py:334
  513.7 19.3 %middle.8 = s16[32,208,128]{2,1,0:T(8,128)(2,1)S(1)} custom-call(s32[1]{0:T(128)} %bitcast.20.refs_0_, s16[32,208,128]{2,1,0:T(8,128)(2,1)} %all-to-all-done.7.refs_1_, bf16[80,240]{1,0:T(8,128)(2,1)S(1)} %copy-done.29, bf16[80,240]{1,0:T(8,128)(2,1)S(1)} %copy-done.29, f32[2048,4096]{1,0:T(8,128)} %schur.1.refs_4_), custom_call_target="tpu_custom_call" | custom-call | flops 18400000000 | bytes 3407872 | tf_op jit(solution)/shard_map/middle/pallas_call | solution.py:194
  540.2 17.9 %middle.9 = s16[32,208,128]{2,1,0:T(8,128)(2,1)S(1)} custom-call(s32[1]{0:T(128)} %bitcast.21.refs_0_, s16[32,208,128]{2,1,0:T(8,128)(2,1)S(1)} %all-to-all-done.9.refs_1_, bf16[80,240]{1,0:T(8,128)(2,1)S(1)} %copy-done.29, bf16[80,240]{1,0:T(8,128)(2,1)S(1)} %copy-done.29), custom_call_target="tpu_custom_call" | custom-call | flops 18400000000 | bytes 3407872 | tf_op jit(solution)/shard_map/middle/pallas_call | solution.py:194
  559.2 21.0 %all-to-all-done.10.refs_1_ = s16[32,208,128]{2,1,0:T(8,128)(2,1)S(1)} async-done(((s16[32,208,128]{2,1,0:T(8,128)(2,1)}), s16[32,208,128]{2,1,0:T(8,128)(2,1)S(1)}, u32[]{:S(2)}, u32[]{:S(2)}) %all-to-all-start.10) | async-done | bytes 1703968 | tf_op jit(solution)/shard_map/all_to_all | solution.py:461
  584.7 13.9 %target.2.refs_4_ = f32[16000,256]{1,0:T(8,128)} custom-call(s16[32,208,128]{2,1,0:T(8,128)(2,1)S(1)} %copy-done.6, s16[32,208,128]{2,1,0:T(8,128)(2,1)} %all-to-all-done.6.refs_1_, s16[32,208,128]{2,1,0:T(8,128)(2,1)} %copy-done.7, bf16[80,240]{1,0:T(8,128)(2,1)S(1)} %copy-done.29), custom_call_target="tpu_custom_call" | custom-call | flops 15333332992 | bytes 12288000 | tf_op jit(solution)/shard_map/target/pallas_call | solution.py:251
  598.6 26.2 %all-to-all-done.11.refs_2_ = s16[32,208,128]{2,1,0:T(8,128)(2,1)} async-done(((s16[32,208,128]{2,1,0:T(8,128)(2,1)}), s16[32,208,128]{2,1,0:T(8,128)(2,1)}, u32[]{:S(2)}, u32[]{:S(2)}) %all-to-all-start.11) | async-done | bytes 1703968 | tf_op jit(solution)/shard_map/all_to_all | solution.py:461
  626.2 13.3 %target.3 = f32[16000,256]{1,0:T(8,128)} custom-call(s16[32,208,128]{2,1,0:T(8,128)(2,1)S(1)} %copy-done.8, s16[32,208,128]{2,1,0:T(8,128)(2,1)S(1)} %copy-done.10, s16[32,208,128]{2,1,0:T(8,128)(2,1)} %all-to-all-done.11.refs_2_, bf16[80,240]{1,0:T(8,128)(2,1)S(1)} %copy-done.29, f32[16000,256]{1,0:T(8,128)} %target.2.refs_4_), custom_call_target="tpu_custom_call", output_to_operand_aliasing={{}: (4, {})} | custom-call | flops 15333332992 | bytes 12288000 | tf_op jit(solution)/shard_map/target/pallas_call | solution.py:251
  (116 shorter events, 102.1 us)
Async XLA Ops:
  20.5 17.4 %all-to-all-start = ((bf16[32,16,256]{2,1,0:T(8,128)(2,1)}), bf16[32,16,256]{2,1,0:T(8,128)(2,1)S(1)}, u32[]{:S(2)}, u32[]{:S(2)}) async-start(bf16[32,16,256]{2,1,0:T(8,128)(2,1)} %bitcast.6), calls=%async_computation | async-start | bytes 524288 | tf_op jit(solution)/shard_map/all_to_all | solution.py:461
  38.7 12.9 %all-to-all-start.1 = ((bf16[32,16,256]{2,1,0:T(8,128)(2,1)}), bf16[32,16,256]{2,1,0:T(8,128)(2,1)S(1)}, u32[]{:S(2)}, u32[]{:S(2)}) async-start(bf16[32,16,256]{2,1,0:T(8,128)(2,1)} %broadcast_in_dim.14), calls=%async_computation.1 | async-start | bytes 524288 | tf_op jit(solution)/shard_map/all_to_all | solution.py:461
  41.3 188.0 %all-gather.3.cloned.1.call-start = ((), (), s32[]{:S(2)}) async-start(), calls=%async_computation.12 | async-start | bytes 2621440 | tf_op jit(solution)/shard_map/all_gather | solution.py:478
  51.6 177.7 %all-gather.5.cloned.1.call-start = ((), (), s32[]{:S(2)}) async-start(), calls=%async_computation.13 | async-start | bytes 4718592 | tf_op jit(solution)/shard_map/all_gather | solution.py:479
  51.7 66.1 %collective-permute-start = (bf16[2,512,256]{2,1,0:T(8,128)(2,1)}, bf16[2,512,256]{2,1,0:T(8,128)(2,1)S(1)}, u32[]{:S(2)}, u32[]{:S(2)}) collective-permute-start(bf16[2,512,256]{2,1,0:T(8,128)(2,1)} %pad_maximum_fusion), channel_id=1, source_target_pairs={{0,0},{8,1},{16,2},{24,3},{1,4},{9,5},{17,6},{25,7},{2,8},{10,9},{... | collective-permute-start | bytes 1572872 | tf_op jit(solution)/shard_map/ppermute | solution.py:477
  54.4 64.2 %copy-start.24 = (bf16[80,240]{1,0:T(8,128)(2,1)S(1)}, bf16[80,240]{1,0:T(8,128)(2,1)}, u32[]{:S(2)}) copy-start(bf16[80,240]{1,0:T(8,128)(2,1)} %constant.101.clone.refs_5_.refs_2_.refs_3_) | copy-start | bytes 115204
  145.5 43.4 %all-to-all-start.2 = ((s16[32,208,128]{2,1,0:T(8,128)(2,1)}), s16[32,208,128]{2,1,0:T(8,128)(2,1)S(1)}, u32[]{:S(2)}, u32[]{:S(2)}) async-start(s16[32,208,128]{2,1,0:T(8,128)(2,1)} %get-tuple-element.34), calls=%async_computation.2 | async-start | bytes 3407872 | tf_op jit(solution)/shard_map/all_to_all | solution.py:461
  188.9 64.1 %all-to-all-start.3 = ((s16[32,208,128]{2,1,0:T(8,128)(2,1)}), s16[32,208,128]{2,1,0:T(8,128)(2,1)S(1)}, u32[]{:S(2)}, u32[]{:S(2)}) async-start(s16[32,208,128]{2,1,0:T(8,128)(2,1)} %get-tuple-element.37), calls=%async_computation.3 | async-start | bytes 3407872 | tf_op jit(solution)/shard_map/all_to_all | solution.py:461
  253.0 45.9 %all-to-all-start.4 = ((s16[32,208,128]{2,1,0:T(8,128)(2,1)}), s16[32,208,128]{2,1,0:T(8,128)(2,1)S(1)}, u32[]{:S(2)}, u32[]{:S(2)}) async-start(s16[32,208,128]{2,1,0:T(8,128)(2,1)} %copy-done.13), calls=%async_computation.4 | async-start | bytes 3407872 | tf_op jit(solution)/shard_map/all_to_all | solution.py:461
  298.9 43.3 %all-to-all-start.5 = ((s16[32,208,128]{2,1,0:T(8,128)(2,1)}), s16[32,208,128]{2,1,0:T(8,128)(2,1)}, u32[]{:S(2)}, u32[]{:S(2)}) async-start(s16[32,208,128]{2,1,0:T(8,128)(2,1)} %pad_add_fusion), calls=%async_computation.5 | async-start | bytes 3407872 | tf_op jit(solution)/shard_map/all_to_all | solution.py:461
  322.0 23.6 %copy-start.2 = (bf16[2,2048,256]{2,1,0:T(8,128)(2,1)S(1)}, bf16[2,2048,256]{2,1,0:T(8,128)(2,1)}, u32[]{:S(2)}) copy-start(bf16[2,2048,256]{2,1,0:T(8,128)(2,1)} %all-gather.3.cloned.1.call-done.refs_5_) | copy-start | bytes 6291460
  342.2 43.4 %all-to-all-start.6 = ((s16[32,208,128]{2,1,0:T(8,128)(2,1)}), s16[32,208,128]{2,1,0:T(8,128)(2,1)}, u32[]{:S(2)}, u32[]{:S(2)}) async-start(s16[32,208,128]{2,1,0:T(8,128)(2,1)} %copy-done.11), calls=%async_computation.6 | async-start | bytes 3407872 | tf_op jit(solution)/shard_map/all_to_all | solution.py:461
  354.5 47.5 %copy-start.30 = (bf16[2048,256]{1,0:T(8,128)(2,1)}, bf16[2048,256]{1,0:T(8,128)(2,1)S(1)}, u32[]{:S(2)}) copy-start(bf16[2048,256]{1,0:T(8,128)(2,1)S(1)} %get-tuple-element.27.row_high.refs_4_) | copy-start | bytes 3145732
  385.7 43.4 %all-to-all-start.7 = ((s16[32,208,128]{2,1,0:T(8,128)(2,1)}), s16[32,208,128]{2,1,0:T(8,128)(2,1)}, u32[]{:S(2)}, u32[]{:S(2)}) async-start(s16[32,208,128]{2,1,0:T(8,128)(2,1)} %get-tuple-element.42), calls=%async_computation.7 | async-start | bytes 3407872 | tf_op jit(solution)/shard_map/all_to_all | solution.py:461
  391.5 9.2 %copy-start.3 = (bf16[4096,256]{1,0:T(8,128)(2,1)}, bf16[4096,256]{1,0:T(8,128)(2,1)S(1)}, u32[]{:S(2)}) copy-start(bf16[4096,256]{1,0:T(8,128)(2,1)S(1)} %get-tuple-element.47.left_b.col_b) | copy-start | bytes 6291460
  391.5 9.2 %copy-start.4 = (bf16[4096,256]{1,0:T(8,128)(2,1)}, bf16[4096,256]{1,0:T(8,128)(2,1)S(1)}, u32[]{:S(2)}) copy-start(bf16[4096,256]{1,0:T(8,128)(2,1)S(1)} %get-tuple-element.48.left_a.col_a) | copy-start | bytes 6291460
  391.5 10.5 %copy-start.28 = (bf16[80,240]{1,0:T(8,128)(2,1)S(1)}, bf16[80,240]{1,0:T(8,128)(2,1)}, u32[]{:S(2)}) copy-start(bf16[80,240]{1,0:T(8,128)(2,1)} %constant.101.clone.refs_5_.refs_2_.refs_3_) | copy-start | bytes 115204
  429.0 43.3 %all-to-all-start.8 = ((s16[32,208,128]{2,1,0:T(8,128)(2,1)}), s16[32,208,128]{2,1,0:T(8,128)(2,1)S(1)}, u32[]{:S(2)}, u32[]{:S(2)}) async-start(s16[32,208,128]{2,1,0:T(8,128)(2,1)} %middle.6), calls=%async_computation.8 | async-start | bytes 3407872 | tf_op jit(solution)/shard_map/all_to_all | solution.py:461
  472.4 61.9 %all-to-all-start.9 = ((s16[32,208,128]{2,1,0:T(8,128)(2,1)}), s16[32,208,128]{2,1,0:T(8,128)(2,1)S(1)}, u32[]{:S(2)}, u32[]{:S(2)}) async-start(s16[32,208,128]{2,1,0:T(8,128)(2,1)} %get-tuple-element.44.refs_4_), calls=%async_computation.9 | async-start | bytes 3407872 | tf_op jit(solution)/shard_map/all_to_all | solution.py:461
  479.2 34.5 %copy-start.29 = (bf16[80,240]{1,0:T(8,128)(2,1)S(1)}, bf16[80,240]{1,0:T(8,128)(2,1)}, u32[]{:S(2)}) copy-start(bf16[80,240]{1,0:T(8,128)(2,1)} %constant.101.clone.refs_5_.refs_2_.refs_3_) | copy-start | bytes 115204
  534.2 46.0 %all-to-all-start.10 = ((s16[32,208,128]{2,1,0:T(8,128)(2,1)}), s16[32,208,128]{2,1,0:T(8,128)(2,1)S(1)}, u32[]{:S(2)}, u32[]{:S(2)}) async-start(s16[32,208,128]{2,1,0:T(8,128)(2,1)} %copy-done.12), calls=%async_computation.10 | async-start | bytes 3407872 | tf_op jit(solution)/shard_map/all_to_all | solution.py:461
  559.2 25.4 %copy-start.6 = (s16[32,208,128]{2,1,0:T(8,128)(2,1)S(1)}, s16[32,208,128]{2,1,0:T(8,128)(2,1)}, u32[]{:S(2)}) copy-start(s16[32,208,128]{2,1,0:T(8,128)(2,1)} %copy-done.5) | copy-start | bytes 5111812
  581.4 43.3 %all-to-all-start.11 = ((s16[32,208,128]{2,1,0:T(8,128)(2,1)}), s16[32,208,128]{2,1,0:T(8,128)(2,1)}, u32[]{:S(2)}, u32[]{:S(2)}) async-start(s16[32,208,128]{2,1,0:T(8,128)(2,1)} %copy-done.14), calls=%async_computation.11 | async-start | bytes 3407872 | tf_op jit(solution)/shard_map/all_to_all | solution.py:461
  584.6 40.1 %copy-start.8 = (s16[32,208,128]{2,1,0:T(8,128)(2,1)S(1)}, s16[32,208,128]{2,1,0:T(8,128)(2,1)}, u32[]{:S(2)}) copy-start(s16[32,208,128]{2,1,0:T(8,128)(2,1)} %copy-done.7) | copy-start | bytes 5111812
  (31 other events, 39.7 us)
Sparse Core Ops, SparseCore 0:
  51.8 72.8 all-gather.2
  126.5 48.2 all-gather.4

commit v3 on v2

--- a/solution.py
+++ b/solution.py
@@ -11,6 +11,7 @@
 
 
 PB = 256
+GROUP = 20
 LANES = 128
 SHIFT = 4.0
 BOX = 2.0
@@ -82,7 +83,7 @@
     )
     columns = [fitting[g * depth : (g + 1) * depth] for g in range(group)]
     for g, out in enumerate(transform(table[...], columns)):
-        grid_rows[pl.ds(step * group + g, depth, stride=cells), :] = out
+        grid_rows[pl.ds(step * group + g, out.shape[0], stride=cells), :] = out
 
     @pl.when(step == pl.num_programs(0) - 1)
     def _():
@@ -99,7 +100,7 @@
 
 
 def source(phi, psi, pivot_a, pivot_b, inverse, half, table, cells, depth, padded, pieces):
-    group = max(g for g in range(1, 11) if cells % g == 0)
+    group = max(g for g in range(1, GROUP + 1) if cells % g == 0)
     orbitals = phi.shape[1]
     pivots = pivot_a.shape[0]
     whole = lambda shape: pl.BlockSpec(shape, lambda i: (0,) * len(shape))
@@ -116,7 +117,7 @@
         ],
         out_specs=[whole((n, padded, LANES)) for n in pieces],
         out_shape=[jax.ShapeDtypeStruct((n, padded, LANES), jnp.int16) for n in pieces],
-        scratch_shapes=[pltpu.VMEM((depth * cells, LANES), jnp.float32)],
+        scratch_shapes=[pltpu.VMEM((table.shape[0] * cells, LANES), jnp.float32)],
         compiler_params=pltpu.CompilerParams(vmem_limit_bytes=50 * MIB),
         cost_estimate=cost(
             cells * depth / 600, 4 * cells * depth * orbitals
@@ -186,20 +187,14 @@
     lax.fori_loop(0, blocks, store, 0)
 
 
-def middle(z_freq, piece, x_table, y_table, grid_x, grid_y, lines, after):
+def middle(z_freq, piece, x_table, y_table, grid_x, grid_y, lines):
     blocks, padded, _ = piece.shape
     sizes = (grid_x, grid_y, lines, blocks)
     vmem = pl.BlockSpec(memory_space=pltpu.VMEM)
     points = grid_x * grid_y
     return pl.pallas_call(
-        lambda *refs: middle_kernel(sizes, padded, *refs[:4], *refs[4 + len(after) :]),
-        in_specs=[
-            pl.BlockSpec(memory_space=pltpu.SMEM),
-            vmem,
-            vmem,
-            vmem,
-            *[pl.BlockSpec(memory_space=pl.ANY) for _ in after],
-        ],
+        lambda *refs: middle_kernel(sizes, padded, *refs),
+        in_specs=[pl.BlockSpec(memory_space=pltpu.SMEM), vmem, vmem, vmem],
         out_specs=vmem,
         out_shape=jax.ShapeDtypeStruct(piece.shape, jnp.int16),
         scratch_shapes=[
@@ -209,7 +204,7 @@
         compiler_params=pltpu.CompilerParams(vmem_limit_bytes=32 * MIB),
         cost_estimate=cost(points / 400, 4 * blocks * padded * LANES),
         name="middle",
-    )(z_freq, piece, x_table, y_table, *after)
+    )(z_freq, piece, x_table, y_table)
 
 
 def target_kernel(group, cells, depth, spans, *refs):
@@ -239,7 +234,7 @@
 
 
 def target(pieces, spans, table, before, half, cells, depth, functions):
-    group = max(g for g in range(1, 11) if cells % g == 0)
+    group = max(g for g in range(1, GROUP + 1) if cells % g == 0)
     whole = lambda shape: pl.BlockSpec(shape, lambda i: (0,) * len(shape))
     in_specs = [whole(p.shape) for p in pieces] + [whole(table.shape)]
     operands = [*pieces, table]
@@ -463,20 +458,19 @@
     held = min(owned, PB)
     piece_rows = 2 * PB // devices
     offered = jnp.concatenate([own[:, :held]] * (PB // held), axis=1)
-    offered = exchange(offered.reshape(devices, piece_rows, orbitals))
-    owner = me * piece_rows % PB // owned
-    piece = lax.dynamic_index_in_dim(offered, owner, axis=0, keepdims=True)
-    pivot = exchange(jnp.broadcast_to(piece, offered.shape)).reshape(2, PB, orbitals)
-
-    own, pivot = lax.optimization_barrier((own, pivot))
     swap = [
         (c * row_count + r, r * col_count + c)
         for r in range(row_count)
         for c in range(col_count)
     ]
     crossed = lax.ppermute(own, axes, swap)
+    offered = exchange(offered.reshape(devices, piece_rows, orbitals))
+    own, crossed, offered = lax.optimization_barrier((own, crossed, offered))
+    owner = me * piece_rows % PB // owned
+    piece = lax.dynamic_index_in_dim(offered, owner, axis=0, keepdims=True)
+    pivot = exchange(jnp.broadcast_to(piece, offered.shape)).reshape(2, PB, orbitals)
+
     row_samples = lax.all_gather(own, "col", axis=1, tiled=True)
-    col_samples = lax.all_gather(crossed, "row", axis=1, tiled=True)
 
     lead_inverse = factor_call(lead_kernel, "lead", half, 10, pivot[0, :half], pivot[1, :half])
     inverse = factor_call(rest_kernel, "rest", PB, 14, pivot[0], pivot[1], lead_inverse)
@@ -493,8 +487,11 @@
         parts.append([(a // devices, a % devices, b - a) for a, b in zip(marks, marks[1:])])
 
     outgoing = [[] for _ in range(rounds)]
-    for h, rows in enumerate((lead_inverse, inverse)):
+
+    def make(h, chosen, rows):
         used = rows.shape[1]
+        first = chosen[0][0] * devices + chosen[0][1] - h * depth
+        count = sum(n for _, _, n in chosen)
         made = source(
             flat_phi,
             flat_psi,
@@ -502,60 +499,82 @@
             pivot[1, :used],
             rows,
             h,
-            z_table,
+            z_table[first : first + count],
             cells,
             depth,
             padded,
-            [n for _, _, n in parts[h]],
+            [n for _, _, n in chosen],
         )
-        for (k, _, _), piece in zip(parts[h], made):
-            outgoing[k].append(piece)
-    spare = rounds * devices - depth * halves
-    if spare:
-        outgoing[-1].append(jnp.zeros((spare, padded, LANES), jnp.int16))
-
+        for (k, _, _), part in zip(chosen, made):
+            outgoing[k].append(part)
+
+    def after(value, gate):
+        return lax.optimization_barrier((value, gate))[0]
+
+    make(0, parts[0][:1], lead_inverse)
+    if parts[0][1:]:
+        make(0, parts[0][1:], after(lead_inverse, row_samples))
     row_start = row_index * row_samples.shape[1]
-    col_start = col_index * col_samples.shape[1]
+    col_start = col_index * row_count * owned
     scalar = lambda *v: jnp.stack([jnp.asarray(a, jnp.int32) for a in v])
-    panel, row_high, row_low = panel_rows(scalar(row_start), row_samples, pivot, inverse)
-    _, col_high, col_low = panel_rows(scalar(col_start), col_samples, pivot, inverse)
-    schur = schur_block(
-        scalar(row_start, col_start),
-        (row_samples[0], row_samples[1], row_high, row_low),
-        (col_samples[0], col_samples[1], col_high, col_low),
-    )
-
-    waits = [[] for _ in range(rounds)]
-    waits[0] += [made[-1], row_samples, col_samples]
-    waits[min(2, rounds - 1)] += [row_high, col_high]
-    waits[min(3, rounds - 1)] += [schur]
-    latest = None
-
-    def in_turn(block):
-        nonlocal latest
-        if latest is not None:
-            block, latest = lax.optimization_barrier((block, latest))
-        latest = exchange(block)
+
+    latest = outgoing[0][0]
+    columns = crossed.reshape(2, 1, owned, orbitals)
+    distances = [1 << b for b in reversed(range(row_count.bit_length() - 1))]
+
+    def double(block):
+        distance = distances.pop(0)
+        pairs = [(r, r ^ distance) for r in range(row_count)]
+        other = lax.ppermute(block, "row", pairs)
+        upper = row_index // distance % 2 == 1
+        halves = [jnp.where(upper, other, block), jnp.where(upper, block, other)]
+        return jnp.stack(halves, axis=2).reshape(2, -1, owned, orbitals)
+
+    def in_turn(block, *ready):
+        nonlocal latest, columns
+        before, latest = latest, lax.optimization_barrier((block, latest, columns, *ready))[0]
+        if distances:
+            columns = double(after(columns, before))
+        latest = exchange(latest)
         return latest
 
+    second_round = parts[1][0][0]
+    panel_round = max(min(2, rounds - 1), second_round)
+    schur_round = max(min(3, rounds - 1), panel_round)
+    ready = []
     arrived, returned = [], []
     for k in range(rounds + 1):
+        if k == second_round:
+            gated = after(inverse, latest if k < 2 else arrived[k - 1])
+            make(1, parts[1], gated)
         if k < rounds:
-            pieces = outgoing[k]
+            pieces = list(outgoing[k])
+            spare = devices - sum(p.shape[0] for p in pieces)
+            if spare:
+                pieces.append(jnp.zeros((spare, padded, LANES), jnp.int16))
             sent = pieces[0] if len(pieces) == 1 else jnp.concatenate(pieces, axis=0)
-            arrived.append(in_turn(sent))
+            arrived.append(in_turn(sent, *ready))
+            ready = []
+        if k == panel_round:
+            while distances:
+                columns = double(columns)
+            col_samples = columns.reshape(2, row_count * owned, orbitals)
+            gated = after(inverse, latest)
+            panel, row_high, row_low = panel_rows(scalar(row_start), row_samples, pivot, gated)
+            _, col_high, col_low = panel_rows(scalar(col_start), col_samples, pivot, gated)
+            ready += [row_high, col_high]
+        if k == schur_round:
+            schur = schur_block(
+                after(scalar(row_start, col_start), latest),
+                (row_samples[0], row_samples[1], row_high, row_low),
+                (col_samples[0], col_samples[1], col_high, col_low),
+            )
+            ready += [schur]
         if k > 0:
             z_index = ((k - 1) * devices + me) % depth
             z_freq = jnp.minimum(z_index, depth - z_index).astype(jnp.int32).reshape(1)
             back = middle(
-                z_freq,
-                arrived[k - 1],
-                x_table,
-                y_table,
-                grid_x,
-                grid_y,
-                line_count,
-                waits[k - 1],
+                z_freq, arrived[k - 1], x_table, y_table, grid_x, grid_y, line_count
             )
             returned.append(in_turn(back))
 

time: 649 us -> 577 us (0.89)
  waiting for transfers between devices: 292 us -> 222 us
  Pallas kernels: 240 us -> 233 us
    ppermute x1, waiting for transfers between devices: 58.3 us -> 0.01 us  [on_device(): crossed = lax.ppermute(own, axes, swap)]
    all_to_all x12, waiting for transfers between devices: 234 us -> 179 us  [on_device(): lax.all_to_all(a, axes, split_axis=0, concat_axis=0, tiled=True)]
    ppermute x0 -> x3, waiting for transfers between devices: none -> 29.5 us  [double(): other = lax.ppermute(block, 'row', pairs)]
    all_gather x1, waiting for transfers between devices: 0.01 us -> 13 us  [on_device(): row_samples = lax.all_gather(own, 'col', axis=1, tiled=True)]
    pallas_call x2, Pallas kernels: 27.2 us -> 20 us  [target(): pl.pallas_call(lambda *refs: target_kernel(group, cells, depth, spans, *r...]
    pallas_call x2 -> x3, Pallas kernels: 59.7 us -> 62.4 us  [source(): pl.pallas_call(lambda *refs: source_kernel(group, cells, depth, padded, p...]
    unnamed x80 -> x94, local copies, waits for them, and re-layouts: 29.6 us -> 26.9 us
  transfers between devices with their start and end apart: 15 -> 17, of which waited for: 11 -> 14; matrix products, arithmetic and copies ran while one was open for 1% -> 2% of each run, Pallas kernels for 35% -> 39%
where the time goes in v3:
time: 577 us; the launch traced here: 574 us
  Pallas kernels  233 us (40%)
  waiting for transfers between devices  222 us (38%)
  starting transfers between devices  53 us (9%)
  local copies, waits for them, and re-layouts  43.8 us (8%)
  between operations  14.7 us (3%)
  other arithmetic  8.25 us (1%)
    all_to_all x12, waiting for transfers between devices, on_device(): lax.all_to_all(a, axes, split_axis=0, concat_axis=0, tiled=True)  179 us
    pallas_call x5, Pallas kernels, middle(): pl.pallas_call(lambda *refs: middle_kernel(sizes, padded, *refs), in_spec...  90.8 us
    pallas_call x3, Pallas kernels, source(): pl.pallas_call(lambda *refs: source_kernel(group, cells, depth, padded, p...  62.4 us
    all_to_all x12, starting transfers between devices, on_device(): lax.all_to_all(a, axes, split_axis=0, concat_axis=0, tiled=True)  46.1 us
    pallas_call x1, Pallas kernels, schur_block(): pl.pallas_call(schur_kernel, grid=(rows // row_tile, cols // col_tile), i...  34.5 us
    ppermute x3, waiting for transfers between devices, double(): other = lax.ppermute(block, 'row', pairs)  29.5 us
    unnamed x94, local copies, waits for them, and re-layouts  26.9 us
    pallas_call x2, Pallas kernels, target(): pl.pallas_call(lambda *refs: target_kernel(group, cells, depth, spans, *r...  20 us
  transfers between devices with their start and end apart: 17, of which 14 were waited for; matrix products, arithmetic and copies ran while one was open for 2% of the time, Pallas kernels for 39%

profile of v3, /device:TPU:1, one launch (start us, length us, event | category | flops | bytes accessed | tf_op | source)
XLA Modules:
  0.0 574.2 jit_solution(2421807274852829398)
XLA Ops:
  30.2 33.4 %all-to-all-done = bf16[32,16,256]{2,1,0:T(8,128)(2,1)S(1)} async-done(((bf16[32,16,256]{2,1,0:T(8,128)(2,1)}), bf16[32,16,256]{2,1,0:T(8,128)(2,1)S(1)}, u32[]{:S(2)}, u32[]{:S(2)}) %all-to-all-start) | async-done | bytes 262176 | tf_op jit(solution)/shard_map/all_to_all | solution.py:456
  71.0 9.6 %all-to-all-done.1 = bf16[32,16,256]{2,1,0:T(8,128)(2,1)S(1)} async-done(((bf16[32,16,256]{2,1,0:T(8,128)(2,1)}), bf16[32,16,256]{2,1,0:T(8,128)(2,1)S(1)}, u32[]{:S(2)}, u32[]{:S(2)}) %all-to-all-start.1) | async-done | bytes 262176 | tf_op jit(solution)/shard_map/all_to_all | solution.py:456
  85.7 16.9 %source.4 = s16[32,208,128]{2,1,0:T(8,128)(2,1)} custom-call(bf16[16000,256]{1,0:T(8,128)(2,1)} %bitcast.69, bf16[16000,256]{1,0:T(8,128)(2,1)} %bitcast.65, bf16[128,256]{1,0:T(8,128)(2,1)S(1)} %get-tuple-element.74.pivot_a.refs_2_, bf16[128,256]{1,0:T(8,128)(2,1)S(1)} %get-tuple-element.73.pivot_b.refs_3_, f32[128,128]{1,0:T(8,128)S(1)} %lead.1.lead_inverse.refs_4_, ...), custom_call_target="tpu_custom_call" | custom-call | flops 30666665984 | bytes 16384000 | tf_op jit(solution)/shard_map/source/pallas_call | solution.py:107
  107.4 14.0 %collective-permute-done.1 = bf16[2,1,512,256]{3,2,0,1:T(8,128)(2,1)} collective-permute-done((bf16[2,1,512,256]{3,2,0,1:T(8,128)(2,1)S(1)}, bf16[2,1,512,256]{3,2,0,1:T(8,128)(2,1)}, u32[]{:S(2)}, u32[]{:S(2)}) %collective-permute-start.1) | collective-permute-done | bytes 524320 | tf_op jit(solution)/shard_map/ppermute | solution.py:528
  123.7 13.0 %all-gather.2.cloned.1.call-done = bf16[2,2048,256]{2,1,0:T(8,128)(2,1)} async-done(((bf16[2,512,256]{2,1,0:T(8,128)(2,1)}), bf16[2,2048,256]{2,1,0:T(8,128)(2,1)}) %all-gather.2.cloned.1.call-update) | async-done | bytes 2097168 | tf_op jit(solution)/shard_map/all_gather | solution.py:473
  136.7 16.6 %source.3 = (s16[32,208,128]{2,1,0:T(8,128)(2,1)S(1)}, s16[16,208,128]{2,1,0:T(8,128)(2,1)S(1)}) custom-call(bf16[16000,256]{1,0:T(8,128)(2,1)} %bitcast.70, bf16[16000,256]{1,0:T(8,128)(2,1)} %bitcast.66, bf16[128,256]{1,0:T(8,128)(2,1)S(1)} %get-tuple-element.74.pivot_a.refs_2_, bf16[128,256]{1,0:T(8,128)(2,1)S(1)} %get-tuple-element.73.pivot_b.refs_3_, ...), custom_call_target="tpu_custom_call" | custom-call | flops 30666665984 | bytes 16384000 | tf_op jit(solution)/shard_map/source/pallas_call | solution.py:107
  169.4 17.9 %middle.6 = s16[32,208,128]{2,1,0:T(8,128)(2,1)S(1)} custom-call(s32[1]{0:T(128)} %bitcast.18.refs_0_, s16[32,208,128]{2,1,0:T(8,128)(2,1)S(1)} %all-to-all-done.2.refs_1_, bf16[80,240]{1,0:T(8,128)(2,1)S(1)} %copy-done.25, bf16[80,240]{1,0:T(8,128)(2,1)S(1)} %copy-done.25), custom_call_target="tpu_custom_call" | custom-call | flops 18400000000 | bytes 3407872 | tf_op jit(solution)/shard_map/middle/pallas_call | solution.py:195
  187.3 15.5 %collective-permute-done.2 = bf16[2,2,512,256]{3,2,0,1:T(8,128)(2,1)S(1)} collective-permute-done((bf16[2,2,512,256]{3,2,0,1:T(8,128)(2,1)S(1)}, bf16[2,2,512,256]{3,2,0,1:T(8,128)(2,1)S(1)}, u32[]{:S(2)}, u32[]{:S(2)}) %collective-permute-start.2) | collective-permute-done | bytes 1048608 | tf_op jit(solution)/shard_map/ppermute | solution.py:528
  211.3 28.9 %source.5 = (s16[16,208,128]{2,1,0:T(8,128)(2,1)S(1)}, s16[32,208,128]{2,1,0:T(8,128)(2,1)}, s16[32,208,128]{2,1,0:T(8,128)(2,1)}) custom-call(bf16[16000,256]{1,0:T(8,128)(2,1)} %bitcast.71, bf16[16000,256]{1,0:T(8,128)(2,1)} %bitcast.67, bf16[256,256]{1,0:T(8,128)(2,1)S(1)} %bitcast.54, bf16[256,256]{1,0:T(8,128)(2,1)S(1)} %bitcast.50, ...), custom_call_target="tpu_custom_call" | custom-call | flops 30666665984 | bytes 16384000 | tf_op jit(solution)/shard_map/source/pallas_call | solution.py:107
  244.7 6.3 %all-to-all-done.4.refs_0_ = s16[32,208,128]{2,1,0:T(8,128)(2,1)S(1)} async-done(((s16[32,208,128]{2,1,0:T(8,128)(2,1)}), s16[32,208,128]{2,1,0:T(8,128)(2,1)S(1)}, u32[]{:S(2)}, u32[]{:S(2)}) %all-to-all-start.4) | async-done | bytes 1703968 | tf_op jit(solution)/shard_map/all_to_all | solution.py:456
  256.5 17.9 %middle.5 = s16[32,208,128]{2,1,0:T(8,128)(2,1)S(1)} custom-call(s32[1]{0:T(128)} %bitcast.17.refs_0_, s16[32,208,128]{2,1,0:T(8,128)(2,1)S(1)} %copy-done.7, bf16[80,240]{1,0:T(8,128)(2,1)S(1)} %copy-done.27, bf16[80,240]{1,0:T(8,128)(2,1)S(1)} %copy-done.27), custom_call_target="tpu_custom_call" | custom-call | flops 18400000000 | bytes 3407872 | tf_op jit(solution)/shard_map/middle/pallas_call | solution.py:195
  275.6 18.7 %all-to-all-done.5.refs_1_ = s16[32,208,128]{2,1,0:T(8,128)(2,1)S(1)} async-done(((s16[32,208,128]{2,1,0:T(8,128)(2,1)}), s16[32,208,128]{2,1,0:T(8,128)(2,1)S(1)}, u32[]{:S(2)}, u32[]{:S(2)}) %all-to-all-start.5) | async-done | bytes 1703968 | tf_op jit(solution)/shard_map/all_to_all | solution.py:456
  309.2 9.1 %panel.3 = (f32[4096,256]{1,0:T(8,128)}, bf16[4096,256]{1,0:T(8,128)(2,1)S(1)}, bf16[4096,256]{1,0:T(8,128)(2,1)S(1)}) custom-call(s32[1]{0:T(128)} %bitcast.1.first_row, bf16[4096,256]{1,0:T(8,128)(2,1)S(1)} %bitcast.45, bf16[4096,256]{1,0:T(8,128)(2,1)S(1)} %bitcast.47, bf16[256,256]{1,0:T(8,128)(2,1)S(1)} %bitcast.56, bf16[256,256]{1,0:T(8,128)(2,1)S(1)} %bitcast.52, ...), custom_call_target="tpu_custom_call" | custom-call | flops 11776000000 | bytes 12582912 | tf_op jit(solution)/shard_map/panel/pallas_call | solution.py:281
  320.9 16.7 %all-to-all-done.6.refs_1_ = s16[32,208,128]{2,1,0:T(8,128)(2,1)} async-done(((s16[32,208,128]{2,1,0:T(8,128)(2,1)}), s16[32,208,128]{2,1,0:T(8,128)(2,1)}, u32[]{:S(2)}, u32[]{:S(2)}) %all-to-all-start.6) | async-done | bytes 1703968 | tf_op jit(solution)/shard_map/all_to_all | solution.py:456
  341.0 17.9 %middle.7 = s16[32,208,128]{2,1,0:T(8,128)(2,1)S(1)} custom-call(s32[1]{0:T(128)} %bitcast.29.refs_0_, s16[32,208,128]{2,1,0:T(8,128)(2,1)S(1)} %all-to-all-done.5.refs_1_, bf16[80,240]{1,0:T(8,128)(2,1)S(1)} %copy-done.28, bf16[80,240]{1,0:T(8,128)(2,1)S(1)} %copy-done.28), custom_call_target="tpu_custom_call" | custom-call | flops 18400000000 | bytes 3407872 | tf_op jit(solution)/shard_map/middle/pallas_call | solution.py:195
  360.1 20.9 %all-to-all-done.7.refs_1_ = s16[32,208,128]{2,1,0:T(8,128)(2,1)S(1)} async-done(((s16[32,208,128]{2,1,0:T(8,128)(2,1)}), s16[32,208,128]{2,1,0:T(8,128)(2,1)S(1)}, u32[]{:S(2)}, u32[]{:S(2)}) %all-to-all-start.7) | async-done | bytes 1703968 | tf_op jit(solution)/shard_map/all_to_all | solution.py:456
  387.8 34.5 %schur.1 = f32[2048,4096]{1,0:T(8,128)} custom-call(s32[2]{0:T(128)S(1)} %pad_add_fusion.1.offsets, bf16[2048,256]{1,0:T(8,128)(2,1)S(1)} %copy-done.19, bf16[2048,256]{1,0:T(8,128)(2,1)S(1)} %copy-done.17, bf16[2048,256]{1,0:T(8,128)(2,1)S(1)} %copy-done.32, bf16[2048,256]{1,0:T(8,128)(2,1)} %copy-done.33, bf16[4096,256]{1,0:T(8,128)(2,1)} %bitcast.46, ...), custom_call_target="tpu_custom_call" | custom-call | flops 40195411968 | bytes 33554432 | tf_op jit(solution)/shard_map/schur/pallas_call | solution.py:329
  428.3 17.9 %middle.8 = s16[32,208,128]{2,1,0:T(8,128)(2,1)S(1)} custom-call(s32[1]{0:T(128)} %bitcast.30.refs_0_, s16[32,208,128]{2,1,0:T(8,128)(2,1)S(1)} %all-to-all-done.7.refs_1_, bf16[80,240]{1,0:T(8,128)(2,1)S(1)} %copy-done.28, bf16[80,240]{1,0:T(8,128)(2,1)S(1)} %copy-done.28), custom_call_target="tpu_custom_call" | custom-call | flops 18400000000 | bytes 3407872 | tf_op jit(solution)/shard_map/middle/pallas_call | solution.py:195
  447.4 21.0 %all-to-all-done.9.refs_1_ = s16[32,208,128]{2,1,0:T(8,128)(2,1)} async-done(((s16[32,208,128]{2,1,0:T(8,128)(2,1)}), s16[32,208,128]{2,1,0:T(8,128)(2,1)}, u32[]{:S(2)}, u32[]{:S(2)}) %all-to-all-start.9) | async-done | bytes 1703968 | tf_op jit(solution)/shard_map/all_to_all | solution.py:456
  471.6 19.3 %middle.9 = s16[32,208,128]{2,1,0:T(8,128)(2,1)S(1)} custom-call(s32[1]{0:T(128)} %bitcast.31.refs_0_, s16[32,208,128]{2,1,0:T(8,128)(2,1)} %all-to-all-done.9.refs_1_, bf16[80,240]{1,0:T(8,128)(2,1)S(1)} %copy-done.28, bf16[80,240]{1,0:T(8,128)(2,1)S(1)} %copy-done.28), custom_call_target="tpu_custom_call" | custom-call | flops 18400000000 | bytes 3407872 | tf_op jit(solution)/shard_map/middle/pallas_call | solution.py:195
  492.2 19.5 %all-to-all-done.10.refs_1_ = s16[32,208,128]{2,1,0:T(8,128)(2,1)S(1)} async-done(((s16[32,208,128]{2,1,0:T(8,128)(2,1)}), s16[32,208,128]{2,1,0:T(8,128)(2,1)S(1)}, u32[]{:S(2)}, u32[]{:S(2)}) %all-to-all-start.10) | async-done | bytes 1703968 | tf_op jit(solution)/shard_map/all_to_all | solution.py:456
  516.1 10.3 %target.2.refs_4_ = f32[16000,256]{1,0:T(8,128)} custom-call(s16[32,208,128]{2,1,0:T(8,128)(2,1)S(1)} %copy-done.3, s16[32,208,128]{2,1,0:T(8,128)(2,1)} %all-to-all-done.6.refs_1_, s16[32,208,128]{2,1,0:T(8,128)(2,1)} %copy-done.4, bf16[80,240]{1,0:T(8,128)(2,1)S(1)} %copy-done.28), custom_call_target="tpu_custom_call" | custom-call | flops 15333332992 | bytes 12288000 | tf_op jit(solution)/shard_map/target/pallas_call | solution.py:246
  526.4 29.8 %all-to-all-done.11.refs_2_ = s16[32,208,128]{2,1,0:T(8,128)(2,1)} async-done(((s16[32,208,128]{2,1,0:T(8,128)(2,1)}), s16[32,208,128]{2,1,0:T(8,128)(2,1)}, u32[]{:S(2)}, u32[]{:S(2)}) %all-to-all-start.11) | async-done | bytes 1703968 | tf_op jit(solution)/shard_map/all_to_all | solution.py:456
  557.7 9.6 %target.3 = f32[16000,256]{1,0:T(8,128)} custom-call(s16[32,208,128]{2,1,0:T(8,128)(2,1)S(1)} %copy-done.5, s16[32,208,128]{2,1,0:T(8,128)(2,1)S(1)} %copy-done.10, s16[32,208,128]{2,1,0:T(8,128)(2,1)} %all-to-all-done.11.refs_2_, bf16[80,240]{1,0:T(8,128)(2,1)S(1)} %copy-done.28, f32[16000,256]{1,0:T(8,128)} %target.2.refs_4_), custom_call_target="tpu_custom_call", output_to_operand_aliasing={{}: (4, {})} | custom-call | flops 15333332992 | bytes 12288000 | tf_op jit(solution)/shard_map/target/pallas_call | solution.py:246
  (142 shorter events, 124.3 us)
Async XLA Ops:
  19.9 50.5 %copy-start.45 = (bf16[2,512,256]{2,1,0:T(8,128)(2,1)}, bf16[2,512,256]{2,1,0:T(8,128)(2,1)S(1)}, u32[]{:S(2)}) copy-start(bf16[2,512,256]{2,1,0:T(8,128)(2,1)S(1)} %pad_maximum_fusion.2) | copy-start | bytes 1572868
  19.9 43.7 %collective-permute-start = (bf16[2,512,256]{2,1,0:T(8,128)(2,1)S(1)}, bf16[2,512,256]{2,1,0:T(8,128)(2,1)S(1)}, u32[]{:S(2)}, u32[]{:S(2)}) collective-permute-start(bf16[2,512,256]{2,1,0:T(8,128)(2,1)S(1)} %pad_maximum_fusion.2), channel_id=1, source_target_pairs={{0,0},{8,1},{16,2},{24,3},{1,4},{9,5},{17,6},{25,7},{2,8},{10,9},{... | collective-permute-start | bytes 1572872 | tf_op jit(solution)/shard_map/ppermute | solution.py:466
  25.1 38.4 %all-to-all-start = ((bf16[32,16,256]{2,1,0:T(8,128)(2,1)}), bf16[32,16,256]{2,1,0:T(8,128)(2,1)S(1)}, u32[]{:S(2)}, u32[]{:S(2)}) async-start(bf16[32,16,256]{2,1,0:T(8,128)(2,1)} %bitcast.6), calls=%async_computation | async-start | bytes 524288 | tf_op jit(solution)/shard_map/all_to_all | solution.py:456
  63.5 39.1 %copy-start.46 = (bf16[2,512,256]{2,1,0:T(8,128)(2,1)}, bf16[2,512,256]{2,1,0:T(8,128)(2,1)S(1)}, u32[]{:S(2)}) copy-start(bf16[2,512,256]{2,1,0:T(8,128)(2,1)S(1)} %collective-permute-done) | copy-start | bytes 1572868
  64.3 16.3 %all-to-all-start.1 = ((bf16[32,16,256]{2,1,0:T(8,128)(2,1)}), bf16[32,16,256]{2,1,0:T(8,128)(2,1)S(1)}, u32[]{:S(2)}, u32[]{:S(2)}) async-start(bf16[32,16,256]{2,1,0:T(8,128)(2,1)} %broadcast_in_dim.14), calls=%async_computation.1 | async-start | bytes 524288 | tf_op jit(solution)/shard_map/all_to_all | solution.py:456
  70.3 66.4 %all-gather.2.cloned.1.call-start = ((), (), s32[]{:S(2)}) async-start(), calls=%async_computation.12 | async-start | bytes 2621440 | tf_op jit(solution)/shard_map/all_gather | solution.py:473
  85.7 51.0 %copy-start.39 = (f32[128,128]{1,0:T(8,128)}, f32[128,128]{1,0:T(8,128)S(1)}, u32[]{:S(2)}) copy-start(f32[128,128]{1,0:T(8,128)S(1)} %lead.1.lead_inverse.refs_4_) | copy-start | bytes 196612
  102.7 18.7 %collective-permute-start.1 = (bf16[2,1,512,256]{3,2,0,1:T(8,128)(2,1)S(1)}, bf16[2,1,512,256]{3,2,0,1:T(8,128)(2,1)}, u32[]{:S(2)}, u32[]{:S(2)}) collective-permute-start(bf16[2,1,512,256]{3,2,0,1:T(8,128)(2,1)S(1)} %bitcast.72), channel_id=1, source_target_pairs={{0,16},{4,20},{8,24},{12,28},{16,0},{20,4},{24,8},{28,12},{1,17},{... | collective-permute-start | bytes 1572872 | tf_op jit(solution)/shard_map/ppermute | solution.py:528
  103.3 52.9 %all-to-all-start.2 = ((s16[32,208,128]{2,1,0:T(8,128)(2,1)}), s16[32,208,128]{2,1,0:T(8,128)(2,1)S(1)}, u32[]{:S(2)}, u32[]{:S(2)}) async-start(s16[32,208,128]{2,1,0:T(8,128)(2,1)} %source.4), calls=%async_computation.2 | async-start | bytes 3407872 | tf_op jit(solution)/shard_map/all_to_all | solution.py:456
  107.4 29.3 %copy-start.29 = (bf16[48,240]{1,0:T(8,128)(2,1)S(1)}, bf16[48,240]{1,0:T(8,128)(2,1)}, u32[]{:S(2)}) copy-start(bf16[48,240]{1,0:T(8,128)(2,1)} %constant.148.refs_5_) | copy-start | bytes 69124
  156.2 48.4 %all-to-all-start.3 = ((s16[32,208,128]{2,1,0:T(8,128)(2,1)}), s16[32,208,128]{2,1,0:T(8,128)(2,1)S(1)}, u32[]{:S(2)}, u32[]{:S(2)}) async-start(s16[32,208,128]{2,1,0:T(8,128)(2,1)} %copy-done.12), calls=%async_computation.3 | async-start | bytes 3407872 | tf_op jit(solution)/shard_map/all_to_all | solution.py:456
  168.0 34.8 %collective-permute-start.2 = (bf16[2,2,512,256]{3,2,0,1:T(8,128)(2,1)S(1)}, bf16[2,2,512,256]{3,2,0,1:T(8,128)(2,1)S(1)}, u32[]{:S(2)}, u32[]{:S(2)}) collective-permute-start(bf16[2,2,512,256]{3,2,0,1:T(8,128)(2,1)S(1)} %copy-done.44), channel_id=1, source_target_pairs={{0,8},{4,12},{8,0},{12,4},{16,24},{20,28},{24,16},{28,20},{1,9},{5... | collective-permute-start | bytes 3145736 | tf_op jit(solution)/shard_map/ppermute | solution.py:528
  205.8 45.3 %all-to-all-start.4 = ((s16[32,208,128]{2,1,0:T(8,128)(2,1)}), s16[32,208,128]{2,1,0:T(8,128)(2,1)S(1)}, u32[]{:S(2)}, u32[]{:S(2)}) async-start(s16[32,208,128]{2,1,0:T(8,128)(2,1)} %copy-done.8), calls=%async_computation.4 | async-start | bytes 3407872 | tf_op jit(solution)/shard_map/all_to_all | solution.py:456
  211.0 29.3 %copy-start.21 = (s16[16,208,128]{2,1,0:T(8,128)(2,1)S(1)}, s16[16,208,128]{2,1,0:T(8,128)(2,1)}, u32[]{:S(2)}) copy-start(s16[16,208,128]{2,1,0:T(8,128)(2,1)} %copy-done.20) | copy-start | bytes 2555908
  211.0 30.6 %collective-permute-start.3 = (bf16[2,4,512,256]{3,2,1,0:T(8,128)(2,1)}, bf16[2,4,512,256]{3,2,1,0:T(8,128)(2,1)S(1)}, u32[]{:S(2)}, u32[]{:S(2)}) collective-permute-start(bf16[2,4,512,256]{3,2,1,0:T(8,128)(2,1)} %bitcast.57), channel_id=1, source_target_pairs={{0,4},{4,0},{8,12},{12,8},{16,20},{20,16},{24,28},{28,24},{1,5},{5... | collective-permute-start | bytes 6291464 | tf_op jit(solution)/shard_map/ppermute | solution.py:528
  251.1 43.2 %all-to-all-start.5 = ((s16[32,208,128]{2,1,0:T(8,128)(2,1)}), s16[32,208,128]{2,1,0:T(8,128)(2,1)S(1)}, u32[]{:S(2)}, u32[]{:S(2)}) async-start(s16[32,208,128]{2,1,0:T(8,128)(2,1)} %pad_add_fusion), calls=%async_computation.5 | async-start | bytes 3407872 | tf_op jit(solution)/shard_map/all_to_all | solution.py:456
  294.3 43.3 %all-to-all-start.6 = ((s16[32,208,128]{2,1,0:T(8,128)(2,1)}), s16[32,208,128]{2,1,0:T(8,128)(2,1)}, u32[]{:S(2)}, u32[]{:S(2)}) async-start(s16[32,208,128]{2,1,0:T(8,128)(2,1)} %copy-done.11), calls=%async_computation.6 | async-start | bytes 3407872 | tf_op jit(solution)/shard_map/all_to_all | solution.py:456
  337.6 43.3 %all-to-all-start.7 = ((s16[32,208,128]{2,1,0:T(8,128)(2,1)}), s16[32,208,128]{2,1,0:T(8,128)(2,1)S(1)}, u32[]{:S(2)}, u32[]{:S(2)}) async-start(s16[32,208,128]{2,1,0:T(8,128)(2,1)} %get-tuple-element.53), calls=%async_computation.7 | async-start | bytes 3407872 | tf_op jit(solution)/shard_map/all_to_all | solution.py:456
  381.0 43.2 %all-to-all-start.8 = ((s16[32,208,128]{2,1,0:T(8,128)(2,1)}), s16[32,208,128]{2,1,0:T(8,128)(2,1)S(1)}, u32[]{:S(2)}, u32[]{:S(2)}) async-start(s16[32,208,128]{2,1,0:T(8,128)(2,1)} %copy-done.14), calls=%async_computation.8 | async-start | bytes 3407872 | tf_op jit(solution)/shard_map/all_to_all | solution.py:456
  424.2 44.2 %all-to-all-start.9 = ((s16[32,208,128]{2,1,0:T(8,128)(2,1)}), s16[32,208,128]{2,1,0:T(8,128)(2,1)}, u32[]{:S(2)}, u32[]{:S(2)}) async-start(s16[32,208,128]{2,1,0:T(8,128)(2,1)} %get-tuple-element.60), calls=%async_computation.9 | async-start | bytes 3407872 | tf_op jit(solution)/shard_map/all_to_all | solution.py:456
  468.4 43.2 %all-to-all-start.10 = ((s16[32,208,128]{2,1,0:T(8,128)(2,1)}), s16[32,208,128]{2,1,0:T(8,128)(2,1)S(1)}, u32[]{:S(2)}, u32[]{:S(2)}) async-start(s16[32,208,128]{2,1,0:T(8,128)(2,1)} %copy-done.13), calls=%async_computation.10 | async-start | bytes 3407872 | tf_op jit(solution)/shard_map/all_to_all | solution.py:456
  492.2 23.9 %copy-start.3 = (s16[32,208,128]{2,1,0:T(8,128)(2,1)S(1)}, s16[32,208,128]{2,1,0:T(8,128)(2,1)}, u32[]{:S(2)}) copy-start(s16[32,208,128]{2,1,0:T(8,128)(2,1)} %copy-done.2) | copy-start | bytes 5111812
  512.9 43.3 %all-to-all-start.11 = ((s16[32,208,128]{2,1,0:T(8,128)(2,1)}), s16[32,208,128]{2,1,0:T(8,128)(2,1)}, u32[]{:S(2)}, u32[]{:S(2)}) async-start(s16[32,208,128]{2,1,0:T(8,128)(2,1)} %copy-done.15), calls=%async_computation.11 | async-start | bytes 3407872 | tf_op jit(solution)/shard_map/all_to_all | solution.py:456
  516.1 40.1 %copy-start.5 = (s16[32,208,128]{2,1,0:T(8,128)(2,1)S(1)}, s16[32,208,128]{2,1,0:T(8,128)(2,1)}, u32[]{:S(2)}) copy-start(s16[32,208,128]{2,1,0:T(8,128)(2,1)} %copy-done.4) | copy-start | bytes 5111812
  (40 other events, 173.4 us)
Sparse Core Ops, SparseCore 0:
  73.3 63.3 all-gather.1

commit v4 on v3

--- a/solution.py
+++ b/solution.py
@@ -11,7 +11,7 @@
 
 
 PB = 256
-GROUP = 20
+GROUP = 40
 LANES = 128
 SHIFT = 4.0
 BOX = 2.0
@@ -458,14 +458,8 @@
     held = min(owned, PB)
     piece_rows = 2 * PB // devices
     offered = jnp.concatenate([own[:, :held]] * (PB // held), axis=1)
-    swap = [
-        (c * row_count + r, r * col_count + c)
-        for r in range(row_count)
-        for c in range(col_count)
-    ]
-    crossed = lax.ppermute(own, axes, swap)
     offered = exchange(offered.reshape(devices, piece_rows, orbitals))
-    own, crossed, offered = lax.optimization_barrier((own, crossed, offered))
+    own, offered = lax.optimization_barrier((own, offered))
     owner = me * piece_rows % PB // owned
     piece = lax.dynamic_index_in_dim(offered, owner, axis=0, keepdims=True)
     pivot = exchange(jnp.broadcast_to(piece, offered.shape)).reshape(2, PB, orbitals)
@@ -519,22 +513,42 @@
     scalar = lambda *v: jnp.stack([jnp.asarray(a, jnp.int32) for a in v])
 
     latest = outgoing[0][0]
-    columns = crossed.reshape(2, 1, owned, orbitals)
-    distances = [1 << b for b in reversed(range(row_count.bit_length() - 1))]
-
-    def double(block):
-        distance = distances.pop(0)
+    members = row_count // col_count
+    bits = [1 << b for b in range(row_count.bit_length() - 1)]
+    inner = [b for b in bits if b < members]
+    outer = [b for b in bits if b >= members]
+    columns = jnp.where(row_index // members == col_index, row_samples, 0)
+    steps = []
+    for t in range(len(outer)):
+        pairs = []
+        for c in range(col_count):
+            for j in range(members):
+                order = outer[j % len(outer) :] + outer[: j % len(outer)]
+                holders = [members * c + j]
+                for b in order[:t]:
+                    holders += [r ^ b for r in holders]
+                pairs += [
+                    (r * col_count + c, (r ^ order[t]) * col_count + c) for r in holders
+                ]
+        steps.append(lambda block, pairs=pairs: block + lax.ppermute(block, axes, pairs))
+
+    def double(block, distance):
         pairs = [(r, r ^ distance) for r in range(row_count)]
         other = lax.ppermute(block, "row", pairs)
         upper = row_index // distance % 2 == 1
-        halves = [jnp.where(upper, other, block), jnp.where(upper, block, other)]
-        return jnp.stack(halves, axis=2).reshape(2, -1, owned, orbitals)
+        return jnp.concatenate(
+            [jnp.where(upper, other, block), jnp.where(upper, block, other)], axis=1
+        )
+
+    steps += [lambda block, distance=d: double(block, distance) for d in inner]
+
+    arrived = []
 
     def in_turn(block, *ready):
         nonlocal latest, columns
         before, latest = latest, lax.optimization_barrier((block, latest, columns, *ready))[0]
-        if distances:
-            columns = double(after(columns, before))
+        if steps and arrived:
+            columns = steps.pop(0)(after(columns, before))
         latest = exchange(latest)
         return latest
 
@@ -542,7 +556,7 @@
     panel_round = max(min(2, rounds - 1), second_round)
     schur_round = max(min(3, rounds - 1), panel_round)
     ready = []
-    arrived, returned = [], []
+    returned = []
     for k in range(rounds + 1):
         if k == second_round:
             gated = after(inverse, latest if k < 2 else arrived[k - 1])
@@ -554,11 +568,11 @@
                 pieces.append(jnp.zeros((spare, padded, LANES), jnp.int16))
             sent = pieces[0] if len(pieces) == 1 else jnp.concatenate(pieces, axis=0)
             arrived.append(in_turn(sent, *ready))
-            ready = []
+            ready = [inverse] if k == 0 else []
         if k == panel_round:
-            while distances:
-                columns = double(columns)
-            col_samples = columns.reshape(2, row_count * owned, orbitals)
+            while steps:
+                columns = steps.pop(0)(columns)
+            col_samples = columns
             gated = after(inverse, latest)
             panel, row_high, row_low = panel_rows(scalar(row_start), row_samples, pivot, gated)
             _, col_high, col_low = panel_rows(scalar(col_start), col_samples, pivot, gated)

time: 577 us -> 567 us (0.983)
  waiting for transfers between devices: 222 us -> 211 us
  other arithmetic: 8.25 us -> 16.7 us
  local copies, waits for them, and re-layouts: 43.8 us -> 36.5 us
  Pallas kernels: 233 us -> 227 us
    ppermute x3 -> x1, waiting for transfers between devices: 29.5 us -> 0.01 us  [double(): other = lax.ppermute(block, 'row', pairs)]
    ppermute x1 -> x2, waiting for transfers between devices: 0.01 us -> 28.9 us  [on_device(): lax.ppermute(block, axes, pairs)]
    all_to_all x12, waiting for transfers between devices: 179 us -> 162 us  [on_device(): lax.all_to_all(a, axes, split_axis=0, concat_axis=0, tiled=True)]
    select_n x0 -> x2, other arithmetic: none -> 6.92 us  [the longest x1 3.87 us: double(): jnp.where(upper, other, block)]
    all_gather x1, waiting for transfers between devices: 13 us -> 19.7 us  [on_device(): row_samples = lax.all_gather(own, 'col', axis=1, tiled=True)]
    unnamed x94 -> x84, local copies, waits for them, and re-layouts: 26.9 us -> 22 us
  transfers between devices with their start and end apart: 17 -> 16, of which waited for: 14 -> 13; matrix products, arithmetic and copies ran while one was open for 2% -> 3% of each run, Pallas kernels for 39% -> 39%
where the time goes in v4:
time: 567 us; the launch traced here: 564 us
  Pallas kernels  227 us (40%)
  waiting for transfers between devices  211 us (37%)
  starting transfers between devices  58.5 us (10%)
  local copies, waits for them, and re-layouts  36.5 us (6%)
  other arithmetic  16.7 us (3%)
  between operations  14.6 us (3%)
    all_to_all x12, waiting for transfers between devices, on_device(): lax.all_to_all(a, axes, split_axis=0, concat_axis=0, tiled=True)  162 us
    pallas_call x5, Pallas kernels, middle(): pl.pallas_call(lambda *refs: middle_kernel(sizes, padded, *refs), in_spec...  92 us
    pallas_call x3, Pallas kernels, source(): pl.pallas_call(lambda *refs: source_kernel(group, cells, depth, padded, p...  57.9 us
    all_to_all x12, starting transfers between devices, on_device(): lax.all_to_all(a, axes, split_axis=0, concat_axis=0, tiled=True)  49.8 us
    pallas_call x1, Pallas kernels, schur_block(): pl.pallas_call(schur_kernel, grid=(rows // row_tile, cols // col_tile), i...  34.5 us
    ppermute x2, waiting for transfers between devices, on_device(): lax.ppermute(block, axes, pairs)  28.9 us
    unnamed x84, local copies, waits for them, and re-layouts  22 us
    all_gather x1, waiting for transfers between devices, on_device(): row_samples = lax.all_gather(own, 'col', axis=1, tiled=True)  19.7 us
  transfers between devices with their start and end apart: 16, of which 13 were waited for; matrix products, arithmetic and copies ran while one was open for 3% of the time, Pallas kernels for 39%

profile of v4, /device:TPU:1, one launch (start us, length us, event | category | flops | bytes accessed | tf_op | source)
XLA Modules:
  0.0 564.4 jit_solution(16587523555679821397)
XLA Ops:
  28.5 9.5 %all-to-all-done = bf16[32,16,256]{2,1,0:T(8,128)(2,1)S(1)} async-done(((bf16[32,16,256]{2,1,0:T(8,128)(2,1)}), bf16[32,16,256]{2,1,0:T(8,128)(2,1)S(1)}, u32[]{:S(2)}, u32[]{:S(2)}) %all-to-all-start) | async-done | bytes 262176 | tf_op jit(solution)/shard_map/all_to_all | solution.py:456
  42.0 9.6 %all-to-all-done.1 = bf16[32,16,256]{2,1,0:T(8,128)(2,1)S(1)} async-done(((bf16[32,16,256]{2,1,0:T(8,128)(2,1)}), bf16[32,16,256]{2,1,0:T(8,128)(2,1)S(1)}, u32[]{:S(2)}, u32[]{:S(2)}) %all-to-all-start.1) | async-done | bytes 262176 | tf_op jit(solution)/shard_map/all_to_all | solution.py:456
  56.7 14.8 %source.4 = s16[32,208,128]{2,1,0:T(8,128)(2,1)} custom-call(bf16[16000,256]{1,0:T(8,128)(2,1)} %bitcast.48, bf16[16000,256]{1,0:T(8,128)(2,1)} %bitcast.44, bf16[128,256]{1,0:T(8,128)(2,1)S(1)} %get-tuple-element.68.pivot_a.refs_2_, bf16[128,256]{1,0:T(8,128)(2,1)S(1)} %get-tuple-element.67.pivot_b.refs_3_, f32[128,128]{1,0:T(8,128)S(1)} %lead.1.lead_inverse.refs_4_, ...), custom_call_target="tpu_custom_call" | custom-call | flops 30666665984 | bytes 16384000 | tf_op jit(solution)/shard_map/source/pallas_call | solution.py:107
  71.6 19.7 %all-gather.2.cloned.1.call-done = bf16[2,2048,256]{2,1,0:T(8,128)(2,1)} async-done(((bf16[2,512,256]{2,1,0:T(8,128)(2,1)}), bf16[2,2048,256]{2,1,0:T(8,128)(2,1)}) %all-gather.2.cloned.1.call-update) | async-done | bytes 2097168 | tf_op jit(solution)/shard_map/all_gather | solution.py:467
  104.4 16.0 %source.3 = (s16[32,208,128]{2,1,0:T(8,128)(2,1)}, s16[16,208,128]{2,1,0:T(8,128)(2,1)S(1)}) custom-call(bf16[16000,256]{1,0:T(8,128)(2,1)} %bitcast.49, bf16[16000,256]{1,0:T(8,128)(2,1)} %bitcast.45, bf16[128,256]{1,0:T(8,128)(2,1)S(1)} %get-tuple-element.68.pivot_a.refs_2_, bf16[128,256]{1,0:T(8,128)(2,1)S(1)} %get-tuple-element.67.pivot_b.refs_3_, ...), custom_call_target="tpu_custom_call" | custom-call | flops 30666665984 | bytes 16384000 | tf_op jit(solution)/shard_map/source/pallas_call | solution.py:107
  121.3 16.5 %all-to-all-done.2.refs_1_ = s16[32,208,128]{2,1,0:T(8,128)(2,1)S(1)} async-done(((s16[32,208,128]{2,1,0:T(8,128)(2,1)}), s16[32,208,128]{2,1,0:T(8,128)(2,1)S(1)}, u32[]{:S(2)}, u32[]{:S(2)}) %all-to-all-start.2) | async-done | bytes 1703968 | tf_op jit(solution)/shard_map/all_to_all | solution.py:456
  146.3 17.9 %middle.6 = s16[32,208,128]{2,1,0:T(8,128)(2,1)S(1)} custom-call(s32[1]{0:T(128)} %bitcast.14.refs_0_, s16[32,208,128]{2,1,0:T(8,128)(2,1)S(1)} %all-to-all-done.2.refs_1_, bf16[80,240]{1,0:T(8,128)(2,1)S(1)} %copy-done.23, bf16[80,240]{1,0:T(8,128)(2,1)S(1)} %copy-done.23), custom_call_target="tpu_custom_call" | custom-call | flops 18400000000 | bytes 3407872 | tf_op jit(solution)/shard_map/middle/pallas_call | solution.py:195
  164.2 18.1 %collective-permute-done = bf16[2,2048,256]{2,1,0:T(8,128)(2,1)} collective-permute-done((bf16[2,2048,256]{2,1,0:T(8,128)(2,1)}, bf16[2,2048,256]{2,1,0:T(8,128)(2,1)}, u32[]{:S(2)}, u32[]{:S(2)}) %collective-permute-start) | collective-permute-done | bytes 2097184 | tf_op jit(solution)/shard_map/ppermute | solution.py:533
  197.6 27.1 %source.5 = (s16[16,208,128]{2,1,0:T(8,128)(2,1)S(1)}, s16[32,208,128]{2,1,0:T(8,128)(2,1)}, s16[32,208,128]{2,1,0:T(8,128)(2,1)}) custom-call(bf16[16000,256]{1,0:T(8,128)(2,1)} %bitcast.50, bf16[16000,256]{1,0:T(8,128)(2,1)} %bitcast.46, bf16[256,256]{1,0:T(8,128)(2,1)S(1)} %bitcast.35, bf16[256,256]{1,0:T(8,128)(2,1)S(1)} %bitcast.31, ...), custom_call_target="tpu_custom_call" | custom-call | flops 30666665984 | bytes 16384000 | tf_op jit(solution)/shard_map/source/pallas_call | solution.py:107
  224.7 10.7 %collective-permute-done.1 = bf16[2,2048,256]{2,1,0:T(8,128)(2,1)S(1)} collective-permute-done((bf16[2,2048,256]{2,1,0:T(8,128)(2,1)}, bf16[2,2048,256]{2,1,0:T(8,128)(2,1)S(1)}, u32[]{:S(2)}, u32[]{:S(2)}) %collective-permute-start.1) | collective-permute-done | bytes 2097184 | tf_op jit(solution)/shard_map/ppermute | solution.py:533
  248.1 19.1 %middle.5 = s16[32,208,128]{2,1,0:T(8,128)(2,1)} custom-call(s32[1]{0:T(128)} %bitcast.13.refs_0_, s16[32,208,128]{2,1,0:T(8,128)(2,1)S(1)} %copy-done.5, bf16[80,240]{1,0:T(8,128)(2,1)S(1)} %copy-done.25, bf16[80,240]{1,0:T(8,128)(2,1)S(1)} %copy-done.25), custom_call_target="tpu_custom_call" | custom-call | flops 18400000000 | bytes 3407872 | tf_op jit(solution)/shard_map/middle/pallas_call | solution.py:195
  271.1 14.8 %all-to-all-done.5.refs_1_ = s16[32,208,128]{2,1,0:T(8,128)(2,1)S(1)} async-done(((s16[32,208,128]{2,1,0:T(8,128)(2,1)}), s16[32,208,128]{2,1,0:T(8,128)(2,1)S(1)}, u32[]{:S(2)}, u32[]{:S(2)}) %all-to-all-start.5) | async-done | bytes 1703968 | tf_op jit(solution)/shard_map/all_to_all | solution.py:456
  300.2 9.1 %panel.3 = (f32[4096,256]{1,0:T(8,128)}, bf16[4096,256]{1,0:T(8,128)(2,1)S(1)}, bf16[4096,256]{1,0:T(8,128)(2,1)S(1)}) custom-call(s32[1]{0:T(128)} %bitcast.1.first_row, bf16[4096,256]{1,0:T(8,128)(2,1)S(1)} %get-tuple-element.62.left_a.col_a, bf16[4096,256]{1,0:T(8,128)(2,1)S(1)} %get-tuple-element.61.left_b.col_b, bf16[256,256]{1,0:T(8,128)(2,1)S(1)} %bitcast.37, ...), custom_call_target="tpu_custom_call" | custom-call | flops 11776000000 | bytes 12582912 | tf_op jit(solution)/shard_map/panel/pallas_call | solution.py:281
  311.9 17.3 %all-to-all-done.6.refs_1_ = s16[32,208,128]{2,1,0:T(8,128)(2,1)} async-done(((s16[32,208,128]{2,1,0:T(8,128)(2,1)}), s16[32,208,128]{2,1,0:T(8,128)(2,1)}, u32[]{:S(2)}, u32[]{:S(2)}) %all-to-all-start.6) | async-done | bytes 1703968 | tf_op jit(solution)/shard_map/all_to_all | solution.py:456
  332.6 17.9 %middle.7 = s16[32,208,128]{2,1,0:T(8,128)(2,1)S(1)} custom-call(s32[1]{0:T(128)} %bitcast.19.refs_0_, s16[32,208,128]{2,1,0:T(8,128)(2,1)S(1)} %all-to-all-done.5.refs_1_, bf16[80,240]{1,0:T(8,128)(2,1)S(1)} %copy-done.26, bf16[80,240]{1,0:T(8,128)(2,1)S(1)} %copy-done.26), custom_call_target="tpu_custom_call" | custom-call | flops 18400000000 | bytes 3407872 | tf_op jit(solution)/shard_map/middle/pallas_call | solution.py:195
  351.7 20.9 %all-to-all-done.7.refs_1_ = s16[32,208,128]{2,1,0:T(8,128)(2,1)S(1)} async-done(((s16[32,208,128]{2,1,0:T(8,128)(2,1)}), s16[32,208,128]{2,1,0:T(8,128)(2,1)S(1)}, u32[]{:S(2)}, u32[]{:S(2)}) %all-to-all-start.7) | async-done | bytes 1703968 | tf_op jit(solution)/shard_map/all_to_all | solution.py:456
  379.4 34.5 %schur.1 = f32[2048,4096]{1,0:T(8,128)} custom-call(s32[2]{0:T(128)S(1)} %pad_add_fusion.1.offsets, bf16[2048,256]{1,0:T(8,128)(2,1)S(1)} %copy-done.17, bf16[2048,256]{1,0:T(8,128)(2,1)S(1)} %copy-done.15, bf16[2048,256]{1,0:T(8,128)(2,1)S(1)} %copy-done.30, bf16[2048,256]{1,0:T(8,128)(2,1)} %copy-done.31, bf16[4096,256]{1,0:T(8,128)(2,1)} %copy-done.1, ...), custom_call_target="tpu_custom_call" | custom-call | flops 40195411968 | bytes 33554432 | tf_op jit(solution)/shard_map/schur/pallas_call | solution.py:329
  419.9 17.9 %middle.8 = s16[32,208,128]{2,1,0:T(8,128)(2,1)S(1)} custom-call(s32[1]{0:T(128)} %bitcast.20.refs_0_, s16[32,208,128]{2,1,0:T(8,128)(2,1)S(1)} %all-to-all-done.7.refs_1_, bf16[80,240]{1,0:T(8,128)(2,1)S(1)} %copy-done.26, bf16[80,240]{1,0:T(8,128)(2,1)S(1)} %copy-done.26), custom_call_target="tpu_custom_call" | custom-call | flops 18400000000 | bytes 3407872 | tf_op jit(solution)/shard_map/middle/pallas_call | solution.py:195
  438.9 21.0 %all-to-all-done.9.refs_1_ = s16[32,208,128]{2,1,0:T(8,128)(2,1)} async-done(((s16[32,208,128]{2,1,0:T(8,128)(2,1)}), s16[32,208,128]{2,1,0:T(8,128)(2,1)}, u32[]{:S(2)}, u32[]{:S(2)}) %all-to-all-start.9) | async-done | bytes 1703968 | tf_op jit(solution)/shard_map/all_to_all | solution.py:456
  463.2 19.3 %middle.9 = s16[32,208,128]{2,1,0:T(8,128)(2,1)S(1)} custom-call(s32[1]{0:T(128)} %bitcast.21.refs_0_, s16[32,208,128]{2,1,0:T(8,128)(2,1)} %all-to-all-done.9.refs_1_, bf16[80,240]{1,0:T(8,128)(2,1)S(1)} %copy-done.26, bf16[80,240]{1,0:T(8,128)(2,1)S(1)} %copy-done.26), custom_call_target="tpu_custom_call" | custom-call | flops 18400000000 | bytes 3407872 | tf_op jit(solution)/shard_map/middle/pallas_call | solution.py:195
  483.7 19.5 %all-to-all-done.10.refs_1_ = s16[32,208,128]{2,1,0:T(8,128)(2,1)S(1)} async-done(((s16[32,208,128]{2,1,0:T(8,128)(2,1)}), s16[32,208,128]{2,1,0:T(8,128)(2,1)S(1)}, u32[]{:S(2)}, u32[]{:S(2)}) %all-to-all-start.10) | async-done | bytes 1703968 | tf_op jit(solution)/shard_map/all_to_all | solution.py:456
  507.7 9.0 %target.2.refs_4_ = f32[16000,256]{1,0:T(8,128)} custom-call(s16[32,208,128]{2,1,0:T(8,128)(2,1)S(1)} %copy-done.3, s16[32,208,128]{2,1,0:T(8,128)(2,1)} %all-to-all-done.6.refs_1_, s16[32,208,128]{2,1,0:T(8,128)(2,1)} %copy-done.6, bf16[80,240]{1,0:T(8,128)(2,1)S(1)} %copy-done.26), custom_call_target="tpu_custom_call" | custom-call | flops 15333332992 | bytes 12288000 | tf_op jit(solution)/shard_map/target/pallas_call | solution.py:246
  516.6 31.1 %all-to-all-done.11.refs_2_ = s16[32,208,128]{2,1,0:T(8,128)(2,1)} async-done(((s16[32,208,128]{2,1,0:T(8,128)(2,1)}), s16[32,208,128]{2,1,0:T(8,128)(2,1)}, u32[]{:S(2)}, u32[]{:S(2)}) %all-to-all-start.11) | async-done | bytes 1703968 | tf_op jit(solution)/shard_map/all_to_all | solution.py:456
  549.2 8.3 %target.3 = f32[16000,256]{1,0:T(8,128)} custom-call(s16[32,208,128]{2,1,0:T(8,128)(2,1)S(1)} %copy-done.7, s16[32,208,128]{2,1,0:T(8,128)(2,1)S(1)} %copy-done.9, s16[32,208,128]{2,1,0:T(8,128)(2,1)} %all-to-all-done.11.refs_2_, bf16[80,240]{1,0:T(8,128)(2,1)S(1)} %copy-done.26, f32[16000,256]{1,0:T(8,128)} %target.2.refs_4_), custom_call_target="tpu_custom_call", output_to_operand_aliasing={{}: (4, {})} | custom-call | flops 15333332992 | bytes 12288000 | tf_op jit(solution)/shard_map/target/pallas_call | solution.py:246
  (126 shorter events, 130.2 us)
Async XLA Ops:
  20.5 17.4 %all-to-all-start = ((bf16[32,16,256]{2,1,0:T(8,128)(2,1)}), bf16[32,16,256]{2,1,0:T(8,128)(2,1)S(1)}, u32[]{:S(2)}, u32[]{:S(2)}) async-start(bf16[32,16,256]{2,1,0:T(8,128)(2,1)} %bitcast.6), calls=%async_computation | async-start | bytes 524288 | tf_op jit(solution)/shard_map/all_to_all | solution.py:456
  38.7 12.9 %all-to-all-start.1 = ((bf16[32,16,256]{2,1,0:T(8,128)(2,1)}), bf16[32,16,256]{2,1,0:T(8,128)(2,1)S(1)}, u32[]{:S(2)}, u32[]{:S(2)}) async-start(bf16[32,16,256]{2,1,0:T(8,128)(2,1)} %broadcast_in_dim.18), calls=%async_computation.1 | async-start | bytes 524288 | tf_op jit(solution)/shard_map/all_to_all | solution.py:456
  41.3 50.0 %all-gather.2.cloned.1.call-start = ((), (), s32[]{:S(2)}) async-start(), calls=%async_computation.12 | async-start | bytes 2621440 | tf_op jit(solution)/shard_map/all_gather | solution.py:467
  56.7 40.9 %copy-start.20 = (bf16[16,16,256]{2,1,0:T(8,128)(2,1)}, bf16[16,16,256]{2,1,0:T(8,128)(2,1)S(1)}, u32[]{:S(2)}) copy-start(bf16[16,16,256]{2,1,0:T(8,128)(2,1)S(1)} %get-tuple-element.70) | copy-start | bytes 393220
  94.3 43.4 %all-to-all-start.2 = ((s16[32,208,128]{2,1,0:T(8,128)(2,1)}), s16[32,208,128]{2,1,0:T(8,128)(2,1)S(1)}, u32[]{:S(2)}, u32[]{:S(2)}) async-start(s16[32,208,128]{2,1,0:T(8,128)(2,1)} %source.4), calls=%async_computation.2 | async-start | bytes 3407872 | tf_op jit(solution)/shard_map/all_to_all | solution.py:456
  137.7 48.1 %all-to-all-start.3 = ((s16[32,208,128]{2,1,0:T(8,128)(2,1)}), s16[32,208,128]{2,1,0:T(8,128)(2,1)S(1)}, u32[]{:S(2)}, u32[]{:S(2)}) async-start(s16[32,208,128]{2,1,0:T(8,128)(2,1)} %get-tuple-element.37), calls=%async_computation.3 | async-start | bytes 3407872 | tf_op jit(solution)/shard_map/all_to_all | solution.py:456
  140.9 41.4 %collective-permute-start = (bf16[2,2048,256]{2,1,0:T(8,128)(2,1)}, bf16[2,2048,256]{2,1,0:T(8,128)(2,1)}, u32[]{:S(2)}, u32[]{:S(2)}) collective-permute-start(bf16[2,2048,256]{2,1,0:T(8,128)(2,1)} %broadcast_select_fusion.2), channel_id=1, source_target_pairs={{0,8},{4,20},{9,1},{13,29},{18,26},{22,6},{27,19},{31,15}} | collective-permute-start | bytes 6291464 | tf_op jit(solution)/shard_map/ppermute | solution.py:533
  146.3 36.0 %copy-start.38 = (bf16[2,2048,256]{2,1,0:T(8,128)(2,1)S(1)}, bf16[2,2048,256]{2,1,0:T(8,128)(2,1)}, u32[]{:S(2)}) copy-start(bf16[2,2048,256]{2,1,0:T(8,128)(2,1)} %broadcast_select_fusion.2) | copy-start | bytes 6291460
  187.1 50.2 %all-to-all-start.4 = ((s16[32,208,128]{2,1,0:T(8,128)(2,1)}), s16[32,208,128]{2,1,0:T(8,128)(2,1)S(1)}, u32[]{:S(2)}, u32[]{:S(2)}) async-start(s16[32,208,128]{2,1,0:T(8,128)(2,1)} %copy-done.11), calls=%async_computation.4 | async-start | bytes 3407872 | tf_op jit(solution)/shard_map/all_to_all | solution.py:456
  194.0 41.4 %copy-start.37 = (bf16[2,2048,256]{2,1,0:T(8,128)(2,1)S(1)}, bf16[2,2048,256]{2,1,0:T(8,128)(2,1)}, u32[]{:S(2)}) copy-start(bf16[2,2048,256]{2,1,0:T(8,128)(2,1)} %add.65) | copy-start | bytes 6291460
  194.0 41.4 %collective-permute-start.1 = (bf16[2,2048,256]{2,1,0:T(8,128)(2,1)}, bf16[2,2048,256]{2,1,0:T(8,128)(2,1)S(1)}, u32[]{:S(2)}, u32[]{:S(2)}) collective-permute-start(bf16[2,2048,256]{2,1,0:T(8,128)(2,1)} %add.65), channel_id=1, source_target_pairs={{0,16},{8,24},{4,12},{20,28},{9,25},{1,17},{13,5},{29,21},{18,2},{... | collective-permute-start | bytes 6291464 | tf_op jit(solution)/shard_map/ppermute | solution.py:533
  237.3 29.9 %collective-permute-start.2 = (bf16[2,2048,256]{2,1,0:T(8,128)(2,1)}, bf16[2,2048,256]{2,1,0:T(8,128)(2,1)}, u32[]{:S(2)}, u32[]{:S(2)}) collective-permute-start(bf16[2,2048,256]{2,1,0:T(8,128)(2,1)} %add.66), channel_id=1, source_target_pairs={{0,4},{4,0},{8,12},{12,8},{16,20},{20,16},{24,28},{28,24},{1,5},{5... | collective-permute-start | bytes 6291464 | tf_op jit(solution)/shard_map/ppermute | solution.py:537
  239.0 46.9 %all-to-all-start.5 = ((s16[32,208,128]{2,1,0:T(8,128)(2,1)}), s16[32,208,128]{2,1,0:T(8,128)(2,1)S(1)}, u32[]{:S(2)}, u32[]{:S(2)}) async-start(s16[32,208,128]{2,1,0:T(8,128)(2,1)} %pad_add_fusion), calls=%async_computation.5 | async-start | bytes 3407872 | tf_op jit(solution)/shard_map/all_to_all | solution.py:456
  248.1 19.1 %copy-start.39 = (bf16[2,2048,256]{2,1,0:T(8,128)(2,1)S(1)}, bf16[2,2048,256]{2,1,0:T(8,128)(2,1)}, u32[]{:S(2)}) copy-start(bf16[2,2048,256]{2,1,0:T(8,128)(2,1)} %add.66) | copy-start | bytes 6291460
  285.9 43.3 %all-to-all-start.6 = ((s16[32,208,128]{2,1,0:T(8,128)(2,1)}), s16[32,208,128]{2,1,0:T(8,128)(2,1)}, u32[]{:S(2)}, u32[]{:S(2)}) async-start(s16[32,208,128]{2,1,0:T(8,128)(2,1)} %middle.5), calls=%async_computation.6 | async-start | bytes 3407872 | tf_op jit(solution)/shard_map/all_to_all | solution.py:456
  311.9 20.6 %copy-start.26 = (bf16[80,240]{1,0:T(8,128)(2,1)S(1)}, bf16[80,240]{1,0:T(8,128)(2,1)}, u32[]{:S(2)}) copy-start(bf16[80,240]{1,0:T(8,128)(2,1)} %constant.131.clone.refs_5_.refs_2_.refs_3_) | copy-start | bytes 115204
  329.2 43.3 %all-to-all-start.7 = ((s16[32,208,128]{2,1,0:T(8,128)(2,1)}), s16[32,208,128]{2,1,0:T(8,128)(2,1)S(1)}, u32[]{:S(2)}, u32[]{:S(2)}) async-start(s16[32,208,128]{2,1,0:T(8,128)(2,1)} %get-tuple-element.51), calls=%async_computation.7 | async-start | bytes 3407872 | tf_op jit(solution)/shard_map/all_to_all | solution.py:456
  372.6 43.2 %all-to-all-start.8 = ((s16[32,208,128]{2,1,0:T(8,128)(2,1)}), s16[32,208,128]{2,1,0:T(8,128)(2,1)S(1)}, u32[]{:S(2)}, u32[]{:S(2)}) async-start(s16[32,208,128]{2,1,0:T(8,128)(2,1)} %copy-done.12), calls=%async_computation.8 | async-start | bytes 3407872 | tf_op jit(solution)/shard_map/all_to_all | solution.py:456
  415.8 21.9 %copy-start.6 = (s16[32,208,128]{2,1,0:T(8,128)(2,1)}, s16[32,208,128]{2,1,0:T(8,128)(2,1)S(1)}, u32[]{:S(2)}) copy-start(s16[32,208,128]{2,1,0:T(8,128)(2,1)S(1)} %all-to-all-done.8.refs_2_.refs_0_) | copy-start | bytes 5111812
  415.8 44.2 %all-to-all-start.9 = ((s16[32,208,128]{2,1,0:T(8,128)(2,1)}), s16[32,208,128]{2,1,0:T(8,128)(2,1)}, u32[]{:S(2)}, u32[]{:S(2)}) async-start(s16[32,208,128]{2,1,0:T(8,128)(2,1)} %get-tuple-element.58), calls=%async_computation.9 | async-start | bytes 3407872 | tf_op jit(solution)/shard_map/all_to_all | solution.py:456
  460.0 43.2 %all-to-all-start.10 = ((s16[32,208,128]{2,1,0:T(8,128)(2,1)}), s16[32,208,128]{2,1,0:T(8,128)(2,1)S(1)}, u32[]{:S(2)}, u32[]{:S(2)}) async-start(s16[32,208,128]{2,1,0:T(8,128)(2,1)} %copy-done.10), calls=%async_computation.10 | async-start | bytes 3407872 | tf_op jit(solution)/shard_map/all_to_all | solution.py:456
  483.7 23.9 %copy-start.3 = (s16[32,208,128]{2,1,0:T(8,128)(2,1)S(1)}, s16[32,208,128]{2,1,0:T(8,128)(2,1)}, u32[]{:S(2)}) copy-start(s16[32,208,128]{2,1,0:T(8,128)(2,1)} %copy-done.2) | copy-start | bytes 5111812
  504.4 43.3 %all-to-all-start.11 = ((s16[32,208,128]{2,1,0:T(8,128)(2,1)}), s16[32,208,128]{2,1,0:T(8,128)(2,1)}, u32[]{:S(2)}, u32[]{:S(2)}) async-start(s16[32,208,128]{2,1,0:T(8,128)(2,1)} %copy-done.13), calls=%async_computation.11 | async-start | bytes 3407872 | tf_op jit(solution)/shard_map/all_to_all | solution.py:456
  507.7 40.1 %copy-start.7 = (s16[32,208,128]{2,1,0:T(8,128)(2,1)S(1)}, s16[32,208,128]{2,1,0:T(8,128)(2,1)}, u32[]{:S(2)}) copy-start(s16[32,208,128]{2,1,0:T(8,128)(2,1)} %copy-done.6) | copy-start | bytes 5111812
  (34 other events, 125.0 us)
Sparse Core Ops, SparseCore 0:
  44.3 46.9 all-gather.1

commit v5 on v4

--- a/solution.py
+++ b/solution.py
@@ -425,6 +425,42 @@
     )(*operands)
 
 
+def pick_kernel(index, phi, psi, out_ref, sums):
+    step = pl.program_id(0)
+    rows, chunk = index.shape[0], phi.shape[0]
+    cell = lax.broadcasted_iota(jnp.int32, (rows, chunk), 1) + step * chunk
+    chosen = jnp.where(cell == index[...], 1.0, 0.0).astype(jnp.bfloat16)
+
+    @pl.when(step == 0)
+    def _():
+        sums[...] = jnp.zeros_like(sums)
+
+    for i, field in enumerate((phi, psi)):
+        sums[i] += jnp.dot(chosen, field[...], preferred_element_type=jnp.float32)
+
+    @pl.when(step == pl.num_programs(0) - 1)
+    def _():
+        out_ref[...] = sums[...].astype(out_ref.dtype)
+
+
+def pick_rows(index, phi, psi):
+    rows = index.shape[0]
+    total, orbitals = phi.shape
+    chunk = total // 5 if total % 80 == 0 else total
+    field = pl.BlockSpec((chunk, orbitals), lambda i: (i, 0))
+    return pl.pallas_call(
+        pick_kernel,
+        grid=(total // chunk,),
+        in_specs=[pl.BlockSpec((rows, 1), lambda i: (0, 0)), field, field],
+        out_specs=pl.BlockSpec((2, rows, orbitals), lambda i: (0, 0, 0)),
+        out_shape=jax.ShapeDtypeStruct((2, rows, orbitals), phi.dtype),
+        scratch_shapes=[pltpu.VMEM((2, rows, orbitals), jnp.float32)],
+        compiler_params=pltpu.CompilerParams(vmem_limit_bytes=50 * MIB),
+        cost_estimate=cost(total / 2500, 4 * total * orbitals),
+        name="pick",
+    )(index.reshape(rows, 1), phi, psi)
+
+
 def on_device(phi, psi, points):
     col_count = lax.axis_size("col")
     row_count = lax.axis_size("row")
@@ -447,17 +483,19 @@
         (global_x - col_index * plane_count) * line_count + global_y - row_index * line_count
     ) * depth + points % depth
 
+    exchange = lambda a: lax.all_to_all(a, axes, split_axis=0, concat_axis=0, tiled=True)
+
+    held = min(owned, PB)
+    piece_rows = 2 * PB // devices
+    offered = pick_rows(local_cell[:held], flat_phi, flat_psi)
+    local_cell, offered = lax.optimization_barrier((local_cell, offered))
     own = jnp.stack(
         [
             jnp.take(flat_phi, local_cell, axis=0, mode="clip"),
             jnp.take(flat_psi, local_cell, axis=0, mode="clip"),
         ]
     )
-    exchange = lambda a: lax.all_to_all(a, axes, split_axis=0, concat_axis=0, tiled=True)
-
-    held = min(owned, PB)
-    piece_rows = 2 * PB // devices
-    offered = jnp.concatenate([own[:, :held]] * (PB // held), axis=1)
+    offered = jnp.concatenate([offered] * (PB // held), axis=1)
     offered = exchange(offered.reshape(devices, piece_rows, orbitals))
     own, offered = lax.optimization_barrier((own, offered))
     owner = me * piece_rows % PB // owned
@@ -507,12 +545,12 @@
 
     make(0, parts[0][:1], lead_inverse)
     if parts[0][1:]:
-        make(0, parts[0][1:], after(lead_inverse, row_samples))
+        make(0, parts[0][1:], after(lead_inverse, outgoing[0][0]))
     row_start = row_index * row_samples.shape[1]
     col_start = col_index * row_count * owned
     scalar = lambda *v: jnp.stack([jnp.asarray(a, jnp.int32) for a in v])
 
-    latest = outgoing[0][0]
+    latest = previous = outgoing[0][0]
     members = row_count // col_count
     bits = [1 << b for b in range(row_count.bit_length() - 1)]
     inner = [b for b in bits if b < members]
@@ -544,20 +582,27 @@
 
     arrived = []
 
+    exchanges = 0
+
     def in_turn(block, *ready):
-        nonlocal latest, columns
-        before, latest = latest, lax.optimization_barrier((block, latest, columns, *ready))[0]
-        if steps and arrived:
-            columns = steps.pop(0)(after(columns, before))
-        latest = exchange(latest)
+        nonlocal latest, previous, columns, exchanges
+        previous = latest
+        even = exchanges % 2 == 0
+        due = [columns] if exchanges and (even or not steps) else []
+        block = lax.optimization_barrier((block, previous, *due, *ready))[0]
+        if steps and even:
+            columns = steps.pop(0)(after(columns, previous))
+        exchanges += 1
+        latest = exchange(block)
         return latest
 
     second_round = parts[1][0][0]
-    panel_round = max(min(2, rounds - 1), second_round)
+    panel_round = max(min(3, rounds - 1), second_round)
     schur_round = max(min(3, rounds - 1), panel_round)
     ready = []
     returned = []
     for k in range(rounds + 1):
+        updated = []
         if k == second_round:
             gated = after(inverse, latest if k < 2 else arrived[k - 1])
             make(1, parts[1], gated)
@@ -568,12 +613,12 @@
                 pieces.append(jnp.zeros((spare, padded, LANES), jnp.int16))
             sent = pieces[0] if len(pieces) == 1 else jnp.concatenate(pieces, axis=0)
             arrived.append(in_turn(sent, *ready))
-            ready = [inverse] if k == 0 else []
+            ready = [inverse, row_samples] if k == 0 else []
         if k == panel_round:
             while steps:
                 columns = steps.pop(0)(columns)
             col_samples = columns
-            gated = after(inverse, latest)
+            gated = after(inverse, previous)
             panel, row_high, row_low = panel_rows(scalar(row_start), row_samples, pivot, gated)
             _, col_high, col_low = panel_rows(scalar(col_start), col_samples, pivot, gated)
             ready += [row_high, col_high]
@@ -583,14 +628,15 @@
                 (row_samples[0], row_samples[1], row_high, row_low),
                 (col_samples[0], col_samples[1], col_high, col_low),
             )
-            ready += [schur]
+            updated = [schur]
         if k > 0:
             z_index = ((k - 1) * devices + me) % depth
             z_freq = jnp.minimum(z_index, depth - z_index).astype(jnp.int32).reshape(1)
             back = middle(
                 z_freq, arrived[k - 1], x_table, y_table, grid_x, grid_y, line_count
             )
-            returned.append(in_turn(back))
+            returned.append(in_turn(back, *ready))
+            ready = updated
 
     potential = None
     for h in range(halves):

time: 567 us -> 583 us (1.028)
  Pallas kernels: 227 us -> 237 us
    ppermute x2, waiting for transfers between devices: 28.9 us -> 52.3 us  [on_device(): lax.ppermute(block, axes, pairs)]
    all_to_all x12, waiting for transfers between devices: 162 us -> 143 us  [on_device(): lax.all_to_all(a, axes, split_axis=0, concat_axis=0, tiled=True)]
    pallas_call x0 -> x1, Pallas kernels: none -> 10 us  [pick_rows(): pl.pallas_call(pick_kernel, grid=(total // chunk,), in_specs=[pl.BlockSpe...]
    all_gather x1, waiting for transfers between devices: 19.7 us -> 11.9 us  [on_device(): row_samples = lax.all_gather(own, 'col', axis=1, tiled=True)]
    unnamed x84 -> x80, local copies, waits for them, and re-layouts: 22 us -> 23.9 us
  transfers between devices with their start and end apart: 16 -> 16, of which waited for: 13 -> 11; matrix products, arithmetic and copies ran while one was open for 3% -> 6% of each run, Pallas kernels for 39% -> 38%
where the time goes in v5:
time: 583 us; the launch traced here: 581 us
  Pallas kernels  237 us (41%)
  waiting for transfers between devices  207 us (36%)
  starting transfers between devices  63.2 us (11%)
  local copies, waits for them, and re-layouts  39.8 us (7%)
  other arithmetic  18.8 us (3%)
  between operations  14.6 us (3%)
    all_to_all x12, waiting for transfers between devices, on_device(): lax.all_to_all(a, axes, split_axis=0, concat_axis=0, tiled=True)  143 us
    pallas_call x5, Pallas kernels, middle(): pl.pallas_call(lambda *refs: middle_kernel(sizes, padded, *refs), in_spec...  93.6 us
    pallas_call x3, Pallas kernels, source(): pl.pallas_call(lambda *refs: source_kernel(group, cells, depth, padded, p...  56.7 us
    all_to_all x12, starting transfers between devices, on_device(): lax.all_to_all(a, axes, split_axis=0, concat_axis=0, tiled=True)  55 us
    ppermute x2, waiting for transfers between devices, on_device(): lax.ppermute(block, axes, pairs)  52.3 us
    pallas_call x1, Pallas kernels, schur_block(): pl.pallas_call(schur_kernel, grid=(rows // row_tile, cols // col_tile), i...  34.5 us
    unnamed x80, local copies, waits for them, and re-layouts  23.9 us
    pallas_call x2, Pallas kernels, target(): pl.pallas_call(lambda *refs: target_kernel(group, cells, depth, spans, *r...  17.2 us
  transfers between devices with their start and end apart: 16, of which 11 were waited for; matrix products, arithmetic and copies ran while one was open for 6% of the time, Pallas kernels for 38%

profile of v5, /device:TPU:1, one launch (start us, length us, event | category | flops | bytes accessed | tf_op | source)
XLA Modules:
  0.0 580.8 jit_solution(3623504777770606104)
XLA Ops:
  8.0 10.0 %pick.1 = bf16[2,256,256]{2,1,0:T(8,128)(2,1)} custom-call(s32[256,1]{1,0:T(8,128)S(1)} %copy.10.index, bf16[16000,256]{1,0:T(8,128)(2,1)} %bitcast.47, bf16[16000,256]{1,0:T(8,128)(2,1)} %bitcast.42), custom_call_target="tpu_custom_call" | custom-call | flops 7360000000 | bytes 16384000 | tf_op jit(solution)/shard_map/pick/pallas_call | solution.py:451
  18.0 7.1 %all-to-all-start = ((bf16[32,16,256]{2,1,0:T(8,128)(2,1)}), bf16[32,16,256]{2,1,0:T(8,128)(2,1)S(1)}, u32[]{:S(2)}, u32[]{:S(2)}) async-start(bf16[32,16,256]{2,1,0:T(8,128)(2,1)} %bitcast.7), calls=%async_computation | async-start | bytes 524288 | tf_op jit(solution)/shard_map/all_to_all | solution.py:486
  45.2 9.6 %all-to-all-done.1 = bf16[32,16,256]{2,1,0:T(8,128)(2,1)S(1)} async-done(((bf16[32,16,256]{2,1,0:T(8,128)(2,1)}), bf16[32,16,256]{2,1,0:T(8,128)(2,1)S(1)}, u32[]{:S(2)}, u32[]{:S(2)}) %all-to-all-start.1) | async-done | bytes 262176 | tf_op jit(solution)/shard_map/all_to_all | solution.py:486
  59.9 14.8 %source.3 = s16[32,208,128]{2,1,0:T(8,128)(2,1)} custom-call(bf16[16000,256]{1,0:T(8,128)(2,1)} %bitcast.49, bf16[16000,256]{1,0:T(8,128)(2,1)} %bitcast.44, bf16[128,256]{1,0:T(8,128)(2,1)S(1)} %get-tuple-element.72.pivot_a.refs_2_, bf16[128,256]{1,0:T(8,128)(2,1)S(1)} %get-tuple-element.71.pivot_b.refs_3_, f32[128,128]{1,0:T(8,128)S(1)} %lead.1.lead_inverse.refs_4_, ...), custom_call_target="tpu_custom_call" | custom-call | flops 30666665984 | bytes 16384000 | tf_op jit(solution)/shard_map/source/pallas_call | solution.py:107
  84.7 14.8 %source.4 = (s16[32,208,128]{2,1,0:T(8,128)(2,1)S(1)}, s16[16,208,128]{2,1,0:T(8,128)(2,1)S(1)}) custom-call(bf16[16000,256]{1,0:T(8,128)(2,1)} %bitcast.50, bf16[16000,256]{1,0:T(8,128)(2,1)} %bitcast.45, bf16[128,256]{1,0:T(8,128)(2,1)S(1)} %get-tuple-element.72.pivot_a.refs_2_, bf16[128,256]{1,0:T(8,128)(2,1)S(1)} %get-tuple-element.71.pivot_b.refs_3_, ...), custom_call_target="tpu_custom_call" | custom-call | flops 30666665984 | bytes 16384000 | tf_op jit(solution)/shard_map/source/pallas_call | solution.py:107
  101.7 11.9 %all-gather.2.cloned.1.call-done = bf16[2,2048,256]{2,1,0:T(8,128)(2,1)} async-done(((bf16[2,512,256]{2,1,0:T(8,128)(2,1)}), bf16[2,2048,256]{2,1,0:T(8,128)(2,1)}) %all-gather.2.cloned.1.call-update) | async-done | bytes 2097168 | tf_op jit(solution)/shard_map/all_gather | solution.py:505
  113.6 16.7 %all-to-all-done.2.refs_1_ = s16[32,208,128]{2,1,0:T(8,128)(2,1)S(1)} async-done(((s16[32,208,128]{2,1,0:T(8,128)(2,1)}), s16[32,208,128]{2,1,0:T(8,128)(2,1)S(1)}, u32[]{:S(2)}, u32[]{:S(2)}) %all-to-all-start.2) | async-done | bytes 1703968 | tf_op jit(solution)/shard_map/all_to_all | solution.py:486
  140.6 17.9 %middle.6 = s16[32,208,128]{2,1,0:T(8,128)(2,1)S(1)} custom-call(s32[1]{0:T(128)} %bitcast.15.refs_0_, s16[32,208,128]{2,1,0:T(8,128)(2,1)S(1)} %all-to-all-done.2.refs_1_, bf16[80,240]{1,0:T(8,128)(2,1)S(1)} %copy-done.22, bf16[80,240]{1,0:T(8,128)(2,1)S(1)} %copy-done.22), custom_call_target="tpu_custom_call" | custom-call | flops 18400000000 | bytes 3407872 | tf_op jit(solution)/shard_map/middle/pallas_call | solution.py:195
  159.7 15.6 %collective-permute-done = bf16[2,2048,256]{2,1,0:T(8,128)(2,1)} collective-permute-done((bf16[2,2048,256]{2,1,0:T(8,128)(2,1)}, bf16[2,2048,256]{2,1,0:T(8,128)(2,1)}, u32[]{:S(2)}, u32[]{:S(2)}) %collective-permute-start) | collective-permute-done | bytes 2097184 | tf_op jit(solution)/shard_map/ppermute | solution.py:571
  188.7 27.1 %source.5 = (s16[16,208,128]{2,1,0:T(8,128)(2,1)S(1)}, s16[32,208,128]{2,1,0:T(8,128)(2,1)}, s16[32,208,128]{2,1,0:T(8,128)(2,1)}) custom-call(bf16[16000,256]{1,0:T(8,128)(2,1)} %bitcast.51, bf16[16000,256]{1,0:T(8,128)(2,1)} %bitcast.46, bf16[256,256]{1,0:T(8,128)(2,1)S(1)} %bitcast.36, bf16[256,256]{1,0:T(8,128)(2,1)S(1)} %bitcast.32, ...), custom_call_target="tpu_custom_call" | custom-call | flops 30666665984 | bytes 16384000 | tf_op jit(solution)/shard_map/source/pallas_call | solution.py:107
  217.1 9.0 %all-to-all-done.4.refs_0_ = s16[32,208,128]{2,1,0:T(8,128)(2,1)S(1)} async-done(((s16[32,208,128]{2,1,0:T(8,128)(2,1)}), s16[32,208,128]{2,1,0:T(8,128)(2,1)S(1)}, u32[]{:S(2)}, u32[]{:S(2)}) %all-to-all-start.4) | async-done | bytes 1703968 | tf_op jit(solution)/shard_map/all_to_all | solution.py:486
  234.0 36.7 %collective-permute-done.1 = bf16[2,2048,256]{2,1,0:T(8,128)(2,1)} collective-permute-done((bf16[2,2048,256]{2,1,0:T(8,128)(2,1)}, bf16[2,2048,256]{2,1,0:T(8,128)(2,1)}, u32[]{:S(2)}, u32[]{:S(2)}) %collective-permute-start.1) | collective-permute-done | bytes 2097184 | tf_op jit(solution)/shard_map/ppermute | solution.py:571
  276.0 19.1 %middle.5 = s16[32,208,128]{2,1,0:T(8,128)(2,1)} custom-call(s32[1]{0:T(128)} %bitcast.14.refs_0_, s16[32,208,128]{2,1,0:T(8,128)(2,1)S(1)} %all-to-all-done.3.refs_1_, bf16[80,240]{1,0:T(8,128)(2,1)S(1)} %copy-done.24, bf16[80,240]{1,0:T(8,128)(2,1)S(1)} %copy-done.24), custom_call_target="tpu_custom_call" | custom-call | flops 18400000000 | bytes 3407872 | tf_op jit(solution)/shard_map/middle/pallas_call | solution.py:195
  308.8 32.9 %all-to-all-done.6.refs_1_ = s16[32,208,128]{2,1,0:T(8,128)(2,1)S(1)} async-done(((s16[32,208,128]{2,1,0:T(8,128)(2,1)}), s16[32,208,128]{2,1,0:T(8,128)(2,1)S(1)}, u32[]{:S(2)}, u32[]{:S(2)}) %all-to-all-start.6) | async-done | bytes 1703968 | tf_op jit(solution)/shard_map/all_to_all | solution.py:486
  345.7 19.5 %middle.7 = s16[32,208,128]{2,1,0:T(8,128)(2,1)S(1)} custom-call(s32[1]{0:T(128)} %bitcast.20.refs_0_, s16[32,208,128]{2,1,0:T(8,128)(2,1)} %all-to-all-done.5.refs_1_, bf16[80,240]{1,0:T(8,128)(2,1)S(1)} %copy-done.25, bf16[80,240]{1,0:T(8,128)(2,1)S(1)} %copy-done.25), custom_call_target="tpu_custom_call" | custom-call | flops 18400000000 | bytes 3407872 | tf_op jit(solution)/shard_map/middle/pallas_call | solution.py:195
  375.0 9.1 %panel.3 = (f32[4096,256]{1,0:T(8,128)}, bf16[4096,256]{1,0:T(8,128)(2,1)S(1)}, bf16[4096,256]{1,0:T(8,128)(2,1)S(1)}) custom-call(s32[1]{0:T(128)} %bitcast.1.first_row, bf16[4096,256]{1,0:T(8,128)(2,1)S(1)} %get-tuple-element.66.left_a.col_a, bf16[4096,256]{1,0:T(8,128)(2,1)S(1)} %get-tuple-element.65.left_b.col_b, bf16[256,256]{1,0:T(8,128)(2,1)S(1)} %bitcast.38, ...), custom_call_target="tpu_custom_call" | custom-call | flops 11776000000 | bytes 12582912 | tf_op jit(solution)/shard_map/panel/pallas_call | solution.py:281
  396.3 34.5 %schur.1 = f32[2048,4096]{1,0:T(8,128)} custom-call(s32[2]{0:T(128)S(1)} %pad_add_fusion.1.offsets, bf16[2048,256]{1,0:T(8,128)(2,1)S(1)} %copy-done.16, bf16[2048,256]{1,0:T(8,128)(2,1)S(1)} %copy-done.14, bf16[2048,256]{1,0:T(8,128)(2,1)S(1)} %copy-done.30, bf16[2048,256]{1,0:T(8,128)(2,1)} %copy-done.31, bf16[4096,256]{1,0:T(8,128)(2,1)} %copy-done.1, ...), custom_call_target="tpu_custom_call" | custom-call | flops 40195411968 | bytes 33554432 | tf_op jit(solution)/shard_map/schur/pallas_call | solution.py:329
  436.7 17.9 %middle.8 = s16[32,208,128]{2,1,0:T(8,128)(2,1)S(1)} custom-call(s32[1]{0:T(128)} %bitcast.21.refs_0_, s16[32,208,128]{2,1,0:T(8,128)(2,1)S(1)} %all-to-all-done.7.refs_1_, bf16[80,240]{1,0:T(8,128)(2,1)S(1)} %copy-done.26, bf16[80,240]{1,0:T(8,128)(2,1)S(1)} %copy-done.26), custom_call_target="tpu_custom_call" | custom-call | flops 18400000000 | bytes 3407872 | tf_op jit(solution)/shard_map/middle/pallas_call | solution.py:195
  455.8 21.0 %all-to-all-done.9.refs_1_ = s16[32,208,128]{2,1,0:T(8,128)(2,1)} async-done(((s16[32,208,128]{2,1,0:T(8,128)(2,1)}), s16[32,208,128]{2,1,0:T(8,128)(2,1)}, u32[]{:S(2)}, u32[]{:S(2)}) %all-to-all-start.9) | async-done | bytes 1703968 | tf_op jit(solution)/shard_map/all_to_all | solution.py:486
  480.1 19.3 %middle.9 = s16[32,208,128]{2,1,0:T(8,128)(2,1)S(1)} custom-call(s32[1]{0:T(128)} %bitcast.22.refs_0_, s16[32,208,128]{2,1,0:T(8,128)(2,1)} %all-to-all-done.9.refs_1_, bf16[80,240]{1,0:T(8,128)(2,1)S(1)} %copy-done.26, bf16[80,240]{1,0:T(8,128)(2,1)S(1)} %copy-done.26), custom_call_target="tpu_custom_call" | custom-call | flops 18400000000 | bytes 3407872 | tf_op jit(solution)/shard_map/middle/pallas_call | solution.py:195
  500.6 19.6 %all-to-all-done.10.refs_1_ = s16[32,208,128]{2,1,0:T(8,128)(2,1)} async-done(((s16[32,208,128]{2,1,0:T(8,128)(2,1)}), s16[32,208,128]{2,1,0:T(8,128)(2,1)}, u32[]{:S(2)}, u32[]{:S(2)}) %all-to-all-start.10) | async-done | bytes 1703968 | tf_op jit(solution)/shard_map/all_to_all | solution.py:486
  523.5 8.3 %target.2.refs_4_ = f32[16000,256]{1,0:T(8,128)} custom-call(s16[32,208,128]{2,1,0:T(8,128)(2,1)S(1)} %copy-done.3, s16[32,208,128]{2,1,0:T(8,128)(2,1)S(1)} %copy-done.5, s16[32,208,128]{2,1,0:T(8,128)(2,1)} %copy-done.6, bf16[80,240]{1,0:T(8,128)(2,1)S(1)} %copy-done.26), custom_call_target="tpu_custom_call" | custom-call | flops 15333332992 | bytes 12288000 | tf_op jit(solution)/shard_map/target/pallas_call | solution.py:246
  531.9 31.8 %all-to-all-done.11.refs_2_ = s16[32,208,128]{2,1,0:T(8,128)(2,1)} async-done(((s16[32,208,128]{2,1,0:T(8,128)(2,1)}), s16[32,208,128]{2,1,0:T(8,128)(2,1)}, u32[]{:S(2)}, u32[]{:S(2)}) %all-to-all-start.11) | async-done | bytes 1703968 | tf_op jit(solution)/shard_map/all_to_all | solution.py:486
  565.1 8.8 %target.3 = f32[16000,256]{1,0:T(8,128)} custom-call(s16[32,208,128]{2,1,0:T(8,128)(2,1)S(1)} %copy-done.7, s16[32,208,128]{2,1,0:T(8,128)(2,1)} %all-to-all-done.10.refs_1_, s16[32,208,128]{2,1,0:T(8,128)(2,1)} %all-to-all-done.11.refs_2_, bf16[80,240]{1,0:T(8,128)(2,1)S(1)} %copy-done.26, f32[16000,256]{1,0:T(8,128)} %target.2.refs_4_), custom_call_target="tpu_custom_call", output_to_operand_aliasing={{}: (4, {})} | custom-call | flops 15333332992 | bytes 12288000 | tf_op jit(solution)/shard_map/target/pallas_call | solution.py:246
  (124 shorter events, 133.2 us)
Async XLA Ops:
  18.0 19.9 %all-to-all-start = ((bf16[32,16,256]{2,1,0:T(8,128)(2,1)}), bf16[32,16,256]{2,1,0:T(8,128)(2,1)S(1)}, u32[]{:S(2)}, u32[]{:S(2)}) async-start(bf16[32,16,256]{2,1,0:T(8,128)(2,1)} %bitcast.7), calls=%async_computation | async-start | bytes 524288 | tf_op jit(solution)/shard_map/all_to_all | solution.py:486
  38.7 16.2 %all-to-all-start.1 = ((bf16[32,16,256]{2,1,0:T(8,128)(2,1)}), bf16[32,16,256]{2,1,0:T(8,128)(2,1)S(1)}, u32[]{:S(2)}, u32[]{:S(2)}) async-start(bf16[32,16,256]{2,1,0:T(8,128)(2,1)} %broadcast_in_dim.18), calls=%async_computation.1 | async-start | bytes 524288 | tf_op jit(solution)/shard_map/all_to_all | solution.py:486
  44.5 69.1 %all-gather.2.cloned.1.call-start = ((), (), s32[]{:S(2)}) async-start(), calls=%async_computation.12 | async-start | bytes 2621440 | tf_op jit(solution)/shard_map/all_gather | solution.py:505
  74.7 55.5 %all-to-all-start.2 = ((s16[32,208,128]{2,1,0:T(8,128)(2,1)}), s16[32,208,128]{2,1,0:T(8,128)(2,1)S(1)}, u32[]{:S(2)}, u32[]{:S(2)}) async-start(s16[32,208,128]{2,1,0:T(8,128)(2,1)} %source.3), calls=%async_computation.2 | async-start | bytes 3407872 | tf_op jit(solution)/shard_map/all_to_all | solution.py:486
  130.3 49.1 %all-to-all-start.3 = ((s16[32,208,128]{2,1,0:T(8,128)(2,1)}), s16[32,208,128]{2,1,0:T(8,128)(2,1)S(1)}, u32[]{:S(2)}, u32[]{:S(2)}) async-start(s16[32,208,128]{2,1,0:T(8,128)(2,1)} %copy-done.8), calls=%async_computation.3 | async-start | bytes 3407872 | tf_op jit(solution)/shard_map/all_to_all | solution.py:486
  136.7 38.5 %collective-permute-start = (bf16[2,2048,256]{2,1,0:T(8,128)(2,1)}, bf16[2,2048,256]{2,1,0:T(8,128)(2,1)}, u32[]{:S(2)}, u32[]{:S(2)}) collective-permute-start(bf16[2,2048,256]{2,1,0:T(8,128)(2,1)} %broadcast_select_fusion.2), channel_id=1, source_target_pairs={{0,8},{4,20},{9,1},{13,29},{18,26},{22,6},{27,19},{31,15}} | collective-permute-start | bytes 6291464 | tf_op jit(solution)/shard_map/ppermute | solution.py:571
  179.3 46.8 %all-to-all-start.4 = ((s16[32,208,128]{2,1,0:T(8,128)(2,1)}), s16[32,208,128]{2,1,0:T(8,128)(2,1)S(1)}, u32[]{:S(2)}, u32[]{:S(2)}) async-start(s16[32,208,128]{2,1,0:T(8,128)(2,1)} %copy-done.11), calls=%async_computation.4 | async-start | bytes 3407872 | tf_op jit(solution)/shard_map/all_to_all | solution.py:486
  188.7 27.1 %copy-start.18 = (s16[16,208,128]{2,1,0:T(8,128)(2,1)S(1)}, s16[16,208,128]{2,1,0:T(8,128)(2,1)}, u32[]{:S(2)}) copy-start(s16[16,208,128]{2,1,0:T(8,128)(2,1)} %copy-done.17) | copy-start | bytes 2555908
  226.2 48.7 %copy-start.2 = (s16[32,208,128]{2,1,0:T(8,128)(2,1)}, s16[32,208,128]{2,1,0:T(8,128)(2,1)S(1)}, u32[]{:S(2)}) copy-start(s16[32,208,128]{2,1,0:T(8,128)(2,1)S(1)} %all-to-all-done.4.refs_0_) | copy-start | bytes 5111812
  226.2 48.7 %all-to-all-start.5 = ((s16[32,208,128]{2,1,0:T(8,128)(2,1)}), s16[32,208,128]{2,1,0:T(8,128)(2,1)}, u32[]{:S(2)}, u32[]{:S(2)}) async-start(s16[32,208,128]{2,1,0:T(8,128)(2,1)} %pad_add_fusion), calls=%async_computation.5 | async-start | bytes 3407872 | tf_op jit(solution)/shard_map/all_to_all | solution.py:486
  229.4 41.4 %collective-permute-start.1 = (bf16[2,2048,256]{2,1,0:T(8,128)(2,1)}, bf16[2,2048,256]{2,1,0:T(8,128)(2,1)}, u32[]{:S(2)}, u32[]{:S(2)}) collective-permute-start(bf16[2,2048,256]{2,1,0:T(8,128)(2,1)} %add.65), channel_id=1, source_target_pairs={{0,16},{8,24},{4,12},{20,28},{9,25},{1,17},{13,5},{29,21},{18,2},{... | collective-permute-start | bytes 6291464 | tf_op jit(solution)/shard_map/ppermute | solution.py:571
  274.9 30.1 %collective-permute-start.2 = (bf16[2,2048,256]{2,1,0:T(8,128)(2,1)}, bf16[2,2048,256]{2,1,0:T(8,128)(2,1)}, u32[]{:S(2)}, u32[]{:S(2)}) collective-permute-start(bf16[2,2048,256]{2,1,0:T(8,128)(2,1)} %add.66), channel_id=1, source_target_pairs={{0,4},{4,0},{8,12},{12,8},{16,20},{20,16},{24,28},{28,24},{1,5},{5... | collective-permute-start | bytes 6291464 | tf_op jit(solution)/shard_map/ppermute | solution.py:575
  295.1 46.7 %all-to-all-start.6 = ((s16[32,208,128]{2,1,0:T(8,128)(2,1)}), s16[32,208,128]{2,1,0:T(8,128)(2,1)S(1)}, u32[]{:S(2)}, u32[]{:S(2)}) async-start(s16[32,208,128]{2,1,0:T(8,128)(2,1)} %middle.5), calls=%async_computation.6 | async-start | bytes 3407872 | tf_op jit(solution)/shard_map/all_to_all | solution.py:486
  341.8 45.0 %all-to-all-start.7 = ((s16[32,208,128]{2,1,0:T(8,128)(2,1)}), s16[32,208,128]{2,1,0:T(8,128)(2,1)S(1)}, u32[]{:S(2)}, u32[]{:S(2)}) async-start(s16[32,208,128]{2,1,0:T(8,128)(2,1)} %get-tuple-element.52), calls=%async_computation.7 | async-start | bytes 3407872 | tf_op jit(solution)/shard_map/all_to_all | solution.py:486
  345.7 20.7 %copy-start.38 = (bf16[2,2048,256]{2,1,0:T(8,128)(2,1)S(1)}, bf16[2,2048,256]{2,1,0:T(8,128)(2,1)}, u32[]{:S(2)}) copy-start(bf16[2,2048,256]{2,1,0:T(8,128)(2,1)} %get-tuple-element.67) | copy-start | bytes 6291460
  345.7 20.7 %copy-start.39 = (bf16[2,2048,256]{2,1,0:T(8,128)(2,1)S(1)}, bf16[2,2048,256]{2,1,0:T(8,128)(2,1)}, u32[]{:S(2)}) copy-start(bf16[2,2048,256]{2,1,0:T(8,128)(2,1)} %get-tuple-element.68) | copy-start | bytes 6291460
  367.3 7.7 %copy-start = (bf16[4096,256]{1,0:T(8,128)(2,1)}, bf16[4096,256]{1,0:T(8,128)(2,1)S(1)}, u32[]{:S(2)}) copy-start(bf16[4096,256]{1,0:T(8,128)(2,1)S(1)} %get-tuple-element.65.left_b.col_b) | copy-start | bytes 6291460
  386.8 45.9 %all-to-all-start.8 = ((s16[32,208,128]{2,1,0:T(8,128)(2,1)}), s16[32,208,128]{2,1,0:T(8,128)(2,1)S(1)}, u32[]{:S(2)}, u32[]{:S(2)}) async-start(s16[32,208,128]{2,1,0:T(8,128)(2,1)} %copy-done.9), calls=%async_computation.8 | async-start | bytes 3407872 | tf_op jit(solution)/shard_map/all_to_all | solution.py:486
  432.7 22.0 %copy-start.6 = (s16[32,208,128]{2,1,0:T(8,128)(2,1)}, s16[32,208,128]{2,1,0:T(8,128)(2,1)S(1)}, u32[]{:S(2)}) copy-start(s16[32,208,128]{2,1,0:T(8,128)(2,1)S(1)} %all-to-all-done.8.refs_2_.refs_0_) | copy-start | bytes 5111812
  432.7 44.2 %all-to-all-start.9 = ((s16[32,208,128]{2,1,0:T(8,128)(2,1)}), s16[32,208,128]{2,1,0:T(8,128)(2,1)}, u32[]{:S(2)}, u32[]{:S(2)}) async-start(s16[32,208,128]{2,1,0:T(8,128)(2,1)} %get-tuple-element.62), calls=%async_computation.9 | async-start | bytes 3407872 | tf_op jit(solution)/shard_map/all_to_all | solution.py:486
  476.9 43.3 %all-to-all-start.10 = ((s16[32,208,128]{2,1,0:T(8,128)(2,1)}), s16[32,208,128]{2,1,0:T(8,128)(2,1)}, u32[]{:S(2)}, u32[]{:S(2)}) async-start(s16[32,208,128]{2,1,0:T(8,128)(2,1)} %copy-done.10), calls=%async_computation.10 | async-start | bytes 3407872 | tf_op jit(solution)/shard_map/all_to_all | solution.py:486
  500.6 22.9 %copy-start.3 = (s16[32,208,128]{2,1,0:T(8,128)(2,1)S(1)}, s16[32,208,128]{2,1,0:T(8,128)(2,1)}, u32[]{:S(2)}) copy-start(s16[32,208,128]{2,1,0:T(8,128)(2,1)} %copy-done.2) | copy-start | bytes 5111812
  500.6 22.9 %copy-start.5 = (s16[32,208,128]{2,1,0:T(8,128)(2,1)S(1)}, s16[32,208,128]{2,1,0:T(8,128)(2,1)}, u32[]{:S(2)}) copy-start(s16[32,208,128]{2,1,0:T(8,128)(2,1)} %copy-done.4) | copy-start | bytes 5111812
  520.2 43.4 %all-to-all-start.11 = ((s16[32,208,128]{2,1,0:T(8,128)(2,1)}), s16[32,208,128]{2,1,0:T(8,128)(2,1)}, u32[]{:S(2)}, u32[]{:S(2)}) async-start(s16[32,208,128]{2,1,0:T(8,128)(2,1)} %copy-done.12), calls=%async_computation.11 | async-start | bytes 3407872 | tf_op jit(solution)/shard_map/all_to_all | solution.py:486
  (32 other events, 61.4 us)
Sparse Core Ops, SparseCore 0:
  47.5 66.0 all-gather.1

commit v6 on v4

--- a/solution.py
+++ b/solution.py
@@ -459,7 +459,6 @@
     piece_rows = 2 * PB // devices
     offered = jnp.concatenate([own[:, :held]] * (PB // held), axis=1)
     offered = exchange(offered.reshape(devices, piece_rows, orbitals))
-    own, offered = lax.optimization_barrier((own, offered))
     owner = me * piece_rows % PB // owned
     piece = lax.dynamic_index_in_dim(offered, owner, axis=0, keepdims=True)
     pivot = exchange(jnp.broadcast_to(piece, offered.shape)).reshape(2, PB, orbitals)
@@ -507,7 +506,7 @@
 
     make(0, parts[0][:1], lead_inverse)
     if parts[0][1:]:
-        make(0, parts[0][1:], after(lead_inverse, row_samples))
+        make(0, parts[0][1:], after(lead_inverse, outgoing[0][0]))
     row_start = row_index * row_samples.shape[1]
     col_start = col_index * row_count * owned
     scalar = lambda *v: jnp.stack([jnp.asarray(a, jnp.int32) for a in v])
@@ -530,13 +529,19 @@
                 pairs += [
                     (r * col_count + c, (r ^ order[t]) * col_count + c) for r in holders
                 ]
-        steps.append(lambda block, pairs=pairs: block + lax.ppermute(block, axes, pairs))
+
+
+        def spread(block, pairs=pairs):
+            other = lax.ppermute(block, axes, pairs)
+            return other, block + other
+
+        steps.append(spread)
 
     def double(block, distance):
         pairs = [(r, r ^ distance) for r in range(row_count)]
         other = lax.ppermute(block, "row", pairs)
         upper = row_index // distance % 2 == 1
-        return jnp.concatenate(
+        return other, jnp.concatenate(
             [jnp.where(upper, other, block), jnp.where(upper, block, other)], axis=1
         )
 
@@ -544,12 +549,17 @@
 
     arrived = []
 
+    coming = []
+
     def in_turn(block, *ready):
-        nonlocal latest, columns
-        before, latest = latest, lax.optimization_barrier((block, latest, columns, *ready))[0]
+        nonlocal latest, columns, coming
+        before = latest
+        block = lax.optimization_barrier((block, before, *coming, *ready))[0]
+        coming = []
         if steps and arrived:
-            columns = steps.pop(0)(after(columns, before))
-        latest = exchange(latest)
+            other, columns = steps.pop(0)(after(columns, before))
+            coming = [other]
+        latest = exchange(block)
         return latest
 
     second_round = parts[1][0][0]
@@ -568,10 +578,10 @@
                 pieces.append(jnp.zeros((spare, padded, LANES), jnp.int16))
             sent = pieces[0] if len(pieces) == 1 else jnp.concatenate(pieces, axis=0)
             arrived.append(in_turn(sent, *ready))
-            ready = [inverse] if k == 0 else []
+            ready = [inverse, row_samples] if k == 0 else []
         if k == panel_round:
             while steps:
-                columns = steps.pop(0)(columns)
+                _, columns = steps.pop(0)(columns)
             col_samples = columns
             gated = after(inverse, latest)
             panel, row_high, row_low = panel_rows(scalar(row_start), row_samples, pivot, gated)

time: 567 us -> 548 us (0.966)
  waiting for transfers between devices: 211 us -> 195 us
    ppermute x2, waiting for transfers between devices: 28.9 us -> 20.7 us  [spread(): other = lax.ppermute(block, axes, pairs)]
    all_gather x1, waiting for transfers between devices: 19.7 us -> 11.9 us  [on_device(): row_samples = lax.all_gather(own, 'col', axis=1, tiled=True)]
    unnamed x84 -> x76, local copies, waits for them, and re-layouts: 22 us -> 21 us
  transfers between devices with their start and end apart: 16 -> 16, of which waited for: 13 -> 13; matrix products, arithmetic and copies ran while one was open for 3% -> 3% of each run, Pallas kernels for 39% -> 40%
where the time goes in v6:
time: 548 us; the launch traced here: 546 us
  Pallas kernels  227 us (41%)
  waiting for transfers between devices  195 us (36%)
  starting transfers between devices  58.2 us (11%)
  local copies, waits for them, and re-layouts  33.8 us (6%)
  other arithmetic  17.6 us (3%)
  between operations  14.6 us (3%)
    all_to_all x12, waiting for transfers between devices, on_device(): lax.all_to_all(a, axes, split_axis=0, concat_axis=0, tiled=True)  162 us
    pallas_call x5, Pallas kernels, middle(): pl.pallas_call(lambda *refs: middle_kernel(sizes, padded, *refs), in_spec...  93.5 us
    pallas_call x3, Pallas kernels, source(): pl.pallas_call(lambda *refs: source_kernel(group, cells, depth, padded, p...  56.7 us
    all_to_all x12, starting transfers between devices, on_device(): lax.all_to_all(a, axes, split_axis=0, concat_axis=0, tiled=True)  49.6 us
    pallas_call x1, Pallas kernels, schur_block(): pl.pallas_call(schur_kernel, grid=(rows // row_tile, cols // col_tile), i...  34.5 us
    unnamed x76, local copies, waits for them, and re-layouts  21 us
    ppermute x2, waiting for transfers between devices, spread(): other = lax.ppermute(block, axes, pairs)  20.7 us
    pallas_call x2, Pallas kernels, target(): pl.pallas_call(lambda *refs: target_kernel(group, cells, depth, spans, *r...  17.3 us
  transfers between devices with their start and end apart: 16, of which 13 were waited for; matrix products, arithmetic and copies ran while one was open for 3% of the time, Pallas kernels for 40%

profile of v6, /device:TPU:1, one launch (start us, length us, event | category | flops | bytes accessed | tf_op | source)
XLA Modules:
  0.0 545.9 jit_solution(444430187601384166)
XLA Ops:
  27.7 10.3 %all-to-all-done = bf16[32,16,256]{2,1,0:T(8,128)(2,1)S(1)} async-done(((bf16[32,16,256]{2,1,0:T(8,128)(2,1)}), bf16[32,16,256]{2,1,0:T(8,128)(2,1)S(1)}, u32[]{:S(2)}, u32[]{:S(2)}) %all-to-all-start) | async-done | bytes 262176 | tf_op jit(solution)/shard_map/all_to_all | solution.py:456
  42.2 9.4 %all-to-all-done.1 = bf16[32,16,256]{2,1,0:T(8,128)(2,1)S(1)} async-done(((bf16[32,16,256]{2,1,0:T(8,128)(2,1)}), bf16[32,16,256]{2,1,0:T(8,128)(2,1)S(1)}, u32[]{:S(2)}, u32[]{:S(2)}) %all-to-all-start.1) | async-done | bytes 262176 | tf_op jit(solution)/shard_map/all_to_all | solution.py:456
  56.7 14.8 %source.3 = s16[32,208,128]{2,1,0:T(8,128)(2,1)} custom-call(bf16[16000,256]{1,0:T(8,128)(2,1)} %bitcast.48, bf16[16000,256]{1,0:T(8,128)(2,1)} %bitcast.44, bf16[128,256]{1,0:T(8,128)(2,1)S(1)} %get-tuple-element.64.pivot_a.refs_2_, bf16[128,256]{1,0:T(8,128)(2,1)S(1)} %get-tuple-element.63.pivot_b.refs_3_, f32[128,128]{1,0:T(8,128)S(1)} %lead.1.lead_inverse.refs_4_, ...), custom_call_target="tpu_custom_call" | custom-call | flops 30666665984 | bytes 16384000 | tf_op jit(solution)/shard_map/source/pallas_call | solution.py:107
  81.5 14.8 %source.4 = (s16[32,208,128]{2,1,0:T(8,128)(2,1)S(1)}, s16[16,208,128]{2,1,0:T(8,128)(2,1)S(1)}) custom-call(bf16[16000,256]{1,0:T(8,128)(2,1)} %bitcast.49, bf16[16000,256]{1,0:T(8,128)(2,1)} %bitcast.45, bf16[128,256]{1,0:T(8,128)(2,1)S(1)} %get-tuple-element.64.pivot_a.refs_2_, bf16[128,256]{1,0:T(8,128)(2,1)S(1)} %get-tuple-element.63.pivot_b.refs_3_, ...), custom_call_target="tpu_custom_call" | custom-call | flops 30666665984 | bytes 16384000 | tf_op jit(solution)/shard_map/source/pallas_call | solution.py:107
  98.4 11.9 %all-gather.2.cloned.1.call-done = bf16[2,2048,256]{2,1,0:T(8,128)(2,1)} async-done(((bf16[2,512,256]{2,1,0:T(8,128)(2,1)}), bf16[2,2048,256]{2,1,0:T(8,128)(2,1)}) %all-gather.2.cloned.1.call-update) | async-done | bytes 2097168 | tf_op jit(solution)/shard_map/all_gather | solution.py:466
  110.3 16.7 %all-to-all-done.2.refs_1_ = s16[32,208,128]{2,1,0:T(8,128)(2,1)S(1)} async-done(((s16[32,208,128]{2,1,0:T(8,128)(2,1)}), s16[32,208,128]{2,1,0:T(8,128)(2,1)S(1)}, u32[]{:S(2)}, u32[]{:S(2)}) %all-to-all-start.2) | async-done | bytes 1703968 | tf_op jit(solution)/shard_map/all_to_all | solution.py:456
  137.4 17.9 %middle.6 = s16[32,208,128]{2,1,0:T(8,128)(2,1)S(1)} custom-call(s32[1]{0:T(128)} %bitcast.14.refs_0_, s16[32,208,128]{2,1,0:T(8,128)(2,1)S(1)} %all-to-all-done.2.refs_1_, bf16[80,240]{1,0:T(8,128)(2,1)S(1)} %copy-done.22, bf16[80,240]{1,0:T(8,128)(2,1)S(1)} %copy-done.22), custom_call_target="tpu_custom_call" | custom-call | flops 18400000000 | bytes 3407872 | tf_op jit(solution)/shard_map/middle/pallas_call | solution.py:195
  156.5 15.5 %collective-permute-done = bf16[2,2048,256]{2,1,0:T(8,128)(2,1)} collective-permute-done((bf16[2,2048,256]{2,1,0:T(8,128)(2,1)}, bf16[2,2048,256]{2,1,0:T(8,128)(2,1)}, u32[]{:S(2)}, u32[]{:S(2)}) %collective-permute-start) | collective-permute-done | bytes 2097184 | tf_op jit(solution)/shard_map/ppermute | solution.py:535
  186.6 27.0 %source.5 = (s16[16,208,128]{2,1,0:T(8,128)(2,1)S(1)}, s16[32,208,128]{2,1,0:T(8,128)(2,1)}, s16[32,208,128]{2,1,0:T(8,128)(2,1)}) custom-call(bf16[16000,256]{1,0:T(8,128)(2,1)} %bitcast.50, bf16[16000,256]{1,0:T(8,128)(2,1)} %bitcast.46, bf16[256,256]{1,0:T(8,128)(2,1)S(1)} %bitcast.35, bf16[256,256]{1,0:T(8,128)(2,1)S(1)} %bitcast.31, ...), custom_call_target="tpu_custom_call" | custom-call | flops 30666665984 | bytes 16384000 | tf_op jit(solution)/shard_map/source/pallas_call | solution.py:107
  220.1 7.2 %all-to-all-start.5 = ((s16[32,208,128]{2,1,0:T(8,128)(2,1)}), s16[32,208,128]{2,1,0:T(8,128)(2,1)}, u32[]{:S(2)}, u32[]{:S(2)}) async-start(s16[32,208,128]{2,1,0:T(8,128)(2,1)} %pad_add_fusion), calls=%async_computation.5 | async-start | bytes 3407872 | tf_op jit(solution)/shard_map/all_to_all | solution.py:456
  232.7 19.1 %middle.5 = s16[32,208,128]{2,1,0:T(8,128)(2,1)} custom-call(s32[1]{0:T(128)} %bitcast.13.refs_0_, s16[32,208,128]{2,1,0:T(8,128)(2,1)S(1)} %all-to-all-done.3.refs_1_, bf16[80,240]{1,0:T(8,128)(2,1)S(1)} %copy-done.24, bf16[80,240]{1,0:T(8,128)(2,1)S(1)} %copy-done.24), custom_call_target="tpu_custom_call" | custom-call | flops 18400000000 | bytes 3407872 | tf_op jit(solution)/shard_map/middle/pallas_call | solution.py:195
  251.8 15.7 %all-to-all-done.5.refs_1_ = s16[32,208,128]{2,1,0:T(8,128)(2,1)} async-done(((s16[32,208,128]{2,1,0:T(8,128)(2,1)}), s16[32,208,128]{2,1,0:T(8,128)(2,1)}, u32[]{:S(2)}, u32[]{:S(2)}) %all-to-all-start.5) | async-done | bytes 1703968 | tf_op jit(solution)/shard_map/all_to_all | solution.py:456
  282.0 9.1 %panel.3 = (f32[4096,256]{1,0:T(8,128)}, bf16[4096,256]{1,0:T(8,128)(2,1)S(1)}, bf16[4096,256]{1,0:T(8,128)(2,1)S(1)}) custom-call(s32[1]{0:T(128)} %bitcast.1.first_row, bf16[4096,256]{1,0:T(8,128)(2,1)S(1)} %get-tuple-element.58.left_a.col_a, bf16[4096,256]{1,0:T(8,128)(2,1)S(1)} %get-tuple-element.57.left_b.col_b, bf16[256,256]{1,0:T(8,128)(2,1)S(1)} %bitcast.37, ...), custom_call_target="tpu_custom_call" | custom-call | flops 11776000000 | bytes 12582912 | tf_op jit(solution)/shard_map/panel/pallas_call | solution.py:281
  293.7 17.0 %all-to-all-done.6.refs_1_ = s16[32,208,128]{2,1,0:T(8,128)(2,1)} async-done(((s16[32,208,128]{2,1,0:T(8,128)(2,1)}), s16[32,208,128]{2,1,0:T(8,128)(2,1)}, u32[]{:S(2)}, u32[]{:S(2)}) %all-to-all-start.6) | async-done | bytes 1703968 | tf_op jit(solution)/shard_map/all_to_all | solution.py:456
  314.1 19.3 %middle.7 = s16[32,208,128]{2,1,0:T(8,128)(2,1)S(1)} custom-call(s32[1]{0:T(128)} %bitcast.19.refs_0_, s16[32,208,128]{2,1,0:T(8,128)(2,1)} %all-to-all-done.5.refs_1_, bf16[80,240]{1,0:T(8,128)(2,1)S(1)} %copy-done.25, bf16[80,240]{1,0:T(8,128)(2,1)S(1)} %copy-done.25), custom_call_target="tpu_custom_call" | custom-call | flops 18400000000 | bytes 3407872 | tf_op jit(solution)/shard_map/middle/pallas_call | solution.py:195
  334.7 19.4 %all-to-all-done.7.refs_1_ = s16[32,208,128]{2,1,0:T(8,128)(2,1)S(1)} async-done(((s16[32,208,128]{2,1,0:T(8,128)(2,1)}), s16[32,208,128]{2,1,0:T(8,128)(2,1)S(1)}, u32[]{:S(2)}, u32[]{:S(2)}) %all-to-all-start.7) | async-done | bytes 1703968 | tf_op jit(solution)/shard_map/all_to_all | solution.py:456
  361.0 34.5 %schur.1 = f32[2048,4096]{1,0:T(8,128)} custom-call(s32[2]{0:T(128)S(1)} %pad_add_fusion.1.offsets, bf16[2048,256]{1,0:T(8,128)(2,1)S(1)} %copy-done.16, bf16[2048,256]{1,0:T(8,128)(2,1)S(1)} %copy-done.14, bf16[2048,256]{1,0:T(8,128)(2,1)S(1)} %copy-done.29, bf16[2048,256]{1,0:T(8,128)(2,1)} %copy-done.30, bf16[4096,256]{1,0:T(8,128)(2,1)} %copy-done.1, ...), custom_call_target="tpu_custom_call" | custom-call | flops 40195411968 | bytes 33554432 | tf_op jit(solution)/shard_map/schur/pallas_call | solution.py:329
  401.4 17.9 %middle.8 = s16[32,208,128]{2,1,0:T(8,128)(2,1)S(1)} custom-call(s32[1]{0:T(128)} %bitcast.20.refs_0_, s16[32,208,128]{2,1,0:T(8,128)(2,1)S(1)} %all-to-all-done.7.refs_1_, bf16[80,240]{1,0:T(8,128)(2,1)S(1)} %copy-done.25, bf16[80,240]{1,0:T(8,128)(2,1)S(1)} %copy-done.25), custom_call_target="tpu_custom_call" | custom-call | flops 18400000000 | bytes 3407872 | tf_op jit(solution)/shard_map/middle/pallas_call | solution.py:195
  420.5 21.0 %all-to-all-done.9.refs_1_ = s16[32,208,128]{2,1,0:T(8,128)(2,1)} async-done(((s16[32,208,128]{2,1,0:T(8,128)(2,1)}), s16[32,208,128]{2,1,0:T(8,128)(2,1)}, u32[]{:S(2)}, u32[]{:S(2)}) %all-to-all-start.9) | async-done | bytes 1703968 | tf_op jit(solution)/shard_map/all_to_all | solution.py:456
  444.7 19.3 %middle.9 = s16[32,208,128]{2,1,0:T(8,128)(2,1)S(1)} custom-call(s32[1]{0:T(128)} %bitcast.21.refs_0_, s16[32,208,128]{2,1,0:T(8,128)(2,1)} %all-to-all-done.9.refs_1_, bf16[80,240]{1,0:T(8,128)(2,1)S(1)} %copy-done.25, bf16[80,240]{1,0:T(8,128)(2,1)S(1)} %copy-done.25), custom_call_target="tpu_custom_call" | custom-call | flops 18400000000 | bytes 3407872 | tf_op jit(solution)/shard_map/middle/pallas_call | solution.py:195
  465.3 19.5 %all-to-all-done.10.refs_1_ = s16[32,208,128]{2,1,0:T(8,128)(2,1)S(1)} async-done(((s16[32,208,128]{2,1,0:T(8,128)(2,1)}), s16[32,208,128]{2,1,0:T(8,128)(2,1)S(1)}, u32[]{:S(2)}, u32[]{:S(2)}) %all-to-all-start.10) | async-done | bytes 1703968 | tf_op jit(solution)/shard_map/all_to_all | solution.py:456
  489.2 9.0 %target.2.refs_4_ = f32[16000,256]{1,0:T(8,128)} custom-call(s16[32,208,128]{2,1,0:T(8,128)(2,1)S(1)} %copy-done.3, s16[32,208,128]{2,1,0:T(8,128)(2,1)} %all-to-all-done.6.refs_1_, s16[32,208,128]{2,1,0:T(8,128)(2,1)} %copy-done.4, bf16[80,240]{1,0:T(8,128)(2,1)S(1)} %copy-done.25), custom_call_target="tpu_custom_call" | custom-call | flops 15333332992 | bytes 12288000 | tf_op jit(solution)/shard_map/target/pallas_call | solution.py:246
  498.2 31.1 %all-to-all-done.11.refs_2_ = s16[32,208,128]{2,1,0:T(8,128)(2,1)} async-done(((s16[32,208,128]{2,1,0:T(8,128)(2,1)}), s16[32,208,128]{2,1,0:T(8,128)(2,1)}, u32[]{:S(2)}, u32[]{:S(2)}) %all-to-all-start.11) | async-done | bytes 1703968 | tf_op jit(solution)/shard_map/all_to_all | solution.py:456
  530.8 8.3 %target.3 = f32[16000,256]{1,0:T(8,128)} custom-call(s16[32,208,128]{2,1,0:T(8,128)(2,1)S(1)} %copy-done.5, s16[32,208,128]{2,1,0:T(8,128)(2,1)S(1)} %copy-done.8, s16[32,208,128]{2,1,0:T(8,128)(2,1)} %all-to-all-done.11.refs_2_, bf16[80,240]{1,0:T(8,128)(2,1)S(1)} %copy-done.25, f32[16000,256]{1,0:T(8,128)} %target.2.refs_4_), custom_call_target="tpu_custom_call", output_to_operand_aliasing={{}: (4, {})} | custom-call | flops 15333332992 | bytes 12288000 | tf_op jit(solution)/shard_map/target/pallas_call | solution.py:246
  (118 shorter events, 125.5 us)
Async XLA Ops:
  20.5 17.4 %all-to-all-start = ((bf16[32,16,256]{2,1,0:T(8,128)(2,1)}), bf16[32,16,256]{2,1,0:T(8,128)(2,1)S(1)}, u32[]{:S(2)}, u32[]{:S(2)}) async-start(bf16[32,16,256]{2,1,0:T(8,128)(2,1)} %bitcast.6), calls=%async_computation | async-start | bytes 524288 | tf_op jit(solution)/shard_map/all_to_all | solution.py:456
  38.7 12.9 %all-to-all-start.1 = ((bf16[32,16,256]{2,1,0:T(8,128)(2,1)}), bf16[32,16,256]{2,1,0:T(8,128)(2,1)S(1)}, u32[]{:S(2)}, u32[]{:S(2)}) async-start(bf16[32,16,256]{2,1,0:T(8,128)(2,1)} %broadcast_in_dim.18), calls=%async_computation.1 | async-start | bytes 524288 | tf_op jit(solution)/shard_map/all_to_all | solution.py:456
  41.3 69.1 %all-gather.2.cloned.1.call-start = ((), (), s32[]{:S(2)}) async-start(), calls=%async_computation.12 | async-start | bytes 2621440 | tf_op jit(solution)/shard_map/all_gather | solution.py:466
  71.5 55.5 %all-to-all-start.2 = ((s16[32,208,128]{2,1,0:T(8,128)(2,1)}), s16[32,208,128]{2,1,0:T(8,128)(2,1)S(1)}, u32[]{:S(2)}, u32[]{:S(2)}) async-start(s16[32,208,128]{2,1,0:T(8,128)(2,1)} %source.3), calls=%async_computation.2 | async-start | bytes 3407872 | tf_op jit(solution)/shard_map/all_to_all | solution.py:456
  127.0 45.0 %all-to-all-start.3 = ((s16[32,208,128]{2,1,0:T(8,128)(2,1)}), s16[32,208,128]{2,1,0:T(8,128)(2,1)S(1)}, u32[]{:S(2)}, u32[]{:S(2)}) async-start(s16[32,208,128]{2,1,0:T(8,128)(2,1)} %copy-done.6), calls=%async_computation.3 | async-start | bytes 3407872 | tf_op jit(solution)/shard_map/all_to_all | solution.py:456
  133.5 38.5 %collective-permute-start = (bf16[2,2048,256]{2,1,0:T(8,128)(2,1)}, bf16[2,2048,256]{2,1,0:T(8,128)(2,1)}, u32[]{:S(2)}, u32[]{:S(2)}) collective-permute-start(bf16[2,2048,256]{2,1,0:T(8,128)(2,1)} %broadcast_select_fusion.2), channel_id=1, source_target_pairs={{0,8},{4,20},{9,1},{13,29},{18,26},{22,6},{27,19},{31,15}} | collective-permute-start | bytes 6291464 | tf_op jit(solution)/shard_map/ppermute | solution.py:535
  172.0 48.1 %all-to-all-start.4 = ((s16[32,208,128]{2,1,0:T(8,128)(2,1)}), s16[32,208,128]{2,1,0:T(8,128)(2,1)S(1)}, u32[]{:S(2)}, u32[]{:S(2)}) async-start(s16[32,208,128]{2,1,0:T(8,128)(2,1)} %copy-done.10), calls=%async_computation.4 | async-start | bytes 3407872 | tf_op jit(solution)/shard_map/all_to_all | solution.py:456
  181.6 32.0 %copy-start.36 = (bf16[2,2048,256]{2,1,0:T(8,128)(2,1)}, bf16[2,2048,256]{2,1,0:T(8,128)(2,1)S(1)}, u32[]{:S(2)}) copy-start(bf16[2,2048,256]{2,1,0:T(8,128)(2,1)S(1)} %add.65) | copy-start | bytes 6291460
  181.6 32.0 %copy-start.18 = (s16[16,208,128]{2,1,0:T(8,128)(2,1)S(1)}, s16[16,208,128]{2,1,0:T(8,128)(2,1)}, u32[]{:S(2)}) copy-start(s16[16,208,128]{2,1,0:T(8,128)(2,1)} %copy-done.17) | copy-start | bytes 2555908
  181.7 38.5 %collective-permute-start.1 = (bf16[2,2048,256]{2,1,0:T(8,128)(2,1)S(1)}, bf16[2,2048,256]{2,1,0:T(8,128)(2,1)}, u32[]{:S(2)}, u32[]{:S(2)}) collective-permute-start(bf16[2,2048,256]{2,1,0:T(8,128)(2,1)S(1)} %add.65), channel_id=1, source_target_pairs={{0,16},{8,24},{4,12},{20,28},{9,25},{1,17},{13,5},{29,21},{18,2},{... | collective-permute-start | bytes 6291464 | tf_op jit(solution)/shard_map/ppermute | solution.py:535
  220.1 11.3 %copy-start.2 = (s16[32,208,128]{2,1,0:T(8,128)(2,1)}, s16[32,208,128]{2,1,0:T(8,128)(2,1)S(1)}, u32[]{:S(2)}) copy-start(s16[32,208,128]{2,1,0:T(8,128)(2,1)S(1)} %all-to-all-done.4.refs_0_) | copy-start | bytes 5111812
  220.1 47.3 %all-to-all-start.5 = ((s16[32,208,128]{2,1,0:T(8,128)(2,1)}), s16[32,208,128]{2,1,0:T(8,128)(2,1)}, u32[]{:S(2)}, u32[]{:S(2)}) async-start(s16[32,208,128]{2,1,0:T(8,128)(2,1)} %pad_add_fusion), calls=%async_computation.5 | async-start | bytes 3407872 | tf_op jit(solution)/shard_map/all_to_all | solution.py:456
  231.4 20.4 %collective-permute-start.2 = (bf16[2,2048,256]{2,1,0:T(8,128)(2,1)}, bf16[2,2048,256]{2,1,0:T(8,128)(2,1)}, u32[]{:S(2)}, u32[]{:S(2)}) collective-permute-start(bf16[2,2048,256]{2,1,0:T(8,128)(2,1)} %add.66), channel_id=1, source_target_pairs={{0,4},{4,0},{8,12},{12,8},{16,20},{20,16},{24,28},{28,24},{1,5},{5... | collective-permute-start | bytes 6291464 | tf_op jit(solution)/shard_map/ppermute | solution.py:542
  251.8 18.9 %copy-start.37 = (bf16[2,2048,256]{2,1,0:T(8,128)(2,1)S(1)}, bf16[2,2048,256]{2,1,0:T(8,128)(2,1)}, u32[]{:S(2)}) copy-start(bf16[2,2048,256]{2,1,0:T(8,128)(2,1)} %all-gather.2.cloned.1.call-done) | copy-start | bytes 6291460
  267.4 43.3 %all-to-all-start.6 = ((s16[32,208,128]{2,1,0:T(8,128)(2,1)}), s16[32,208,128]{2,1,0:T(8,128)(2,1)}, u32[]{:S(2)}, u32[]{:S(2)}) async-start(s16[32,208,128]{2,1,0:T(8,128)(2,1)} %middle.5), calls=%async_computation.6 | async-start | bytes 3407872 | tf_op jit(solution)/shard_map/all_to_all | solution.py:456
  293.7 20.4 %copy-start.25 = (bf16[80,240]{1,0:T(8,128)(2,1)S(1)}, bf16[80,240]{1,0:T(8,128)(2,1)}, u32[]{:S(2)}) copy-start(bf16[80,240]{1,0:T(8,128)(2,1)} %constant.131.clone.refs_5_.refs_2_.refs_3_) | copy-start | bytes 115204
  310.8 43.3 %all-to-all-start.7 = ((s16[32,208,128]{2,1,0:T(8,128)(2,1)}), s16[32,208,128]{2,1,0:T(8,128)(2,1)S(1)}, u32[]{:S(2)}, u32[]{:S(2)}) async-start(s16[32,208,128]{2,1,0:T(8,128)(2,1)} %get-tuple-element.47), calls=%async_computation.7 | async-start | bytes 3407872 | tf_op jit(solution)/shard_map/all_to_all | solution.py:456
  354.1 43.2 %all-to-all-start.8 = ((s16[32,208,128]{2,1,0:T(8,128)(2,1)}), s16[32,208,128]{2,1,0:T(8,128)(2,1)S(1)}, u32[]{:S(2)}, u32[]{:S(2)}) async-start(s16[32,208,128]{2,1,0:T(8,128)(2,1)} %copy-done.11), calls=%async_computation.8 | async-start | bytes 3407872 | tf_op jit(solution)/shard_map/all_to_all | solution.py:456
  397.4 21.9 %copy-start.4 = (s16[32,208,128]{2,1,0:T(8,128)(2,1)}, s16[32,208,128]{2,1,0:T(8,128)(2,1)S(1)}, u32[]{:S(2)}) copy-start(s16[32,208,128]{2,1,0:T(8,128)(2,1)S(1)} %all-to-all-done.8.refs_2_.refs_0_) | copy-start | bytes 5111812
  397.4 44.2 %all-to-all-start.9 = ((s16[32,208,128]{2,1,0:T(8,128)(2,1)}), s16[32,208,128]{2,1,0:T(8,128)(2,1)}, u32[]{:S(2)}, u32[]{:S(2)}) async-start(s16[32,208,128]{2,1,0:T(8,128)(2,1)} %get-tuple-element.54), calls=%async_computation.9 | async-start | bytes 3407872 | tf_op jit(solution)/shard_map/all_to_all | solution.py:456
  441.5 43.2 %all-to-all-start.10 = ((s16[32,208,128]{2,1,0:T(8,128)(2,1)}), s16[32,208,128]{2,1,0:T(8,128)(2,1)S(1)}, u32[]{:S(2)}, u32[]{:S(2)}) async-start(s16[32,208,128]{2,1,0:T(8,128)(2,1)} %copy-done.9), calls=%async_computation.10 | async-start | bytes 3407872 | tf_op jit(solution)/shard_map/all_to_all | solution.py:456
  465.3 23.9 %copy-start.3 = (s16[32,208,128]{2,1,0:T(8,128)(2,1)S(1)}, s16[32,208,128]{2,1,0:T(8,128)(2,1)}, u32[]{:S(2)}) copy-start(s16[32,208,128]{2,1,0:T(8,128)(2,1)} %copy-done.2) | copy-start | bytes 5111812
  486.0 43.3 %all-to-all-start.11 = ((s16[32,208,128]{2,1,0:T(8,128)(2,1)}), s16[32,208,128]{2,1,0:T(8,128)(2,1)}, u32[]{:S(2)}, u32[]{:S(2)}) async-start(s16[32,208,128]{2,1,0:T(8,128)(2,1)} %copy-done.12), calls=%async_computation.11 | async-start | bytes 3407872 | tf_op jit(solution)/shard_map/all_to_all | solution.py:456
  489.2 40.1 %copy-start.5 = (s16[32,208,128]{2,1,0:T(8,128)(2,1)S(1)}, s16[32,208,128]{2,1,0:T(8,128)(2,1)}, u32[]{:S(2)}) copy-start(s16[32,208,128]{2,1,0:T(8,128)(2,1)} %copy-done.4) | copy-start | bytes 5111812
  (30 other events, 80.9 us)
Sparse Core Ops, SparseCore 0:
  44.3 66.0 all-gather.1

commit v7 on v6

--- a/solution.py
+++ b/solution.py
@@ -272,7 +272,7 @@
 
 
 def panel_rows(first_row, left, pivot, inverse):
-    _, rows, orbitals = left.shape
+    rows, orbitals = left[0].shape
     pivots = pivot.shape[1]
     tile = math.gcd(rows, 512)
     whole = lambda shape: pl.BlockSpec(shape, lambda i: (0,) * len(shape))
@@ -458,6 +458,7 @@
     held = min(owned, PB)
     piece_rows = 2 * PB // devices
     offered = jnp.concatenate([own[:, :held]] * (PB // held), axis=1)
+    own, offered = lax.optimization_barrier((own, offered))
     offered = exchange(offered.reshape(devices, piece_rows, orbitals))
     owner = me * piece_rows % PB // owned
     piece = lax.dynamic_index_in_dim(offered, owner, axis=0, keepdims=True)
@@ -511,12 +512,14 @@
     col_start = col_index * row_count * owned
     scalar = lambda *v: jnp.stack([jnp.asarray(a, jnp.int32) for a in v])
 
-    latest = outgoing[0][0]
+    latest = previous = outgoing[0][0]
     members = row_count // col_count
     bits = [1 << b for b in range(row_count.bit_length() - 1)]
     inner = [b for b in bits if b < members]
     outer = [b for b in bits if b >= members]
-    columns = jnp.where(row_index // members == col_index, row_samples, 0)
+    columns = [
+        jnp.where(row_index // members == col_index, row_samples[i], 0) for i in range(2)
+    ]
     steps = []
     for t in range(len(outer)):
         pairs = []
@@ -535,39 +538,45 @@
             other = lax.ppermute(block, axes, pairs)
             return other, block + other
 
-        steps.append(spread)
+        steps += [((0, 1), spread)] if t == 0 else [((0,), spread), ((1,), spread)]
 
     def double(block, distance):
         pairs = [(r, r ^ distance) for r in range(row_count)]
         other = lax.ppermute(block, "row", pairs)
         upper = row_index // distance % 2 == 1
         return other, jnp.concatenate(
-            [jnp.where(upper, other, block), jnp.where(upper, block, other)], axis=1
+            [jnp.where(upper, other, block), jnp.where(upper, block, other)], axis=0
         )
 
-    steps += [lambda block, distance=d: double(block, distance) for d in inner]
+    steps += [((0, 1), lambda block, distance=d: double(block, distance)) for d in inner]
 
     arrived = []
 
     coming = []
 
+    def step_on(*gate):
+        which, move = steps.pop(0)
+        for i in which:
+            block = after(columns[i], gate) if gate else columns[i]
+            other, columns[i] = move(block)
+            coming.append(other)
+
     def in_turn(block, *ready):
-        nonlocal latest, columns, coming
-        before = latest
-        block = lax.optimization_barrier((block, before, *coming, *ready))[0]
-        coming = []
+        nonlocal latest, previous
+        previous = latest
+        block = lax.optimization_barrier((block, previous, *coming, *ready))[0]
+        coming.clear()
         if steps and arrived:
-            other, columns = steps.pop(0)(after(columns, before))
-            coming = [other]
+            step_on(previous)
         latest = exchange(block)
         return latest
 
     second_round = parts[1][0][0]
-    panel_round = max(min(2, rounds - 1), second_round)
-    schur_round = max(min(3, rounds - 1), panel_round)
+    panel_round = max(min(3, rounds - 1), second_round, 1)
     ready = []
     returned = []
     for k in range(rounds + 1):
+        updated = []
         if k == second_round:
             gated = after(inverse, latest if k < 2 else arrived[k - 1])
             make(1, parts[1], gated)
@@ -578,29 +587,35 @@
                 pieces.append(jnp.zeros((spare, padded, LANES), jnp.int16))
             sent = pieces[0] if len(pieces) == 1 else jnp.concatenate(pieces, axis=0)
             arrived.append(in_turn(sent, *ready))
-            ready = [inverse, row_samples] if k == 0 else []
+            ready = []
+        if k == 0:
+            updated += [inverse, row_samples]
+        if k == panel_round - 1:
+            panel, row_high, row_low = panel_rows(
+                scalar(row_start), row_samples, pivot, after(inverse, latest)
+            )
+            updated += [row_high]
         if k == panel_round:
             while steps:
-                _, columns = steps.pop(0)(columns)
-            col_samples = columns
-            gated = after(inverse, latest)
-            panel, row_high, row_low = panel_rows(scalar(row_start), row_samples, pivot, gated)
-            _, col_high, col_low = panel_rows(scalar(col_start), col_samples, pivot, gated)
-            ready += [row_high, col_high]
-        if k == schur_round:
+                step_on()
+            _, col_high, col_low = panel_rows(
+                scalar(col_start), columns, pivot, after(inverse, previous)
+            )
+            ready += [col_high]
             schur = schur_block(
                 after(scalar(row_start, col_start), latest),
                 (row_samples[0], row_samples[1], row_high, row_low),
-                (col_samples[0], col_samples[1], col_high, col_low),
+                (columns[0], columns[1], col_high, col_low),
             )
-            ready += [schur]
+            updated += [schur]
         if k > 0:
             z_index = ((k - 1) * devices + me) % depth
             z_freq = jnp.minimum(z_index, depth - z_index).astype(jnp.int32).reshape(1)
             back = middle(
                 z_freq, arrived[k - 1], x_table, y_table, grid_x, grid_y, line_count
             )
-            returned.append(in_turn(back))
+            returned.append(in_turn(back, *ready))
+        ready = updated
 
     potential = None
     for h in range(halves):

time: 548 us -> 543 us (level)
  waiting for transfers between devices: 195 us -> 188 us
    ppermute x2 -> x4, starting transfers between devices: 7.99 us -> 14.4 us  [spread(): other = lax.ppermute(block, axes, pairs)]
    ppermute x2 -> x4, waiting for transfers between devices: 20.7 us -> 15.5 us  [spread(): other = lax.ppermute(block, axes, pairs)]
    unnamed x76 -> x106, local copies, waits for them, and re-layouts: 21 us -> 22.8 us
  transfers between devices with their start and end apart: 16 -> 19, of which waited for: 13 -> 15; matrix products, arithmetic and copies ran while one was open for 3% -> 2% of each run, Pallas kernels for 40% -> 40%
where the time goes in v7:
time: 543 us; the launch traced here: 541 us
  Pallas kernels  227 us (42%)
  waiting for transfers between devices  188 us (35%)
  starting transfers between devices  60.8 us (11%)
  local copies, waits for them, and re-layouts  35.6 us (7%)
  other arithmetic  14.9 us (3%)
  between operations  14.8 us (3%)
    all_to_all x12, waiting for transfers between devices, on_device(): lax.all_to_all(a, axes, split_axis=0, concat_axis=0, tiled=True)  160 us
    pallas_call x5, Pallas kernels, middle(): pl.pallas_call(lambda *refs: middle_kernel(sizes, padded, *refs), in_spec...  93.6 us
    pallas_call x3, Pallas kernels, source(): pl.pallas_call(lambda *refs: source_kernel(group, cells, depth, padded, p...  56.6 us
    all_to_all x12, starting transfers between devices, on_device(): lax.all_to_all(a, axes, split_axis=0, concat_axis=0, tiled=True)  45.8 us
    pallas_call x1, Pallas kernels, schur_block(): pl.pallas_call(schur_kernel, grid=(rows // row_tile, cols // col_tile), i...  34.5 us
    unnamed x106, local copies, waits for them, and re-layouts  22.8 us
    pallas_call x2, Pallas kernels, target(): pl.pallas_call(lambda *refs: target_kernel(group, cells, depth, spans, *r...  17.2 us
    ppermute x4, waiting for transfers between devices, spread(): other = lax.ppermute(block, axes, pairs)  15.5 us
  transfers between devices with their start and end apart: 19, of which 15 were waited for; matrix products, arithmetic and copies ran while one was open for 2% of the time, Pallas kernels for 40%

profile of v7, /device:TPU:1, one launch (start us, length us, event | category | flops | bytes accessed | tf_op | source)
XLA Modules:
  0.0 541.0 jit_solution(15524918429400954283)
XLA Ops:
  21.4 7.1 %all-to-all-start = ((bf16[32,16,256]{2,1,0:T(8,128)(2,1)}), bf16[32,16,256]{2,1,0:T(8,128)(2,1)S(1)}, u32[]{:S(2)}, u32[]{:S(2)}) async-start(bf16[32,16,256]{2,1,0:T(8,128)(2,1)} %bitcast.6), calls=%async_computation | async-start | bytes 524288 | tf_op jit(solution)/shard_map/all_to_all | solution.py:456
  28.5 10.3 %all-to-all-done = bf16[32,16,256]{2,1,0:T(8,128)(2,1)S(1)} async-done(((bf16[32,16,256]{2,1,0:T(8,128)(2,1)}), bf16[32,16,256]{2,1,0:T(8,128)(2,1)S(1)}, u32[]{:S(2)}, u32[]{:S(2)}) %all-to-all-start) | async-done | bytes 262176 | tf_op jit(solution)/shard_map/all_to_all | solution.py:456
  42.9 9.6 %all-to-all-done.1 = bf16[32,16,256]{2,1,0:T(8,128)(2,1)S(1)} async-done(((bf16[32,16,256]{2,1,0:T(8,128)(2,1)}), bf16[32,16,256]{2,1,0:T(8,128)(2,1)S(1)}, u32[]{:S(2)}, u32[]{:S(2)}) %all-to-all-start.1) | async-done | bytes 262176 | tf_op jit(solution)/shard_map/all_to_all | solution.py:456
  57.5 14.8 %source.3 = s16[32,208,128]{2,1,0:T(8,128)(2,1)} custom-call(bf16[16000,256]{1,0:T(8,128)(2,1)} %bitcast.48, bf16[16000,256]{1,0:T(8,128)(2,1)} %bitcast.44, bf16[128,256]{1,0:T(8,128)(2,1)S(1)} %get-tuple-element.78.pivot_a.refs_2_, bf16[128,256]{1,0:T(8,128)(2,1)S(1)} %get-tuple-element.77.pivot_b.refs_3_, f32[128,128]{1,0:T(8,128)S(1)} %lead.1.lead_inverse.refs_4_, ...), custom_call_target="tpu_custom_call" | custom-call | flops 30666665984 | bytes 16384000 | tf_op jit(solution)/shard_map/source/pallas_call | solution.py:107
  82.3 14.8 %source.4 = (s16[32,208,128]{2,1,0:T(8,128)(2,1)S(1)}, s16[16,208,128]{2,1,0:T(8,128)(2,1)S(1)}) custom-call(bf16[16000,256]{1,0:T(8,128)(2,1)} %bitcast.49, bf16[16000,256]{1,0:T(8,128)(2,1)} %bitcast.45, bf16[128,256]{1,0:T(8,128)(2,1)S(1)} %get-tuple-element.78.pivot_a.refs_2_, bf16[128,256]{1,0:T(8,128)(2,1)S(1)} %get-tuple-element.77.pivot_b.refs_3_, ...), custom_call_target="tpu_custom_call" | custom-call | flops 30666665984 | bytes 16384000 | tf_op jit(solution)/shard_map/source/pallas_call | solution.py:107
  99.3 11.9 %all-gather.2.cloned.1.call-done = bf16[2,2048,256]{2,1,0:T(8,128)(2,1)} async-done(((bf16[2,512,256]{2,1,0:T(8,128)(2,1)}), bf16[2,2048,256]{2,1,0:T(8,128)(2,1)}) %all-gather.2.cloned.1.call-update) | async-done | bytes 2097168 | tf_op jit(solution)/shard_map/all_gather | solution.py:467
  111.1 16.7 %all-to-all-done.2.refs_1_ = s16[32,208,128]{2,1,0:T(8,128)(2,1)S(1)} async-done(((s16[32,208,128]{2,1,0:T(8,128)(2,1)}), s16[32,208,128]{2,1,0:T(8,128)(2,1)S(1)}, u32[]{:S(2)}, u32[]{:S(2)}) %all-to-all-start.2) | async-done | bytes 1703968 | tf_op jit(solution)/shard_map/all_to_all | solution.py:456
  138.7 17.9 %middle.6 = s16[32,208,128]{2,1,0:T(8,128)(2,1)S(1)} custom-call(s32[1]{0:T(128)} %bitcast.14.refs_0_, s16[32,208,128]{2,1,0:T(8,128)(2,1)S(1)} %all-to-all-done.2.refs_1_, bf16[80,240]{1,0:T(8,128)(2,1)S(1)} %copy-done.23, bf16[80,240]{1,0:T(8,128)(2,1)S(1)} %copy-done.23), custom_call_target="tpu_custom_call" | custom-call | flops 18400000000 | bytes 3407872 | tf_op jit(solution)/shard_map/middle/pallas_call | solution.py:195
  160.3 12.4 %collective-permute-done.1 = bf16[2048,256]{1,0:T(8,128)(2,1)} collective-permute-done((bf16[2048,256]{1,0:T(8,128)(2,1)S(1)}, bf16[2048,256]{1,0:T(8,128)(2,1)}, u32[]{:S(2)}, u32[]{:S(2)}) %collective-permute-start.1) | collective-permute-done | bytes 1048608 | tf_op jit(solution)/shard_map/ppermute | solution.py:538
  172.7 6.8 %all-to-all-start.4 = ((s16[32,208,128]{2,1,0:T(8,128)(2,1)}), s16[32,208,128]{2,1,0:T(8,128)(2,1)S(1)}, u32[]{:S(2)}, u32[]{:S(2)}) async-start(s16[32,208,128]{2,1,0:T(8,128)(2,1)} %copy-done.10), calls=%async_computation.4 | async-start | bytes 3407872 | tf_op jit(solution)/shard_map/all_to_all | solution.py:456
  185.9 27.0 %source.5 = (s16[16,208,128]{2,1,0:T(8,128)(2,1)S(1)}, s16[32,208,128]{2,1,0:T(8,128)(2,1)}, s16[32,208,128]{2,1,0:T(8,128)(2,1)}) custom-call(bf16[16000,256]{1,0:T(8,128)(2,1)} %bitcast.50, bf16[16000,256]{1,0:T(8,128)(2,1)} %bitcast.46, bf16[256,256]{1,0:T(8,128)(2,1)S(1)} %bitcast.35, bf16[256,256]{1,0:T(8,128)(2,1)S(1)} %bitcast.31, ...), custom_call_target="tpu_custom_call" | custom-call | flops 30666665984 | bytes 16384000 | tf_op jit(solution)/shard_map/source/pallas_call | solution.py:107
  229.0 19.1 %middle.5 = s16[32,208,128]{2,1,0:T(8,128)(2,1)} custom-call(s32[1]{0:T(128)} %bitcast.13.refs_0_, s16[32,208,128]{2,1,0:T(8,128)(2,1)S(1)} %all-to-all-done.3.refs_1_, bf16[80,240]{1,0:T(8,128)(2,1)S(1)} %copy-done.25, bf16[80,240]{1,0:T(8,128)(2,1)S(1)} %copy-done.25), custom_call_target="tpu_custom_call" | custom-call | flops 18400000000 | bytes 3407872 | tf_op jit(solution)/shard_map/middle/pallas_call | solution.py:195
  249.6 13.4 %all-to-all-done.5.refs_1_ = s16[32,208,128]{2,1,0:T(8,128)(2,1)} async-done(((s16[32,208,128]{2,1,0:T(8,128)(2,1)}), s16[32,208,128]{2,1,0:T(8,128)(2,1)}, u32[]{:S(2)}, u32[]{:S(2)}) %all-to-all-start.5) | async-done | bytes 1703968 | tf_op jit(solution)/shard_map/all_to_all | solution.py:456
  279.3 27.1 %all-to-all-done.6.refs_1_ = s16[32,208,128]{2,1,0:T(8,128)(2,1)S(1)} async-done(((s16[32,208,128]{2,1,0:T(8,128)(2,1)}), s16[32,208,128]{2,1,0:T(8,128)(2,1)S(1)}, u32[]{:S(2)}, u32[]{:S(2)}) %all-to-all-start.6) | async-done | bytes 1703968 | tf_op jit(solution)/shard_map/all_to_all | solution.py:456
  310.3 19.5 %middle.7 = s16[32,208,128]{2,1,0:T(8,128)(2,1)S(1)} custom-call(s32[1]{0:T(128)} %bitcast.17.refs_0_, s16[32,208,128]{2,1,0:T(8,128)(2,1)} %all-to-all-done.5.refs_1_, bf16[80,240]{1,0:T(8,128)(2,1)S(1)} %copy-done.26, bf16[80,240]{1,0:T(8,128)(2,1)S(1)} %copy-done.26), custom_call_target="tpu_custom_call" | custom-call | flops 18400000000 | bytes 3407872 | tf_op jit(solution)/shard_map/middle/pallas_call | solution.py:195
  333.5 9.1 %panel.3 = (f32[4096,256]{1,0:T(8,128)}, bf16[4096,256]{1,0:T(8,128)(2,1)S(1)}, bf16[4096,256]{1,0:T(8,128)(2,1)S(1)}) custom-call(s32[1]{0:T(128)} %bitcast.1.first_row, bf16[4096,256]{1,0:T(8,128)(2,1)S(1)} %pad_maximum_fusion.left_a.col_a, bf16[4096,256]{1,0:T(8,128)(2,1)S(1)} %pad_maximum_fusion.1.left_b.col_b, bf16[256,256]{1,0:T(8,128)(2,1)S(1)} %bitcast.37, ...), custom_call_target="tpu_custom_call" | custom-call | flops 11776000000 | bytes 12582912 | tf_op jit(solution)/shard_map/panel/pallas_call | solution.py:281
  356.5 34.5 %schur.1 = f32[2048,4096]{1,0:T(8,128)} custom-call(s32[2]{0:T(128)S(1)} %pad_add_fusion.1.offsets, bf16[2048,256]{1,0:T(8,128)(2,1)S(1)} %copy-done.16, bf16[2048,256]{1,0:T(8,128)(2,1)S(1)} %copy-done.14, bf16[2048,256]{1,0:T(8,128)(2,1)S(1)} %copy-done.31, bf16[2048,256]{1,0:T(8,128)(2,1)} %copy-done.32, bf16[4096,256]{1,0:T(8,128)(2,1)} %copy-done.1, ...), custom_call_target="tpu_custom_call" | custom-call | flops 40195411968 | bytes 33554432 | tf_op jit(solution)/shard_map/schur/pallas_call | solution.py:329
  396.9 17.9 %middle.8 = s16[32,208,128]{2,1,0:T(8,128)(2,1)S(1)} custom-call(s32[1]{0:T(128)} %bitcast.18.refs_0_, s16[32,208,128]{2,1,0:T(8,128)(2,1)S(1)} %all-to-all-done.7.refs_1_, bf16[80,240]{1,0:T(8,128)(2,1)S(1)} %copy-done.27, bf16[80,240]{1,0:T(8,128)(2,1)S(1)} %copy-done.27), custom_call_target="tpu_custom_call" | custom-call | flops 18400000000 | bytes 3407872 | tf_op jit(solution)/shard_map/middle/pallas_call | solution.py:195
  416.0 21.0 %all-to-all-done.9.refs_1_ = s16[32,208,128]{2,1,0:T(8,128)(2,1)} async-done(((s16[32,208,128]{2,1,0:T(8,128)(2,1)}), s16[32,208,128]{2,1,0:T(8,128)(2,1)}, u32[]{:S(2)}, u32[]{:S(2)}) %all-to-all-start.9) | async-done | bytes 1703968 | tf_op jit(solution)/shard_map/all_to_all | solution.py:456
  440.3 19.3 %middle.9 = s16[32,208,128]{2,1,0:T(8,128)(2,1)S(1)} custom-call(s32[1]{0:T(128)} %bitcast.19.refs_0_, s16[32,208,128]{2,1,0:T(8,128)(2,1)} %all-to-all-done.9.refs_1_, bf16[80,240]{1,0:T(8,128)(2,1)S(1)} %copy-done.27, bf16[80,240]{1,0:T(8,128)(2,1)S(1)} %copy-done.27), custom_call_target="tpu_custom_call" | custom-call | flops 18400000000 | bytes 3407872 | tf_op jit(solution)/shard_map/middle/pallas_call | solution.py:195
  460.8 19.5 %all-to-all-done.10.refs_1_ = s16[32,208,128]{2,1,0:T(8,128)(2,1)} async-done(((s16[32,208,128]{2,1,0:T(8,128)(2,1)}), s16[32,208,128]{2,1,0:T(8,128)(2,1)}, u32[]{:S(2)}, u32[]{:S(2)}) %all-to-all-start.10) | async-done | bytes 1703968 | tf_op jit(solution)/shard_map/all_to_all | solution.py:456
  483.7 8.3 %target.2.refs_4_ = f32[16000,256]{1,0:T(8,128)} custom-call(s16[32,208,128]{2,1,0:T(8,128)(2,1)S(1)} %copy-done.3, s16[32,208,128]{2,1,0:T(8,128)(2,1)S(1)} %copy-done.5, s16[32,208,128]{2,1,0:T(8,128)(2,1)} %copy-done.6, bf16[80,240]{1,0:T(8,128)(2,1)S(1)} %copy-done.27), custom_call_target="tpu_custom_call" | custom-call | flops 15333332992 | bytes 12288000 | tf_op jit(solution)/shard_map/target/pallas_call | solution.py:246
  492.1 31.8 %all-to-all-done.11.refs_2_ = s16[32,208,128]{2,1,0:T(8,128)(2,1)} async-done(((s16[32,208,128]{2,1,0:T(8,128)(2,1)}), s16[32,208,128]{2,1,0:T(8,128)(2,1)}, u32[]{:S(2)}, u32[]{:S(2)}) %all-to-all-start.11) | async-done | bytes 1703968 | tf_op jit(solution)/shard_map/all_to_all | solution.py:456
  525.3 8.8 %target.3 = f32[16000,256]{1,0:T(8,128)} custom-call(s16[32,208,128]{2,1,0:T(8,128)(2,1)S(1)} %copy-done.7, s16[32,208,128]{2,1,0:T(8,128)(2,1)} %all-to-all-done.10.refs_1_, s16[32,208,128]{2,1,0:T(8,128)(2,1)} %all-to-all-done.11.refs_2_, bf16[80,240]{1,0:T(8,128)(2,1)S(1)} %copy-done.27, f32[16000,256]{1,0:T(8,128)} %target.2.refs_4_), custom_call_target="tpu_custom_call", output_to_operand_aliasing={{}: (4, {})} | custom-call | flops 15333332992 | bytes 12288000 | tf_op jit(solution)/shard_map/target/pallas_call | solution.py:246
  (157 shorter events, 127.4 us)
Async XLA Ops:
  21.4 17.4 %all-to-all-start = ((bf16[32,16,256]{2,1,0:T(8,128)(2,1)}), bf16[32,16,256]{2,1,0:T(8,128)(2,1)S(1)}, u32[]{:S(2)}, u32[]{:S(2)}) async-start(bf16[32,16,256]{2,1,0:T(8,128)(2,1)} %bitcast.6), calls=%async_computation | async-start | bytes 524288 | tf_op jit(solution)/shard_map/all_to_all | solution.py:456
  39.5 12.9 %all-to-all-start.1 = ((bf16[32,16,256]{2,1,0:T(8,128)(2,1)}), bf16[32,16,256]{2,1,0:T(8,128)(2,1)S(1)}, u32[]{:S(2)}, u32[]{:S(2)}) async-start(bf16[32,16,256]{2,1,0:T(8,128)(2,1)} %broadcast_in_dim.19), calls=%async_computation.1 | async-start | bytes 524288 | tf_op jit(solution)/shard_map/all_to_all | solution.py:456
  42.1 69.0 %all-gather.2.cloned.1.call-start = ((), (), s32[]{:S(2)}) async-start(), calls=%async_computation.12 | async-start | bytes 2621440 | tf_op jit(solution)/shard_map/all_gather | solution.py:467
  72.3 55.5 %all-to-all-start.2 = ((s16[32,208,128]{2,1,0:T(8,128)(2,1)}), s16[32,208,128]{2,1,0:T(8,128)(2,1)S(1)}, u32[]{:S(2)}, u32[]{:S(2)}) async-start(s16[32,208,128]{2,1,0:T(8,128)(2,1)} %source.3), calls=%async_computation.2 | async-start | bytes 3407872 | tf_op jit(solution)/shard_map/all_to_all | solution.py:456
  127.8 44.9 %all-to-all-start.3 = ((s16[32,208,128]{2,1,0:T(8,128)(2,1)}), s16[32,208,128]{2,1,0:T(8,128)(2,1)S(1)}, u32[]{:S(2)}, u32[]{:S(2)}) async-start(s16[32,208,128]{2,1,0:T(8,128)(2,1)} %copy-done.8), calls=%async_computation.3 | async-start | bytes 3407872 | tf_op jit(solution)/shard_map/all_to_all | solution.py:456
  133.0 23.6 %copy-start.42 = (bf16[2048,256]{1,0:T(8,128)(2,1)}, bf16[2048,256]{1,0:T(8,128)(2,1)S(1)}, u32[]{:S(2)}) copy-start(bf16[2048,256]{1,0:T(8,128)(2,1)S(1)} %get-tuple-element.47) | copy-start | bytes 3145732
  133.0 23.6 %copy-start.49 = (bf16[2048,256]{1,0:T(8,128)(2,1)}, bf16[2048,256]{1,0:T(8,128)(2,1)S(1)}, u32[]{:S(2)}) copy-start(bf16[2048,256]{1,0:T(8,128)(2,1)S(1)} %get-tuple-element.46) | copy-start | bytes 3145732
  133.0 26.3 %collective-permute-start = (bf16[2048,256]{1,0:T(8,128)(2,1)S(1)}, bf16[2048,256]{1,0:T(8,128)(2,1)S(1)}, u32[]{:S(2)}, u32[]{:S(2)}) collective-permute-start(bf16[2048,256]{1,0:T(8,128)(2,1)S(1)} %get-tuple-element.46), channel_id=1, source_target_pairs={{0,8},{4,20},{9,1},{13,29},{18,26},{22,6},{27,19},{31,15}} | collective-permute-start | bytes 3145736 | tf_op jit(solution)/shard_map/ppermute | solution.py:538
  136.4 36.4 %collective-permute-start.1 = (bf16[2048,256]{1,0:T(8,128)(2,1)S(1)}, bf16[2048,256]{1,0:T(8,128)(2,1)}, u32[]{:S(2)}, u32[]{:S(2)}) collective-permute-start(bf16[2048,256]{1,0:T(8,128)(2,1)S(1)} %get-tuple-element.47), channel_id=1, source_target_pairs={{0,8},{4,20},{9,1},{13,29},{18,26},{22,6},{27,19},{31,15}} | collective-permute-start | bytes 3145736 | tf_op jit(solution)/shard_map/ppermute | solution.py:538
  172.7 46.9 %all-to-all-start.4 = ((s16[32,208,128]{2,1,0:T(8,128)(2,1)}), s16[32,208,128]{2,1,0:T(8,128)(2,1)S(1)}, u32[]{:S(2)}, u32[]{:S(2)}) async-start(s16[32,208,128]{2,1,0:T(8,128)(2,1)} %copy-done.10), calls=%async_computation.4 | async-start | bytes 3407872 | tf_op jit(solution)/shard_map/all_to_all | solution.py:456
  181.5 31.5 %copy-start.40 = (bf16[2048,256]{1,0:T(8,128)(2,1)}, bf16[2048,256]{1,0:T(8,128)(2,1)S(1)}, u32[]{:S(2)}) copy-start(bf16[2048,256]{1,0:T(8,128)(2,1)S(1)} %add.72) | copy-start | bytes 3145732
  181.5 31.5 %copy-start.18 = (s16[16,208,128]{2,1,0:T(8,128)(2,1)S(1)}, s16[16,208,128]{2,1,0:T(8,128)(2,1)}, u32[]{:S(2)}) copy-start(s16[16,208,128]{2,1,0:T(8,128)(2,1)} %copy-done.17) | copy-start | bytes 2555908
  181.5 32.8 %collective-permute-start.2 = (bf16[2048,256]{1,0:T(8,128)(2,1)S(1)}, bf16[2048,256]{1,0:T(8,128)(2,1)}, u32[]{:S(2)}, u32[]{:S(2)}) collective-permute-start(bf16[2048,256]{1,0:T(8,128)(2,1)S(1)} %add.72), channel_id=1, source_target_pairs={{0,16},{8,24},{4,12},{20,28},{9,25},{1,17},{13,5},{29,21},{18,2},{... | collective-permute-start | bytes 3145736 | tf_op jit(solution)/shard_map/ppermute | solution.py:538
  219.7 43.3 %all-to-all-start.5 = ((s16[32,208,128]{2,1,0:T(8,128)(2,1)}), s16[32,208,128]{2,1,0:T(8,128)(2,1)}, u32[]{:S(2)}, u32[]{:S(2)}) async-start(s16[32,208,128]{2,1,0:T(8,128)(2,1)} %pad_add_fusion), calls=%async_computation.5 | async-start | bytes 3407872 | tf_op jit(solution)/shard_map/all_to_all | solution.py:456
  224.8 24.9 %collective-permute-start.3 = (bf16[2048,256]{1,0:T(8,128)(2,1)S(1)}, bf16[2048,256]{1,0:T(8,128)(2,1)}, u32[]{:S(2)}, u32[]{:S(2)}) collective-permute-start(bf16[2048,256]{1,0:T(8,128)(2,1)S(1)} %add.73), channel_id=1, source_target_pairs={{0,16},{8,24},{4,12},{20,28},{9,25},{1,17},{13,5},{29,21},{18,2},{... | collective-permute-start | bytes 3145736 | tf_op jit(solution)/shard_map/ppermute | solution.py:538
  263.0 43.3 %all-to-all-start.6 = ((s16[32,208,128]{2,1,0:T(8,128)(2,1)}), s16[32,208,128]{2,1,0:T(8,128)(2,1)S(1)}, u32[]{:S(2)}, u32[]{:S(2)}) async-start(s16[32,208,128]{2,1,0:T(8,128)(2,1)} %middle.5), calls=%async_computation.6 | async-start | bytes 3407872 | tf_op jit(solution)/shard_map/all_to_all | solution.py:456
  270.0 8.3 %collective-permute-start.4 = (bf16[2048,256]{1,0:T(8,128)(2,1)S(1)}, bf16[2048,256]{1,0:T(8,128)(2,1)S(1)}, u32[]{:S(2)}, u32[]{:S(2)}) collective-permute-start(bf16[2048,256]{1,0:T(8,128)(2,1)S(1)} %add.74), channel_id=1, source_target_pairs={{0,4},{4,0},{8,12},{12,8},{16,20},{20,16},{24,28},{28,24},{1,5},{5... | collective-permute-start | bytes 3145736 | tf_op jit(solution)/shard_map/ppermute | solution.py:545
  270.3 8.9 %collective-permute-start.5 = (bf16[2048,256]{1,0:T(8,128)(2,1)S(1)}, bf16[2048,256]{1,0:T(8,128)(2,1)}, u32[]{:S(2)}, u32[]{:S(2)}) collective-permute-start(bf16[2048,256]{1,0:T(8,128)(2,1)S(1)} %add.75), channel_id=1, source_target_pairs={{0,4},{4,0},{8,12},{12,8},{16,20},{20,16},{24,28},{28,24},{1,5},{5... | collective-permute-start | bytes 3145736 | tf_op jit(solution)/shard_map/ppermute | solution.py:545
  306.4 23.4 %copy-start.4 = (s16[32,208,128]{2,1,0:T(8,128)(2,1)}, s16[32,208,128]{2,1,0:T(8,128)(2,1)S(1)}, u32[]{:S(2)}) copy-start(s16[32,208,128]{2,1,0:T(8,128)(2,1)S(1)} %all-to-all-done.6.refs_1_) | copy-start | bytes 5111812
  306.4 43.2 %all-to-all-start.7 = ((s16[32,208,128]{2,1,0:T(8,128)(2,1)}), s16[32,208,128]{2,1,0:T(8,128)(2,1)S(1)}, u32[]{:S(2)}, u32[]{:S(2)}) async-start(s16[32,208,128]{2,1,0:T(8,128)(2,1)} %get-tuple-element.57), calls=%async_computation.7 | async-start | bytes 3407872 | tf_op jit(solution)/shard_map/all_to_all | solution.py:456
  349.6 43.2 %all-to-all-start.8 = ((s16[32,208,128]{2,1,0:T(8,128)(2,1)}), s16[32,208,128]{2,1,0:T(8,128)(2,1)S(1)}, u32[]{:S(2)}, u32[]{:S(2)}) async-start(s16[32,208,128]{2,1,0:T(8,128)(2,1)} %copy-done.9), calls=%async_computation.8 | async-start | bytes 3407872 | tf_op jit(solution)/shard_map/all_to_all | solution.py:456
  392.9 44.2 %all-to-all-start.9 = ((s16[32,208,128]{2,1,0:T(8,128)(2,1)}), s16[32,208,128]{2,1,0:T(8,128)(2,1)}, u32[]{:S(2)}, u32[]{:S(2)}) async-start(s16[32,208,128]{2,1,0:T(8,128)(2,1)} %get-tuple-element.66), calls=%async_computation.9 | async-start | bytes 3407872 | tf_op jit(solution)/shard_map/all_to_all | solution.py:456
  437.0 43.3 %all-to-all-start.10 = ((s16[32,208,128]{2,1,0:T(8,128)(2,1)}), s16[32,208,128]{2,1,0:T(8,128)(2,1)}, u32[]{:S(2)}, u32[]{:S(2)}) async-start(s16[32,208,128]{2,1,0:T(8,128)(2,1)} %copy-done.11), calls=%async_computation.10 | async-start | bytes 3407872 | tf_op jit(solution)/shard_map/all_to_all | solution.py:456
  480.4 43.4 %all-to-all-start.11 = ((s16[32,208,128]{2,1,0:T(8,128)(2,1)}), s16[32,208,128]{2,1,0:T(8,128)(2,1)}, u32[]{:S(2)}, u32[]{:S(2)}) async-start(s16[32,208,128]{2,1,0:T(8,128)(2,1)} %copy-done.12), calls=%async_computation.11 | async-start | bytes 3407872 | tf_op jit(solution)/shard_map/all_to_all | solution.py:456
  (48 other events, 271.7 us)
Sparse Core Ops, SparseCore 0:
  45.1 65.9 all-gather.1

commit v8 on v7

--- a/solution.py
+++ b/solution.py
@@ -460,11 +460,37 @@
     offered = jnp.concatenate([own[:, :held]] * (PB // held), axis=1)
     own, offered = lax.optimization_barrier((own, offered))
     offered = exchange(offered.reshape(devices, piece_rows, orbitals))
+    rising, falling = [own], [own]
+
+    def pass_on(t):
+        up = [(c, c + 1) for c in range(t, col_count - 1)]
+        down = [(c, c - 1) for c in range(1, col_count - t)]
+        rising.append(lax.ppermute(rising[-1], "col", up))
+        falling.append(lax.ppermute(falling[-1], "col", down))
+        return rising[-1], falling[-1]
+
+    def ordered(value, gate):
+        return lax.optimization_barrier((value, gate))[0]
+
+    passed = pass_on(0)
     owner = me * piece_rows % PB // owned
     piece = lax.dynamic_index_in_dim(offered, owner, axis=0, keepdims=True)
-    pivot = exchange(jnp.broadcast_to(piece, offered.shape)).reshape(2, PB, orbitals)
-
-    row_samples = lax.all_gather(own, "col", axis=1, tiled=True)
+    pieces = ordered(jnp.broadcast_to(piece, offered.shape), passed)
+    pivot = exchange(pieces).reshape(2, PB, orbitals)
+    for t in range(1, col_count - 1):
+        if t == 2:
+            pivot = ordered(pivot, passed)
+        passed = pass_on(t)
+    blocks = []
+    for b in range(col_count):
+        block = own
+        for t in range(1, col_count):
+            if b + t < col_count:
+                block = jnp.where(col_index == b + t, rising[t], block)
+            if b - t >= 0:
+                block = jnp.where(col_index == b - t, falling[t], block)
+        blocks.append(block)
+    row_samples = jnp.concatenate(blocks, axis=1)
 
     lead_inverse = factor_call(lead_kernel, "lead", half, 10, pivot[0, :half], pivot[1, :half])
     inverse = factor_call(rest_kernel, "rest", PB, 14, pivot[0], pivot[1], lead_inverse)
@@ -507,7 +533,7 @@
 
     make(0, parts[0][:1], lead_inverse)
     if parts[0][1:]:
-        make(0, parts[0][1:], after(lead_inverse, outgoing[0][0]))
+        make(0, parts[0][1:], after(lead_inverse, (outgoing[0][0], passed)))
     row_start = row_index * row_samples.shape[1]
     col_start = col_index * row_count * owned
     scalar = lambda *v: jnp.stack([jnp.asarray(a, jnp.int32) for a in v])

time: 543 us -> 550 us (1.013)
  starting transfers between devices: 60.8 us -> 76.2 us
  between operations: 14.8 us -> 1.62 us
  waiting for transfers between devices: 188 us -> 194 us
    ppermute x0 -> x6, waiting for transfers between devices: none -> 36.9 us  [the longest x3 36.9 us: pass_on(): falling.append(lax.ppermute(falling[-1], 'col', down))]
    all_to_all x12, waiting for transfers between devices: 160 us -> 142 us  [on_device(): lax.all_to_all(a, axes, split_axis=0, concat_axis=0, tiled=True)]
    all_gather x1 -> x0, waiting for transfers between devices: 11.9 us -> none  [on_device(): row_samples = lax.all_gather(own, 'col', axis=1, tiled=True)]
    ppermute x0 -> x6, starting transfers between devices: none -> 10.1 us  [the longest x3 6.26 us: pass_on(): rising.append(lax.ppermute(rising[-1], 'col', up))]
    unnamed x106 -> x118, local copies, waits for them, and re-layouts: 22.8 us -> 19.5 us
  transfers between devices with their start and end apart: 19 -> 24, of which waited for: 15 -> 15; matrix products, arithmetic and copies ran while one was open for 2% -> 3% of each run, Pallas kernels for 40% -> 36%
where the time goes in v8:
time: 550 us; the launch traced here: 548 us
  Pallas kernels  228 us (41%)
  waiting for transfers between devices  194 us (35%)
  starting transfers between devices  76.2 us (14%)
  local copies, waits for them, and re-layouts  32.3 us (6%)
  other arithmetic  15.3 us (3%)
    all_to_all x12, waiting for transfers between devices, on_device(): lax.all_to_all(a, axes, split_axis=0, concat_axis=0, tiled=True)  142 us
    pallas_call x5, Pallas kernels, middle(): pl.pallas_call(lambda *refs: middle_kernel(sizes, padded, *refs), in_spec...  94.9 us
    pallas_call x3, Pallas kernels, source(): pl.pallas_call(lambda *refs: source_kernel(group, cells, depth, padded, p...  56.7 us
    all_to_all x12, starting transfers between devices, on_device(): lax.all_to_all(a, axes, split_axis=0, concat_axis=0, tiled=True)  51.2 us
    ppermute x3, waiting for transfers between devices, pass_on(): falling.append(lax.ppermute(falling[-1], 'col', down))  36.9 us
    pallas_call x1, Pallas kernels, schur_block(): pl.pallas_call(schur_kernel, grid=(rows // row_tile, cols // col_tile), i...  34.5 us
    unnamed x118, local copies, waits for them, and re-layouts  19.5 us
    pallas_call x2, Pallas kernels, target(): pl.pallas_call(lambda *refs: target_kernel(group, cells, depth, spans, *r...  17.2 us
  transfers between devices with their start and end apart: 24, of which 15 were waited for; matrix products, arithmetic and copies ran while one was open for 3% of the time, Pallas kernels for 36%

profile of v8, /device:TPU:1, one launch (start us, length us, event | category | flops | bytes accessed | tf_op | source)
XLA Modules:
  0.0 547.9 jit_solution(13793240579904269474)
XLA Ops:
  20.0 6.0 %all-to-all-start = ((bf16[32,16,256]{2,1,0:T(8,128)(2,1)}), bf16[32,16,256]{2,1,0:T(8,128)(2,1)S(1)}, u32[]{:S(2)}, u32[]{:S(2)}) async-start(bf16[32,16,256]{2,1,0:T(8,128)(2,1)} %bitcast.6), calls=%async_computation | async-start | bytes 524288 | tf_op jit(solution)/shard_map/all_to_all | solution.py:456
  31.7 7.2 %all-to-all-done = bf16[32,16,256]{2,1,0:T(8,128)(2,1)S(1)} async-done(((bf16[32,16,256]{2,1,0:T(8,128)(2,1)}), bf16[32,16,256]{2,1,0:T(8,128)(2,1)S(1)}, u32[]{:S(2)}, u32[]{:S(2)}) %all-to-all-start) | async-done | bytes 262176 | tf_op jit(solution)/shard_map/all_to_all | solution.py:456
  39.6 6.7 %all-to-all-start.1 = ((bf16[32,16,256]{2,1,0:T(8,128)(2,1)}), bf16[32,16,256]{2,1,0:T(8,128)(2,1)S(1)}, u32[]{:S(2)}, u32[]{:S(2)}) async-start(bf16[32,16,256]{2,1,0:T(8,128)(2,1)} %broadcast_in_dim.19), calls=%async_computation.1 | async-start | bytes 524288 | tf_op jit(solution)/shard_map/all_to_all | solution.py:456
  46.3 10.3 %all-to-all-done.1 = bf16[32,16,256]{2,1,0:T(8,128)(2,1)S(1)} async-done(((bf16[32,16,256]{2,1,0:T(8,128)(2,1)}), bf16[32,16,256]{2,1,0:T(8,128)(2,1)S(1)}, u32[]{:S(2)}, u32[]{:S(2)}) %all-to-all-start.1) | async-done | bytes 262176 | tf_op jit(solution)/shard_map/all_to_all | solution.py:456
  61.8 14.8 %source.3 = s16[32,208,128]{2,1,0:T(8,128)(2,1)} custom-call(bf16[16000,256]{1,0:T(8,128)(2,1)} %bitcast.43, bf16[16000,256]{1,0:T(8,128)(2,1)} %bitcast.39, bf16[128,256]{1,0:T(8,128)(2,1)S(1)} %get-tuple-element.86.pivot_a.refs_2_, bf16[128,256]{1,0:T(8,128)(2,1)S(1)} %get-tuple-element.85.pivot_b.refs_3_, f32[128,128]{1,0:T(8,128)S(1)} %lead.1.lead_inverse.refs_4_, ...), custom_call_target="tpu_custom_call" | custom-call | flops 30666665984 | bytes 16384000 | tf_op jit(solution)/shard_map/source/pallas_call | solution.py:107
  89.2 33.3 %collective-permute-done.5 = bf16[2,512,256]{2,1,0:T(8,128)(2,1)S(1)} collective-permute-done((bf16[2,512,256]{2,1,0:T(8,128)(2,1)S(1)}, bf16[2,512,256]{2,1,0:T(8,128)(2,1)S(1)}, u32[]{:S(2)}, u32[]{:S(2)}) %collective-permute-start.5) | collective-permute-done | bytes 524320 | tf_op jit(solution)/shard_map/ppermute | solution.py:469
  124.2 14.8 %source.4 = (s16[32,208,128]{2,1,0:T(8,128)(2,1)S(1)}, s16[16,208,128]{2,1,0:T(8,128)(2,1)S(1)}) custom-call(bf16[16000,256]{1,0:T(8,128)(2,1)} %bitcast.44, bf16[16000,256]{1,0:T(8,128)(2,1)} %bitcast.40, bf16[128,256]{1,0:T(8,128)(2,1)S(1)} %get-tuple-element.86.pivot_a.refs_2_, bf16[128,256]{1,0:T(8,128)(2,1)S(1)} %get-tuple-element.85.pivot_b.refs_3_, ...), custom_call_target="tpu_custom_call" | custom-call | flops 30666665984 | bytes 16384000 | tf_op jit(solution)/shard_map/source/pallas_call | solution.py:107
  153.2 17.9 %middle.6 = s16[32,208,128]{2,1,0:T(8,128)(2,1)S(1)} custom-call(s32[1]{0:T(128)} %bitcast.14.refs_0_, s16[32,208,128]{2,1,0:T(8,128)(2,1)S(1)} %all-to-all-done.2.refs_1_, bf16[80,240]{1,0:T(8,128)(2,1)S(1)} %copy-done.21, bf16[80,240]{1,0:T(8,128)(2,1)S(1)} %copy-done.21), custom_call_target="tpu_custom_call" | custom-call | flops 18400000000 | bytes 3407872 | tf_op jit(solution)/shard_map/middle/pallas_call | solution.py:195
  174.4 12.7 %collective-permute-done.7 = bf16[2048,256]{1,0:T(8,128)(2,1)} collective-permute-done((bf16[2048,256]{1,0:T(8,128)(2,1)S(1)}, bf16[2048,256]{1,0:T(8,128)(2,1)}, u32[]{:S(2)}, u32[]{:S(2)}) %collective-permute-start.7) | collective-permute-done | bytes 1048608 | tf_op jit(solution)/shard_map/ppermute | solution.py:564
  187.1 7.0 %all-to-all-start.4 = ((s16[32,208,128]{2,1,0:T(8,128)(2,1)}), s16[32,208,128]{2,1,0:T(8,128)(2,1)S(1)}, u32[]{:S(2)}, u32[]{:S(2)}) async-start(s16[32,208,128]{2,1,0:T(8,128)(2,1)} %copy-done.9), calls=%async_computation.4 | async-start | bytes 3407872 | tf_op jit(solution)/shard_map/all_to_all | solution.py:456
  200.4 27.0 %source.5 = (s16[16,208,128]{2,1,0:T(8,128)(2,1)S(1)}, s16[32,208,128]{2,1,0:T(8,128)(2,1)}, s16[32,208,128]{2,1,0:T(8,128)(2,1)}) custom-call(bf16[16000,256]{1,0:T(8,128)(2,1)} %bitcast.45, bf16[16000,256]{1,0:T(8,128)(2,1)} %bitcast.41, bf16[256,256]{1,0:T(8,128)(2,1)S(1)} %copy-done.19, bf16[256,256]{1,0:T(8,128)(2,1)S(1)} %get-tuple-element.87.pivot_b.refs_3_, ...), custom_call_target="tpu_custom_call" | custom-call | flops 30666665984 | bytes 16384000 | tf_op jit(solution)/shard_map/source/pallas_call | solution.py:107
  243.5 19.1 %middle.5 = s16[32,208,128]{2,1,0:T(8,128)(2,1)} custom-call(s32[1]{0:T(128)} %bitcast.13.refs_0_, s16[32,208,128]{2,1,0:T(8,128)(2,1)S(1)} %all-to-all-done.3.refs_1_, bf16[80,240]{1,0:T(8,128)(2,1)S(1)} %copy-done.23, bf16[80,240]{1,0:T(8,128)(2,1)S(1)} %copy-done.23), custom_call_target="tpu_custom_call" | custom-call | flops 18400000000 | bytes 3407872 | tf_op jit(solution)/shard_map/middle/pallas_call | solution.py:195
  264.1 13.4 %all-to-all-done.5.refs_1_ = s16[32,208,128]{2,1,0:T(8,128)(2,1)} async-done(((s16[32,208,128]{2,1,0:T(8,128)(2,1)}), s16[32,208,128]{2,1,0:T(8,128)(2,1)}, u32[]{:S(2)}, u32[]{:S(2)}) %all-to-all-start.5) | async-done | bytes 1703968 | tf_op jit(solution)/shard_map/all_to_all | solution.py:456
  293.8 27.1 %all-to-all-done.6.refs_1_ = s16[32,208,128]{2,1,0:T(8,128)(2,1)S(1)} async-done(((s16[32,208,128]{2,1,0:T(8,128)(2,1)}), s16[32,208,128]{2,1,0:T(8,128)(2,1)S(1)}, u32[]{:S(2)}, u32[]{:S(2)}) %all-to-all-start.6) | async-done | bytes 1703968 | tf_op jit(solution)/shard_map/all_to_all | solution.py:456
  324.1 20.7 %middle.7 = s16[32,208,128]{2,1,0:T(8,128)(2,1)} custom-call(s32[1]{0:T(128)} %bitcast.17.refs_0_, s16[32,208,128]{2,1,0:T(8,128)(2,1)} %all-to-all-done.5.refs_1_, bf16[80,240]{1,0:T(8,128)(2,1)S(1)} %copy-done.24, bf16[80,240]{1,0:T(8,128)(2,1)S(1)} %copy-done.24), custom_call_target="tpu_custom_call" | custom-call | flops 18400000000 | bytes 3407872 | tf_op jit(solution)/shard_map/middle/pallas_call | solution.py:195
  347.9 9.1 %panel.3 = (f32[4096,256]{1,0:T(8,128)}, bf16[4096,256]{1,0:T(8,128)(2,1)S(1)}, bf16[4096,256]{1,0:T(8,128)(2,1)S(1)}) custom-call(s32[1]{0:T(128)} %bitcast.1.first_row, bf16[4096,256]{1,0:T(8,128)(2,1)S(1)} %pad_maximum_fusion.1.left_a.col_a, bf16[4096,256]{1,0:T(8,128)(2,1)S(1)} %pad_maximum_fusion.2.left_b.col_b, bf16[256,256]{1,0:T(8,128)(2,1)S(1)} %copy-done.20, ...), custom_call_target="tpu_custom_call" | custom-call | flops 11776000000 | bytes 12582912 | tf_op jit(solution)/shard_map/panel/pallas_call | solution.py:281
  369.9 34.5 %schur.1 = f32[2048,4096]{1,0:T(8,128)} custom-call(s32[2]{0:T(128)S(1)} %pad_add_fusion.1.offsets, bf16[2048,256]{1,0:T(8,128)(2,1)S(1)} %copy-done.15, bf16[2048,256]{1,0:T(8,128)(2,1)S(1)} %copy-done.13, bf16[2048,256]{1,0:T(8,128)(2,1)S(1)} %copy-done.29, bf16[2048,256]{1,0:T(8,128)(2,1)} %copy-done.30, bf16[4096,256]{1,0:T(8,128)(2,1)} %copy-done.1, ...), custom_call_target="tpu_custom_call" | custom-call | flops 40195411968 | bytes 33554432 | tf_op jit(solution)/shard_map/schur/pallas_call | solution.py:329
  410.7 19.3 %middle.8 = s16[32,208,128]{2,1,0:T(8,128)(2,1)S(1)} custom-call(s32[1]{0:T(128)} %bitcast.18.refs_0_, s16[32,208,128]{2,1,0:T(8,128)(2,1)} %all-to-all-done.7.refs_1_, bf16[80,240]{1,0:T(8,128)(2,1)S(1)} %copy-done.25, bf16[80,240]{1,0:T(8,128)(2,1)S(1)} %copy-done.25), custom_call_target="tpu_custom_call" | custom-call | flops 18400000000 | bytes 3407872 | tf_op jit(solution)/shard_map/middle/pallas_call | solution.py:195
  431.3 19.5 %all-to-all-done.9.refs_1_ = s16[32,208,128]{2,1,0:T(8,128)(2,1)S(1)} async-done(((s16[32,208,128]{2,1,0:T(8,128)(2,1)}), s16[32,208,128]{2,1,0:T(8,128)(2,1)S(1)}, u32[]{:S(2)}, u32[]{:S(2)}) %all-to-all-start.9) | async-done | bytes 1703968 | tf_op jit(solution)/shard_map/all_to_all | solution.py:456
  454.0 17.9 %middle.9 = s16[32,208,128]{2,1,0:T(8,128)(2,1)S(1)} custom-call(s32[1]{0:T(128)} %bitcast.19.refs_0_, s16[32,208,128]{2,1,0:T(8,128)(2,1)S(1)} %all-to-all-done.9.refs_1_, bf16[80,240]{1,0:T(8,128)(2,1)S(1)} %copy-done.25, bf16[80,240]{1,0:T(8,128)(2,1)S(1)} %copy-done.25), custom_call_target="tpu_custom_call" | custom-call | flops 18400000000 | bytes 3407872 | tf_op jit(solution)/shard_map/middle/pallas_call | solution.py:195
  473.1 21.0 %all-to-all-done.10.refs_1_ = s16[32,208,128]{2,1,0:T(8,128)(2,1)} async-done(((s16[32,208,128]{2,1,0:T(8,128)(2,1)}), s16[32,208,128]{2,1,0:T(8,128)(2,1)}, u32[]{:S(2)}, u32[]{:S(2)}) %all-to-all-start.10) | async-done | bytes 1703968 | tf_op jit(solution)/shard_map/all_to_all | solution.py:456
  497.5 8.3 %target.2.refs_4_ = f32[16000,256]{1,0:T(8,128)} custom-call(s16[32,208,128]{2,1,0:T(8,128)(2,1)S(1)} %copy-done.3, s16[32,208,128]{2,1,0:T(8,128)(2,1)S(1)} %copy-done.5, s16[32,208,128]{2,1,0:T(8,128)(2,1)} %copy-done.6, bf16[80,240]{1,0:T(8,128)(2,1)S(1)} %copy-done.25), custom_call_target="tpu_custom_call" | custom-call | flops 15333332992 | bytes 12288000 | tf_op jit(solution)/shard_map/target/pallas_call | solution.py:246
  505.8 31.8 %all-to-all-done.11.refs_2_ = s16[32,208,128]{2,1,0:T(8,128)(2,1)} async-done(((s16[32,208,128]{2,1,0:T(8,128)(2,1)}), s16[32,208,128]{2,1,0:T(8,128)(2,1)}, u32[]{:S(2)}, u32[]{:S(2)}) %all-to-all-start.11) | async-done | bytes 1703968 | tf_op jit(solution)/shard_map/all_to_all | solution.py:456
  539.0 8.8 %target.3 = f32[16000,256]{1,0:T(8,128)} custom-call(s16[32,208,128]{2,1,0:T(8,128)(2,1)S(1)} %copy-done.7, s16[32,208,128]{2,1,0:T(8,128)(2,1)} %all-to-all-done.10.refs_1_, s16[32,208,128]{2,1,0:T(8,128)(2,1)} %all-to-all-done.11.refs_2_, bf16[80,240]{1,0:T(8,128)(2,1)S(1)} %copy-done.25, f32[16000,256]{1,0:T(8,128)} %target.2.refs_4_), custom_call_target="tpu_custom_call", output_to_operand_aliasing={{}: (4, {})} | custom-call | flops 15333332992 | bytes 12288000 | tf_op jit(solution)/shard_map/target/pallas_call | solution.py:246
  (180 shorter events, 138.1 us)
Async XLA Ops:
  14.0 15.7 %collective-permute-start.1 = (bf16[2,512,256]{2,1,0:T(8,128)(2,1)S(1)}, bf16[2,512,256]{2,1,0:T(8,128)(2,1)S(1)}, u32[]{:S(2)}, u32[]{:S(2)}) collective-permute-start(bf16[2,512,256]{2,1,0:T(8,128)(2,1)S(1)} %pad_maximum_fusion.3), channel_id=1, source_target_pairs={{1,0},{2,1},{3,2},{5,4},{6,5},{7,6},{9,8},{10,9},{11,10},{13,12},{... | collective-permute-start | bytes 1572872 | tf_op jit(solution)/shard_map/ppermute | solution.py:469
  15.3 15.7 %collective-permute-start = (bf16[2,512,256]{2,1,0:T(8,128)(2,1)S(1)}, bf16[2,512,256]{2,1,0:T(8,128)(2,1)S(1)}, u32[]{:S(2)}, u32[]{:S(2)}) collective-permute-start(bf16[2,512,256]{2,1,0:T(8,128)(2,1)S(1)} %pad_maximum_fusion.3), channel_id=1, source_target_pairs={{0,1},{1,2},{2,3},{4,5},{5,6},{6,7},{8,9},{9,10},{10,11},{12,13},{... | collective-permute-start | bytes 1572872 | tf_op jit(solution)/shard_map/ppermute | solution.py:468
  20.0 18.9 %all-to-all-start = ((bf16[32,16,256]{2,1,0:T(8,128)(2,1)}), bf16[32,16,256]{2,1,0:T(8,128)(2,1)S(1)}, u32[]{:S(2)}, u32[]{:S(2)}) async-start(bf16[32,16,256]{2,1,0:T(8,128)(2,1)} %bitcast.6), calls=%async_computation | async-start | bytes 524288 | tf_op jit(solution)/shard_map/all_to_all | solution.py:456
  29.7 26.9 %collective-permute-start.3 = (bf16[2,512,256]{2,1,0:T(8,128)(2,1)S(1)}, bf16[2,512,256]{2,1,0:T(8,128)(2,1)S(1)}, u32[]{:S(2)}, u32[]{:S(2)}) collective-permute-start(bf16[2,512,256]{2,1,0:T(8,128)(2,1)S(1)} %collective-permute-done.1), channel_id=1, source_target_pairs={{1,0},{2,1},{5,4},{6,5},{9,8},{10,9},{13,12},{14,13},{17,16},{18,1... | collective-permute-start | bytes 1572872 | tf_op jit(solution)/shard_map/ppermute | solution.py:469
  31.0 25.6 %collective-permute-start.2 = (bf16[2,512,256]{2,1,0:T(8,128)(2,1)S(1)}, bf16[2,512,256]{2,1,0:T(8,128)(2,1)S(1)}, u32[]{:S(2)}, u32[]{:S(2)}) collective-permute-start(bf16[2,512,256]{2,1,0:T(8,128)(2,1)S(1)} %collective-permute-done), channel_id=1, source_target_pairs={{1,2},{2,3},{5,6},{6,7},{9,10},{10,11},{13,14},{14,15},{17,18},{18... | collective-permute-start | bytes 1572872 | tf_op jit(solution)/shard_map/ppermute | solution.py:468
  39.6 17.0 %all-to-all-start.1 = ((bf16[32,16,256]{2,1,0:T(8,128)(2,1)}), bf16[32,16,256]{2,1,0:T(8,128)(2,1)S(1)}, u32[]{:S(2)}, u32[]{:S(2)}) async-start(bf16[32,16,256]{2,1,0:T(8,128)(2,1)} %broadcast_in_dim.19), calls=%async_computation.1 | async-start | bytes 524288 | tf_op jit(solution)/shard_map/all_to_all | solution.py:456
  76.6 64.5 %all-to-all-start.2 = ((s16[32,208,128]{2,1,0:T(8,128)(2,1)}), s16[32,208,128]{2,1,0:T(8,128)(2,1)S(1)}, u32[]{:S(2)}, u32[]{:S(2)}) async-start(s16[32,208,128]{2,1,0:T(8,128)(2,1)} %source.3), calls=%async_computation.2 | async-start | bytes 3407872 | tf_op jit(solution)/shard_map/all_to_all | solution.py:456
  81.0 41.4 %collective-permute-start.5 = (bf16[2,512,256]{2,1,0:T(8,128)(2,1)S(1)}, bf16[2,512,256]{2,1,0:T(8,128)(2,1)S(1)}, u32[]{:S(2)}, u32[]{:S(2)}) collective-permute-start(bf16[2,512,256]{2,1,0:T(8,128)(2,1)S(1)} %copy-done.55), channel_id=1, source_target_pairs={{1,0},{5,4},{9,8},{13,12},{17,16},{21,20},{25,24},{29,28}} | collective-permute-start | bytes 1572872 | tf_op jit(solution)/shard_map/ppermute | solution.py:469
  82.3 40.1 %collective-permute-start.4 = (bf16[2,512,256]{2,1,0:T(8,128)(2,1)}, bf16[2,512,256]{2,1,0:T(8,128)(2,1)S(1)}, u32[]{:S(2)}, u32[]{:S(2)}) collective-permute-start(bf16[2,512,256]{2,1,0:T(8,128)(2,1)} %copy-done.57), channel_id=1, source_target_pairs={{2,3},{6,7},{10,11},{14,15},{18,19},{22,23},{26,27},{30,31}} | collective-permute-start | bytes 1572872 | tf_op jit(solution)/shard_map/ppermute | solution.py:468
  141.1 46.0 %all-to-all-start.3 = ((s16[32,208,128]{2,1,0:T(8,128)(2,1)}), s16[32,208,128]{2,1,0:T(8,128)(2,1)S(1)}, u32[]{:S(2)}, u32[]{:S(2)}) async-start(s16[32,208,128]{2,1,0:T(8,128)(2,1)} %copy-done.8), calls=%async_computation.3 | async-start | bytes 3407872 | tf_op jit(solution)/shard_map/all_to_all | solution.py:456
  147.5 25.9 %collective-permute-start.6 = (bf16[2048,256]{1,0:T(8,128)(2,1)S(1)}, bf16[2048,256]{1,0:T(8,128)(2,1)S(1)}, u32[]{:S(2)}, u32[]{:S(2)}) collective-permute-start(bf16[2048,256]{1,0:T(8,128)(2,1)S(1)} %get-tuple-element.50), channel_id=1, source_target_pairs={{0,8},{4,20},{9,1},{13,29},{18,26},{22,6},{27,19},{31,15}} | collective-permute-start | bytes 3145736 | tf_op jit(solution)/shard_map/ppermute | solution.py:564
  150.9 36.2 %collective-permute-start.7 = (bf16[2048,256]{1,0:T(8,128)(2,1)S(1)}, bf16[2048,256]{1,0:T(8,128)(2,1)}, u32[]{:S(2)}, u32[]{:S(2)}) collective-permute-start(bf16[2048,256]{1,0:T(8,128)(2,1)S(1)} %get-tuple-element.51), channel_id=1, source_target_pairs={{0,8},{4,20},{9,1},{13,29},{18,26},{22,6},{27,19},{31,15}} | collective-permute-start | bytes 3145736 | tf_op jit(solution)/shard_map/ppermute | solution.py:564
  187.1 47.0 %all-to-all-start.4 = ((s16[32,208,128]{2,1,0:T(8,128)(2,1)}), s16[32,208,128]{2,1,0:T(8,128)(2,1)S(1)}, u32[]{:S(2)}, u32[]{:S(2)}) async-start(s16[32,208,128]{2,1,0:T(8,128)(2,1)} %copy-done.9), calls=%async_computation.4 | async-start | bytes 3407872 | tf_op jit(solution)/shard_map/all_to_all | solution.py:456
  196.0 32.8 %collective-permute-start.8 = (bf16[2048,256]{1,0:T(8,128)(2,1)S(1)}, bf16[2048,256]{1,0:T(8,128)(2,1)}, u32[]{:S(2)}, u32[]{:S(2)}) collective-permute-start(bf16[2048,256]{1,0:T(8,128)(2,1)S(1)} %add.72), channel_id=1, source_target_pairs={{0,16},{8,24},{4,12},{20,28},{9,25},{1,17},{13,5},{29,21},{18,2},{... | collective-permute-start | bytes 3145736 | tf_op jit(solution)/shard_map/ppermute | solution.py:564
  234.2 43.3 %all-to-all-start.5 = ((s16[32,208,128]{2,1,0:T(8,128)(2,1)}), s16[32,208,128]{2,1,0:T(8,128)(2,1)}, u32[]{:S(2)}, u32[]{:S(2)}) async-start(s16[32,208,128]{2,1,0:T(8,128)(2,1)} %pad_add_fusion), calls=%async_computation.5 | async-start | bytes 3407872 | tf_op jit(solution)/shard_map/all_to_all | solution.py:456
  239.2 24.9 %collective-permute-start.9 = (bf16[2048,256]{1,0:T(8,128)(2,1)S(1)}, bf16[2048,256]{1,0:T(8,128)(2,1)}, u32[]{:S(2)}, u32[]{:S(2)}) collective-permute-start(bf16[2048,256]{1,0:T(8,128)(2,1)S(1)} %add.73), channel_id=1, source_target_pairs={{0,16},{8,24},{4,12},{20,28},{9,25},{1,17},{13,5},{29,21},{18,2},{... | collective-permute-start | bytes 3145736 | tf_op jit(solution)/shard_map/ppermute | solution.py:564
  277.5 43.3 %all-to-all-start.6 = ((s16[32,208,128]{2,1,0:T(8,128)(2,1)}), s16[32,208,128]{2,1,0:T(8,128)(2,1)S(1)}, u32[]{:S(2)}, u32[]{:S(2)}) async-start(s16[32,208,128]{2,1,0:T(8,128)(2,1)} %middle.5), calls=%async_computation.6 | async-start | bytes 3407872 | tf_op jit(solution)/shard_map/all_to_all | solution.py:456
  284.5 8.3 %collective-permute-start.10 = (bf16[2048,256]{1,0:T(8,128)(2,1)S(1)}, bf16[2048,256]{1,0:T(8,128)(2,1)S(1)}, u32[]{:S(2)}, u32[]{:S(2)}) collective-permute-start(bf16[2048,256]{1,0:T(8,128)(2,1)S(1)} %add.74), channel_id=1, source_target_pairs={{0,4},{4,0},{8,12},{12,8},{16,20},{20,16},{24,28},{28,24},{1,5},{5... | collective-permute-start | bytes 3145736 | tf_op jit(solution)/shard_map/ppermute | solution.py:571
  284.8 9.0 %collective-permute-start.11 = (bf16[2048,256]{1,0:T(8,128)(2,1)S(1)}, bf16[2048,256]{1,0:T(8,128)(2,1)}, u32[]{:S(2)}, u32[]{:S(2)}) collective-permute-start(bf16[2048,256]{1,0:T(8,128)(2,1)S(1)} %add.75), channel_id=1, source_target_pairs={{0,4},{4,0},{8,12},{12,8},{16,20},{20,16},{24,28},{28,24},{1,5},{5... | collective-permute-start | bytes 3145736 | tf_op jit(solution)/shard_map/ppermute | solution.py:571
  320.9 43.3 %all-to-all-start.7 = ((s16[32,208,128]{2,1,0:T(8,128)(2,1)}), s16[32,208,128]{2,1,0:T(8,128)(2,1)}, u32[]{:S(2)}, u32[]{:S(2)}) async-start(s16[32,208,128]{2,1,0:T(8,128)(2,1)} %get-tuple-element.61), calls=%async_computation.7 | async-start | bytes 3407872 | tf_op jit(solution)/shard_map/all_to_all | solution.py:456
  364.2 43.3 %all-to-all-start.8 = ((s16[32,208,128]{2,1,0:T(8,128)(2,1)}), s16[32,208,128]{2,1,0:T(8,128)(2,1)S(1)}, u32[]{:S(2)}, u32[]{:S(2)}) async-start(s16[32,208,128]{2,1,0:T(8,128)(2,1)} %middle.7), calls=%async_computation.8 | async-start | bytes 3407872 | tf_op jit(solution)/shard_map/all_to_all | solution.py:456
  407.5 43.2 %all-to-all-start.9 = ((s16[32,208,128]{2,1,0:T(8,128)(2,1)}), s16[32,208,128]{2,1,0:T(8,128)(2,1)S(1)}, u32[]{:S(2)}, u32[]{:S(2)}) async-start(s16[32,208,128]{2,1,0:T(8,128)(2,1)} %get-tuple-element.70), calls=%async_computation.9 | async-start | bytes 3407872 | tf_op jit(solution)/shard_map/all_to_all | solution.py:456
  450.8 43.3 %all-to-all-start.10 = ((s16[32,208,128]{2,1,0:T(8,128)(2,1)}), s16[32,208,128]{2,1,0:T(8,128)(2,1)}, u32[]{:S(2)}, u32[]{:S(2)}) async-start(s16[32,208,128]{2,1,0:T(8,128)(2,1)} %copy-done.10), calls=%async_computation.10 | async-start | bytes 3407872 | tf_op jit(solution)/shard_map/all_to_all | solution.py:456
  494.1 43.4 %all-to-all-start.11 = ((s16[32,208,128]{2,1,0:T(8,128)(2,1)}), s16[32,208,128]{2,1,0:T(8,128)(2,1)}, u32[]{:S(2)}, u32[]{:S(2)}) async-start(s16[32,208,128]{2,1,0:T(8,128)(2,1)} %copy-done.11), calls=%async_computation.11 | async-start | bytes 3407872 | tf_op jit(solution)/shard_map/all_to_all | solution.py:456
  (59 other events, 731.9 us)
